TPU v7x, 32 devices: a whole 2x2x4 slice. The times are simulated.
32 devices in a mesh: dp: 8 (over y, x, core), tensor: 4 (over z).
Axes of the slice: x: 2, y: 2, z: 4, core: 2. Of those that a mesh axis runs over, the one named last changes fastest.
Arguments:
- tokens: bfloat16 [16384, 1024], P(('dp', 'tensor')), may hold values from -6 to 6
- group_bucket: int32 [8], P('dp'), may hold values from 0 to 1
- gain_one: float32 [1024], replicated, may hold values from 0.25 to 1.75
- shift_one: float32 [1024], replicated, may hold values from -3 to 3
- w_qkv: bfloat16 [1024, 3, 1024], P(None, None, 'tensor'), may hold values from -0.1875 to 0.1875
- w_out: bfloat16 [1024, 1024], P('tensor'), may hold values from -6 to 6
- gain_two: float32 [1024], replicated, may hold values from 0.25 to 1.75
- shift_two: float32 [1024], replicated, may hold values from -3 to 3
- w_gate_up: bfloat16 [1024, 2, 4096], P(None, None, 'tensor'), may hold values from -0.1875 to 0.1875
- w_down: bfloat16 [4096, 1024], P('tensor'), may hold values from -0.1875 to 0.1875
- cotangent: bfloat16 [16384, 1024], P(('dp', 'tensor')), may hold values from -6 to 6
Outputs:
- layer_out: bfloat16 [16384, 1024], P(('dp', 'tensor'))
- token_grad: float32 [16384, 1024], P(('dp', 'tensor'))
- gain_one_grad: float32 [1024], replicated
- shift_one_grad: float32 [1024], replicated
- qkv_grad: float32 [1024, 3, 1024], P(None, None, 'tensor')
- out_grad: float32 [1024, 1024], P('tensor')
- gain_two_grad: float32 [1024], replicated
- shift_two_grad: float32 [1024], replicated
- gate_up_grad: float32 [1024, 2, 4096], P(None, None, 'tensor')
- down_grad: float32 [4096, 1024], P('tensor')
Inputs may be any that keep to these rules, and one draw needn't show every extreme that they name: `group_bucket`: 1 makes all windows of the group 2048 tokens long; 0 makes them 1000 tokens long, the rest of the group's rows one more window.
All inputs are finite; a program needn't handle non-finite values.
Results may differ from a plain program's by a relative error of at most 0.023.
Values may be sent and summed in bfloat16 or wider, within the bound.
A program may use at most 192 MiB of HBM per device.

v0:
```python
import jax
import jax.numpy as jnp
from jax import lax
from jax.sharding import PartitionSpec as P

HEADS = 16
LONG_LEN = 2048
SHORT_LEN = 1000


norm_eps = 1e-05
mask_fill = -1e30
rope_base = 10000.0


def layout(bucket_id, group_rows):
    positions = jnp.arange(group_rows, dtype=jnp.int32)
    span_len = jnp.where(bucket_id == 1, LONG_LEN, SHORT_LEN).astype(jnp.int32)
    window_ids = positions // span_len
    return (window_ids, positions - window_ids * span_len)


def rotary_tables(places, head_dim):
    half_dim = head_dim // 2
    exponents = jnp.arange(half_dim, dtype=jnp.float32) * (-2.0 / head_dim)
    freqs = jnp.exp(exponents * jnp.log(jnp.float32(rope_base)))
    angles = places.astype(jnp.float32)[:, None] * freqs[None, :]
    return (jnp.cos(angles), jnp.sin(angles))


def rotate(vectors, cos_table, sine_table):
    half_dim = vectors.shape[-1] // 2
    first, second = (vectors[..., :half_dim], vectors[..., half_dim:])
    cos_rows = cos_table[:, None, :]
    sine_rows = sine_table[:, None, :]
    return jnp.concatenate(
        [first * cos_rows - second * sine_rows, second * cos_rows + first * sine_rows], axis=-1
    )


def rotate_back(grads, cos_table, sine_table):
    half_dim = grads.shape[-1] // 2
    first, second = (grads[..., :half_dim], grads[..., half_dim:])
    cos_rows = cos_table[:, None, :]
    sine_rows = sine_table[:, None, :]
    return jnp.concatenate(
        [first * cos_rows + second * sine_rows, second * cos_rows - first * sine_rows], axis=-1
    )


def norm_forward(values, gain, shift):
    average = jnp.mean(values, axis=-1, keepdims=True)
    centred = values - average
    spread_sq = jnp.mean(centred * centred, axis=-1, keepdims=True)
    inv_root = lax.rsqrt(spread_sq + norm_eps)
    unit_rows = centred * inv_root
    return (unit_rows * gain + shift, unit_rows, inv_root)


def norm_backward(out_grad_rows, unit_rows, inv_root, gain):
    scaled = out_grad_rows * gain
    first_mean = jnp.mean(scaled, axis=-1, keepdims=True)
    second_mean = jnp.mean(scaled * unit_rows, axis=-1, keepdims=True)
    in_grad = inv_root * (scaled - first_mean - unit_rows * second_mean)
    return (in_grad, jnp.sum(out_grad_rows * unit_rows, axis=0), jnp.sum(out_grad_rows, axis=0))


def masked_scores(query_block, window_block, key_rows, window_ids, inv_root):
    scores = (
        jnp.einsum("qhd,khd->hqk", query_block, key_rows, preferred_element_type=jnp.float32)
        * inv_root
    )
    same_window = window_block[None, :, None] == window_ids[None, None, :]
    return jnp.where(same_window, scores, mask_fill)


def attend_forward(queries, key_rows, value_rows, window_ids):
    group_rows, head_count, head_dim = queries.shape
    block_rows = min(512, group_rows)
    block_count = group_rows // block_rows
    inv_root = head_dim ** (-0.5)

    def one_block(inputs):
        query_block, window_block = inputs
        scores = masked_scores(query_block, window_block, key_rows, window_ids, inv_root)
        row_max = jnp.max(scores, axis=-1, keepdims=True)
        weights = jnp.exp(scores - row_max)
        totals = jnp.sum(weights, axis=-1, keepdims=True)
        probs = (weights / totals).astype(jnp.bfloat16)
        attended = jnp.einsum("hqk,khd->qhd", probs, value_rows, preferred_element_type=jnp.float32)
        return (attended.astype(jnp.bfloat16), (row_max + jnp.log(totals))[..., 0])

    attended, log_totals = lax.map(
        one_block,
        (
            queries.reshape(block_count, block_rows, head_count, head_dim),
            window_ids.reshape(block_count, block_rows),
        ),
    )
    return (attended.reshape(group_rows, head_count * head_dim), log_totals)


def attend_backward(queries, key_rows, value_rows, window_ids, log_totals, attended_grad):
    group_rows, head_count, head_dim = queries.shape
    block_rows = min(512, group_rows)
    block_count = group_rows // block_rows
    inv_root = head_dim ** (-0.5)

    def one_block(running, inputs):
        key_grad, value_grad = running
        query_block, window_block, log_block, grad_block = inputs
        scores = masked_scores(query_block, window_block, key_rows, window_ids, inv_root)
        probs = jnp.exp(scores - log_block[:, :, None])
        prob_low = probs.astype(jnp.bfloat16)
        prob_grad = jnp.einsum(
            "qhd,khd->hqk", grad_block, value_rows, preferred_element_type=jnp.float32
        )
        score_grad = probs * (prob_grad - jnp.sum(probs * prob_grad, axis=-1, keepdims=True))
        score_low = score_grad.astype(jnp.bfloat16)
        query_grad = (
            jnp.einsum("hqk,khd->qhd", score_low, key_rows, preferred_element_type=jnp.float32)
            * inv_root
        )
        key_grad = (
            key_grad
            + jnp.einsum("hqk,qhd->khd", score_low, query_block, preferred_element_type=jnp.float32)
            * inv_root
        )
        value_grad = value_grad + jnp.einsum(
            "hqk,qhd->khd", prob_low, grad_block, preferred_element_type=jnp.float32
        )
        return ((key_grad, value_grad), query_grad)

    zero_rows = jnp.zeros(key_rows.shape, jnp.float32)
    inputs = (
        queries.reshape(block_count, block_rows, head_count, head_dim),
        window_ids.reshape(block_count, block_rows),
        log_totals,
        attended_grad.reshape(block_count, block_rows, head_count, head_dim),
    )
    (key_grad, value_grad), query_grad = lax.scan(one_block, (zero_rows, zero_rows), inputs)
    return (query_grad.reshape(group_rows, head_count, head_dim), key_grad, value_grad)


def shards(
    tokens,
    group_bucket,
    gain_one,
    shift_one,
    w_qkv,
    w_out,
    gain_two,
    shift_two,
    w_gate_up,
    w_down,
    cotangent,
):
    tensor_ways = lax.axis_size("tensor")
    own_rows = tokens.shape[0]
    group_rows = own_rows * tensor_ways
    model_width = tokens.shape[1]
    local_width = w_out.shape[0]
    head_dim = model_width // HEADS
    local_heads = local_width // head_dim
    hidden_width = w_down.shape[0]
    qkv_matrix = w_qkv.reshape(model_width, 3 * local_width)
    gate_up_matrix = w_gate_up.reshape(model_width, 2 * hidden_width)
    window_ids, places = layout(group_bucket[0], group_rows)
    cos_table, sine_table = rotary_tables(places, head_dim)
    rows_in = tokens.astype(jnp.float32)
    normed_one, unit_one, root_one = norm_forward(rows_in, gain_one, shift_one)
    normed_one_low = normed_one.astype(jnp.bfloat16)
    gathered_one = lax.all_gather(normed_one_low, "tensor", axis=0, tiled=True)
    mixed = jnp.dot(gathered_one, qkv_matrix, preferred_element_type=jnp.float32)
    mixed = mixed.reshape(group_rows, 3, local_heads, head_dim)
    queries = rotate(mixed[:, 0], cos_table, sine_table).astype(jnp.bfloat16)
    key_rows = rotate(mixed[:, 1], cos_table, sine_table).astype(jnp.bfloat16)
    value_rows = mixed[:, 2].astype(jnp.bfloat16)
    attended, log_totals = attend_forward(queries, key_rows, value_rows, window_ids)
    block_vals = attended
    attn_out = lax.psum_scatter(
        jnp.dot(block_vals, w_out, preferred_element_type=jnp.float32).astype(jnp.bfloat16),
        "tensor",
        scatter_dimension=0,
        tiled=True,
    ).astype(jnp.float32)
    resid = rows_in + attn_out
    normed_two, unit_two, root_two = norm_forward(resid, gain_two, shift_two)
    normed_two_low = normed_two.astype(jnp.bfloat16)
    gathered_two = lax.all_gather(normed_two_low, "tensor", axis=0, tiled=True)
    both = jnp.dot(gathered_two, gate_up_matrix, preferred_element_type=jnp.float32).reshape(
        group_rows, 2, hidden_width
    )
    hidden = (jax.nn.silu(both[:, 0]) * both[:, 1]).astype(jnp.bfloat16)
    block_vals = hidden
    ffn_out = lax.psum_scatter(
        jnp.dot(block_vals, w_down, preferred_element_type=jnp.float32).astype(jnp.bfloat16),
        "tensor",
        scatter_dimension=0,
        tiled=True,
    ).astype(jnp.float32)
    layer_out = (resid + ffn_out).astype(jnp.bfloat16)
    rows_two = lax.all_gather(normed_two_low, "tensor", axis=0, tiled=True)
    both_again = jnp.dot(rows_two, gate_up_matrix, preferred_element_type=jnp.float32).reshape(
        group_rows, 2, hidden_width
    )
    gate_vals = both_again[:, 0]
    up_vals = both_again[:, 1]
    gate_sigmoid = jax.nn.sigmoid(gate_vals)
    gate_silu = gate_vals * gate_sigmoid
    hidden_again = (gate_silu * up_vals).astype(jnp.bfloat16)
    shard_rows = lax.all_gather(cotangent, "tensor", axis=0, tiled=True)
    hidden_grad = jnp.dot(shard_rows, w_down.T, preferred_element_type=jnp.float32)
    down_grad = jnp.einsum(
        "sf,sd->fd", hidden_again, shard_rows, preferred_element_type=jnp.float32
    )
    hidden_grad, down_grad = (hidden_grad, down_grad)
    gate_grad = hidden_grad * up_vals * gate_sigmoid * (1.0 + gate_vals * (1.0 - gate_sigmoid))
    up_grad = hidden_grad * gate_silu
    branch_grad = (
        jnp.stack([gate_grad, up_grad], axis=1)
        .astype(jnp.bfloat16)
        .reshape(group_rows, 2 * hidden_width)
    )
    gate_up_grad = jnp.einsum(
        "sd,sf->df", rows_two, branch_grad, preferred_element_type=jnp.float32
    ).reshape(model_width, 2, hidden_width)
    block_vals = branch_grad
    normed_two_grad = lax.psum_scatter(
        jnp.dot(block_vals, gate_up_matrix.T, preferred_element_type=jnp.float32).astype(
            jnp.bfloat16
        ),
        "tensor",
        scatter_dimension=0,
        tiled=True,
    ).astype(jnp.float32)
    resid_part, gain_two_grad, shift_two_grad = norm_backward(
        normed_two_grad, unit_two, root_two, gain_two
    )
    resid_grad = cotangent.astype(jnp.float32) + resid_part
    attn_grad = resid_grad.astype(jnp.bfloat16)
    shard_rows = lax.all_gather(attn_grad, "tensor", axis=0, tiled=True)
    attended_grad = jnp.dot(shard_rows, w_out.T, preferred_element_type=jnp.float32)
    out_grad = jnp.einsum("sf,sd->fd", attended, shard_rows, preferred_element_type=jnp.float32)
    attended_grad, out_grad = (attended_grad, out_grad)
    attended_low = attended_grad.astype(jnp.bfloat16).reshape(group_rows, local_heads, head_dim)
    query_grad, key_grad, value_grad = attend_backward(
        queries, key_rows, value_rows, window_ids, log_totals, attended_low
    )
    mixed_grad = jnp.stack(
        [
            rotate_back(query_grad, cos_table, sine_table),
            rotate_back(key_grad, cos_table, sine_table),
            value_grad,
        ],
        axis=1,
    )
    mixed_grad = mixed_grad.astype(jnp.bfloat16).reshape(group_rows, 3 * local_width)
    rows_one = lax.all_gather(normed_one_low, "tensor", axis=0, tiled=True)
    qkv_grad = jnp.einsum(
        "sd,sf->df", rows_one, mixed_grad, preferred_element_type=jnp.float32
    ).reshape(model_width, 3, local_width)
    block_vals = mixed_grad
    normed_one_grad = lax.psum_scatter(
        jnp.dot(block_vals, qkv_matrix.T, preferred_element_type=jnp.float32).astype(jnp.bfloat16),
        "tensor",
        scatter_dimension=0,
        tiled=True,
    ).astype(jnp.float32)
    input_part, gain_one_grad, shift_one_grad = norm_backward(
        normed_one_grad, unit_one, root_one, gain_one
    )
    token_grad = resid_grad + input_part
    gain_one_grad, shift_one_grad, gain_two_grad, shift_two_grad = lax.psum(
        (gain_one_grad, shift_one_grad, gain_two_grad, shift_two_grad), ("dp", "tensor")
    )
    qkv_grad, out_grad, gate_up_grad, down_grad = (
        lax.psum(qkv_grad.astype(jnp.bfloat16), "dp").astype(jnp.float32),
        lax.psum(out_grad.astype(jnp.bfloat16), "dp").astype(jnp.float32),
        lax.psum(gate_up_grad.astype(jnp.bfloat16), "dp").astype(jnp.float32),
        lax.psum(down_grad.astype(jnp.bfloat16), "dp").astype(jnp.float32),
    )
    return (
        layer_out,
        token_grad,
        gain_one_grad,
        shift_one_grad,
        qkv_grad,
        out_grad,
        gain_two_grad,
        shift_two_grad,
        gate_up_grad,
        down_grad,
    )


def solution(mesh):
    in_specs = (
        P(("dp", "tensor"), None),
        P("dp"),
        P(),
        P(),
        P(None, None, "tensor"),
        P("tensor", None),
        P(),
        P(),
        P(None, None, "tensor"),
        P("tensor", None),
        P(("dp", "tensor"), None),
    )
    out_specs = (
        P(("dp", "tensor"), None),
        P(("dp", "tensor"), None),
        P(),
        P(),
        P(None, None, "tensor"),
        P("tensor", None),
        P(),
        P(),
        P(None, None, "tensor"),
        P("tensor", None),
    )
    return jax.shard_map(shards, mesh=mesh, in_specs=in_specs, out_specs=out_specs, check_vma=False)
```

profile of v0, /device:TPU:0, one launch (start us, length us, event | category | flops | bytes accessed | tf_op | source)
XLA Modules:
  0.0 1189.5 jit_solution(10140255074043842535)
XLA Ops:
  17.9 78.9 %all-gather.5.cloned.1.call-done = bf16[2048,1024]{1,0:T(8,128)(2,1)} async-done(((bf16[512,1024]{1,0:T(8,128)(2,1)}), bf16[2048,1024]{1,0:T(8,128)(2,1)}) %all-gather.5.cloned.1.call-update) | async-done | bytes 4194320 | tf_op jit(solution)/shard_map/all_gather | solution.py:173
  106.0 64.6 %while.28 = (s32[]{:T(128)}, bf16[4,512,4,64]{1,3,2,0:T(8,128)(2,1)}, f32[4,4,512]{2,1,0:T(4,128)}, s32[4,512]{1,0:T(4,128)S(1)}, bf16[4,512,4,64]{1,3,2,0:T(8,1...) while((s32[]{:T(128)}, ...), condition=%wide.region_5.6_spmd.clone, body=%wide.region_2.5_spmd.clone.sunk | while | flops 1125267456 | bytes 61429920 | solution.py:93
  177.5 75.2 %reduce-scatter.5.cloned.1.call-done = bf16[512,1024]{1,0:T(8,128)(2,1)} async-done(((bf16[2048,1024]{1,0:T(8,128)(2,1)}), bf16[512,1024]{1,0:T(8,128)(2,1)}) %reduce-scatter.5.cloned.1.call-update) | async-done | bytes 1048592 | tf_op jit(solution)/shard_map/reduce_scatter | solution.py:181
  271.2 68.6 %all-gather.7.cloned.1.call-done = bf16[2048,1024]{1,0:T(8,128)(2,1)} async-done(((bf16[512,1024]{1,0:T(8,128)(2,1)}), bf16[2048,1024]{1,0:T(8,128)(2,1)}) %all-gather.7.cloned.1.call-update) | async-done | bytes 4194320 | tf_op jit(solution)/shard_map/all_gather | solution.py:190
  339.8 15.1 %fusion.55 = f32[2048,2,1024]{0,2,1:T(8,128)} fusion(bf16[2,1024,1024]{2,1,0:T(8,128)(2,1)} %bitcast.198, bf16[2048,1024]{1,0:T(8,128)(2,1)} %all-gather.7.cloned.1.call-done), kind=kOutput, calls=%fused_computation.77 | convolution fusion | flops 8589934592 | bytes 25165824 | tf_op jit(solution)/shard_map/dot_general | solution.py:191
  354.9 65.7 %all-gather.9.cloned.1.call-done = bf16[2048,1024]{1,0:T(8,128)(2,1)} async-done(((bf16[512,1024]{1,0:T(8,128)(2,1)}), bf16[2048,1024]{1,0:T(8,128)(2,1)}) %all-gather.9.cloned.1.call-update) | async-done | bytes 4194320 | tf_op jit(solution)/shard_map/all_gather | solution.py:212
  420.6 11.6 multiply_bitcast_fusion.1
  435.7 11.7 bitcast_convert_fusion
  447.4 75.4 %reduce-scatter.9.cloned.1.call-done = bf16[512,1024]{1,0:T(8,128)(2,1)} async-done(((bf16[2048,1024]{1,0:T(8,128)(2,1)}), bf16[512,1024]{1,0:T(8,128)(2,1)}) %reduce-scatter.9.cloned.1.call-update) | async-done | bytes 1048592 | tf_op jit(solution)/shard_map/reduce_scatter | solution.py:229
  556.6 55.4 %all-gather.11.cloned.1.call-done = bf16[2048,1024]{1,0:T(8,128)(2,1)} async-done(((bf16[512,1024]{1,0:T(8,128)(2,1)}), bf16[2048,1024]{1,0:T(8,128)(2,1)}) %all-gather.11.cloned.1.call-update) | async-done | bytes 4194320 | tf_op jit(solution)/shard_map/all_gather | solution.py:242
  625.0 248.7 %while.29 = (s32[]{:T(128)}, f32[2048,4,64]{0,2,1:T(8,128)}, f32[2048,4,64]{0,2,1:T(8,128)}, f32[4,512,4,64]{1,0,3,2:T(4,128)}, bf16[4,512,4,64]{1,3,2,0:T(8,128...) while((s32[]{:T(128)}, f32[2048,4,64]{0,2,1:T(8,128)}, ...), condition=%wide.region_15.16_spmd.clone, body=%wide.region_13.15_spmd.clone.sunk | while | flops 2751084544 | bytes 229193984 | solution.py:141
  642.9 12.8 %multiply_reduce_fusion.3 = (f32[4,512]{1,0:T(4,128)S(1)}, f32[4,512,2048]{2,1,0:T(8,128)}) fusion(f32[4,512,2048]{2,1,0:T(8,128)} %copy-done.1, f32[4,512]{1,0:T(4,128)S(1)} %dynamic-slice_bitcast_fusion.2, pred[512,2048]{1,0:T(8,128)(4,1)S(1)} %broadcast_compare_fusion.5, bf16[2048,4,64]{0,2,1:T(8,128)(2,1)} %get-tuple-element.513, ...), kind=kOutput, calls=%fused_computation.25.clone.1 | convolution fusion | flops 557840384 | bytes 35930116 | tf_op jit(solution)/shard_map/while/body/eval_jaxpr/qhd,khd->hqk/dot_general | solution.py:115
  655.7 12.1 %multiply_convert_fusion.3 = bf16[4,512,2048]{2,1,0:T(8,128)(2,1)S(1)} fusion(f32[4,512,2048]{2,1,0:T(8,128)} %get-tuple-element.444, f32[4,512,2048]{2,1,0:T(8,128)} %copy-done.1, f32[4,512]{1,0:T(4,128)S(1)} %get-tuple-element.445, f32[4,512]{1,0:T(4,128)S(1)} %dynamic-slice_bitcast_fusion.2, pred[512,2048]{1,0:T(8,128)(4,1)S(1)} %broadcast_compare_fusion.5), kind=kLoop, calls=%fused_computation.24.clone.1 | loop fusion | flops 25165824 | bytes 43008000 | tf_op jit(solution)/shard_map/while/body/eval_jaxpr/convert_element_type | solution.py:119
  705.1 12.8 %multiply_reduce_fusion.3 = (f32[4,512]{1,0:T(4,128)S(1)}, f32[4,512,2048]{2,1,0:T(8,128)}) fusion(f32[4,512,2048]{2,1,0:T(8,128)} %copy-done.1, f32[4,512]{1,0:T(4,128)S(1)} %dynamic-slice_bitcast_fusion.2, pred[512,2048]{1,0:T(8,128)(4,1)S(1)} %broadcast_compare_fusion.5, bf16[2048,4,64]{0,2,1:T(8,128)(2,1)} %get-tuple-element.513, ...), kind=kOutput, calls=%fused_computation.25.clone.1 | convolution fusion | flops 557840384 | bytes 35930116 | tf_op jit(solution)/shard_map/while/body/eval_jaxpr/qhd,khd->hqk/dot_general | solution.py:115
  717.9 12.1 %multiply_convert_fusion.3 = bf16[4,512,2048]{2,1,0:T(8,128)(2,1)S(1)} fusion(f32[4,512,2048]{2,1,0:T(8,128)} %get-tuple-element.444, f32[4,512,2048]{2,1,0:T(8,128)} %copy-done.1, f32[4,512]{1,0:T(4,128)S(1)} %get-tuple-element.445, f32[4,512]{1,0:T(4,128)S(1)} %dynamic-slice_bitcast_fusion.2, pred[512,2048]{1,0:T(8,128)(4,1)S(1)} %broadcast_compare_fusion.5), kind=kLoop, calls=%fused_computation.24.clone.1 | loop fusion | flops 25165824 | bytes 43008000 | tf_op jit(solution)/shard_map/while/body/eval_jaxpr/convert_element_type | solution.py:119
  767.2 12.8 %multiply_reduce_fusion.3 = (f32[4,512]{1,0:T(4,128)S(1)}, f32[4,512,2048]{2,1,0:T(8,128)}) fusion(f32[4,512,2048]{2,1,0:T(8,128)} %copy-done.1, f32[4,512]{1,0:T(4,128)S(1)} %dynamic-slice_bitcast_fusion.2, pred[512,2048]{1,0:T(8,128)(4,1)S(1)} %broadcast_compare_fusion.5, bf16[2048,4,64]{0,2,1:T(8,128)(2,1)} %get-tuple-element.513, ...), kind=kOutput, calls=%fused_computation.25.clone.1 | convolution fusion | flops 557840384 | bytes 35930116 | tf_op jit(solution)/shard_map/while/body/eval_jaxpr/qhd,khd->hqk/dot_general | solution.py:115
  780.1 12.1 %multiply_convert_fusion.3 = bf16[4,512,2048]{2,1,0:T(8,128)(2,1)S(1)} fusion(f32[4,512,2048]{2,1,0:T(8,128)} %get-tuple-element.444, f32[4,512,2048]{2,1,0:T(8,128)} %copy-done.1, f32[4,512]{1,0:T(4,128)S(1)} %get-tuple-element.445, f32[4,512]{1,0:T(4,128)S(1)} %dynamic-slice_bitcast_fusion.2, pred[512,2048]{1,0:T(8,128)(4,1)S(1)} %broadcast_compare_fusion.5), kind=kLoop, calls=%fused_computation.24.clone.1 | loop fusion | flops 25165824 | bytes 43008000 | tf_op jit(solution)/shard_map/while/body/eval_jaxpr/convert_element_type | solution.py:119
  800.2 11.1 dynamic_update_slice.22
  829.4 12.8 %multiply_reduce_fusion.3 = (f32[4,512]{1,0:T(4,128)S(1)}, f32[4,512,2048]{2,1,0:T(8,128)}) fusion(f32[4,512,2048]{2,1,0:T(8,128)} %copy-done.1, f32[4,512]{1,0:T(4,128)S(1)} %dynamic-slice_bitcast_fusion.2, pred[512,2048]{1,0:T(8,128)(4,1)S(1)} %broadcast_compare_fusion.5, bf16[2048,4,64]{0,2,1:T(8,128)(2,1)} %get-tuple-element.513, ...), kind=kOutput, calls=%fused_computation.25.clone.1 | convolution fusion | flops 557840384 | bytes 35930116 | tf_op jit(solution)/shard_map/while/body/eval_jaxpr/qhd,khd->hqk/dot_general | solution.py:115
  842.2 12.1 %multiply_convert_fusion.3 = bf16[4,512,2048]{2,1,0:T(8,128)(2,1)S(1)} fusion(f32[4,512,2048]{2,1,0:T(8,128)} %get-tuple-element.444, f32[4,512,2048]{2,1,0:T(8,128)} %copy-done.1, f32[4,512]{1,0:T(4,128)S(1)} %get-tuple-element.445, f32[4,512]{1,0:T(4,128)S(1)} %dynamic-slice_bitcast_fusion.2, pred[512,2048]{1,0:T(8,128)(4,1)S(1)} %broadcast_compare_fusion.5), kind=kLoop, calls=%fused_computation.24.clone.1 | loop fusion | flops 25165824 | bytes 43008000 | tf_op jit(solution)/shard_map/while/body/eval_jaxpr/convert_element_type | solution.py:119
  908.2 109.5 %all-reduce.4.cloned.1.call-done = (bf16[1024,2,1024]{2,0,1:T(8,128)(2,1)}, bf16[1024,3,256]{2,0,1:T(8,128)(2,1)}, bf16[256,1024]{1,0:T(8,128)(2,1)}, bf16[1024,1024]{1,0:T(8,128)(2,1)}) async-done(((bf16[1024,2,1024]{2,0,1:T(8,128)(2,1)}, bf16[1024,3,256]{2,0,1:T(8,128)(2,1)}, bf16[256,1024]{1,0:T(8,128)(2,1)}, bf16[1024,1024]{1,0:T(8,128)(2,1)}), (bf16[1024,2,1024]{2,0,1:T(8,128)(2,1)}, ...) | async-done | bytes 8388624 | tf_op jit(solution)/shard_map/psum | solution.py:280
  1037.3 59.8 %reduce-scatter.11.cloned.1.call-done = bf16[512,1024]{1,0:T(8,128)(2,1)} async-done(((bf16[2048,1024]{1,0:T(8,128)(2,1)}), bf16[512,1024]{1,0:T(8,128)(2,1)}) %reduce-scatter.11.cloned.1.call-update) | async-done | bytes 1048592 | tf_op jit(solution)/shard_map/reduce_scatter | solution.py:264
  1099.3 46.3 %all-reduce = (f32[1024]{0:T(1024)}, f32[1024]{0:T(1024)}, f32[1024]{0:T(1024)}, f32[1024]{0:T(1024)}) all-reduce(f32[1024]{0:T(1024)S(1)} %get-tuple-element.228, f32[1024]{0:T(1024)S(1)} %get-tuple-element.233, f32[1024]{0:T(1024)S(1)} %copy-done.35, f32[1024]{0:T(1024)S(1)} %copy-done.36), channel_id=1, replica_groups=mesh['dp'=8,'tensor'=4] {'dp','tensor'}, use_global_device_ids=true, to_apply=%region_20.21 | all-reduce | flops 4096 | bytes 32768 | tf_op jit(solution)/shard_map/psum | solution.py:274
  1145.6 32.0 %reduce-scatter.7.cloned.1.call-done = bf16[512,1024]{1,0:T(8,128)(2,1)} async-done(((bf16[2048,1024]{1,0:T(8,128)(2,1)}), bf16[512,1024]{1,0:T(8,128)(2,1)}) %reduce-scatter.7.cloned.1.call-update) | async-done | bytes 1048592 | tf_op jit(solution)/shard_map/reduce_scatter | solution.py:196
  (259 shorter events, 357.2 us)
Async XLA Ops:
  7.2 413.4 %copy-start = (bf16[1024,1024]{1,0:T(8,128)(2,1)S(1)}, bf16[1024,1024]{1,0:T(8,128)(2,1)}, u32[]{:S(2)}) copy-start(bf16[1024,1024]{1,0:T(8,128)(2,1)} %param.24) | copy-start | bytes 6291460
  7.2 89.6 %all-gather.5.cloned.1.call-start = ((), (), s32[]{:S(2)}) async-start(), calls=%async_computation.4 | async-start | bytes 5242880 | tf_op jit(solution)/shard_map/all_gather | solution.py:173
  13.2 239.5 %reduce-scatter.5.cloned.1.call-start = ((), (), s32[]{:S(2)}) async-start(), calls=%async_computation.5 | async-start | bytes 5242880 | tf_op jit(solution)/shard_map/reduce_scatter | solution.py:181
  17.9 86.2 %copy-start.14 = (f32[2048,32]{0,1:T(8,128)}, f32[2048,32]{0,1:T(8,128)S(1)}, u32[]{:S(2)}) copy-start(f32[2048,32]{0,1:T(8,128)S(1)} %get-tuple-element.306) | copy-start | bytes 786436
  17.9 86.2 %copy-start.16 = (f32[2048,32]{0,1:T(8,128)}, f32[2048,32]{0,1:T(8,128)S(1)}, u32[]{:S(2)}) copy-start(f32[2048,32]{0,1:T(8,128)S(1)} %get-tuple-element.307) | copy-start | bytes 786436
  177.2 79.6 %copy-start.22 = (f32[1024]{0:T(1024)S(1)}, f32[1024]{0:T(1024)}, u32[]{:S(2)}) copy-start(f32[1024]{0:T(1024)} %param.21) | copy-start | bytes 12292
  177.2 79.6 %copy-start.37 = (f32[1024]{0:T(1024)S(1)}, f32[1024]{0:T(1024)}, u32[]{:S(2)}) copy-start(f32[1024]{0:T(1024)} %param.22) | copy-start | bytes 12292
  177.2 162.6 %all-gather.7.cloned.1.call-start = ((), (), s32[]{:S(2)}) async-start(), calls=%async_computation.6 | async-start | bytes 5242880 | tf_op jit(solution)/shard_map/all_gather | solution.py:190
  254.7 271.7 %copy-start.20 = (f32[512]{0:T(512)}, f32[512]{0:T(512)S(1)}, u32[]{:S(2)}) copy-start(f32[512]{0:T(512)S(1)} %broadcast_multiply_fusion.4) | copy-start | bytes 6148
  256.8 269.6 %copy-start.24 = (f32[512]{0:T(512)}, f32[512]{0:T(512)S(1)}, u32[]{:S(2)}) copy-start(f32[512]{0:T(512)S(1)} %add_rsqrt_fusion) | copy-start | bytes 6148
  258.4 162.3 %all-gather.9.cloned.1.call-start = ((), (), s32[]{:S(2)}) async-start(), calls=%async_computation.8 | async-start | bytes 5242880 | tf_op jit(solution)/shard_map/all_gather | solution.py:212
  258.9 263.9 %reduce-scatter.9.cloned.1.call-start = ((), (), s32[]{:S(2)}) async-start(), calls=%async_computation.9 | async-start | bytes 5242880 | tf_op jit(solution)/shard_map/reduce_scatter | solution.py:229
  447.4 164.7 %all-gather.11.cloned.1.call-start = ((), (), s32[]{:S(2)}) async-start(), calls=%async_computation.10 | async-start | bytes 5242880 | tf_op jit(solution)/shard_map/all_gather | solution.py:242
  530.6 487.1 %all-reduce.4.cloned.1.call-start = ((), (), s32[]{:S(2)}) async-start(), calls=%async_computation.12 | async-start | bytes 16777216 | tf_op jit(solution)/shard_map/psum | solution.py:280
  891.4 205.6 %reduce-scatter.11.cloned.1.call-start = ((), (), s32[]{:S(2)}) async-start(), calls=%async_computation.11 | async-start | bytes 5242880 | tf_op jit(solution)/shard_map/reduce_scatter | solution.py:264
  899.4 278.3 %reduce-scatter.7.cloned.1.call-start = ((), (), s32[]{:S(2)}) async-start(), calls=%async_computation.7 | async-start | bytes 5242880 | tf_op jit(solution)/shard_map/reduce_scatter | solution.py:196
  1033.0 64.0 %copy-start.30 = (f32[512]{0:T(512)S(1)}, f32[512]{0:T(512)}, u32[]{:S(2)}) copy-start(f32[512]{0:T(512)} %copy-done.29) | copy-start | bytes 6148
  1033.0 66.3 %copy-start.35 = (f32[1024]{0:T(1024)S(1)}, f32[1024]{0:T(1024)}, u32[]{:S(2)}) copy-start(f32[1024]{0:T(1024)} %get-tuple-element.226) | copy-start | bytes 12292
  1033.1 66.3 %copy-start.36 = (f32[1024]{0:T(1024)S(1)}, f32[1024]{0:T(1024)}, u32[]{:S(2)}) copy-start(f32[1024]{0:T(1024)} %get-tuple-element.232) | copy-start | bytes 12292
  1033.1 144.6 %copy-start.21 = (f32[512]{0:T(512)S(1)}, f32[512]{0:T(512)}, u32[]{:S(2)}) copy-start(f32[512]{0:T(512)} %copy-done.20) | copy-start | bytes 6148
  1033.1 144.6 %copy-start.23 = (f32[1024]{0:T(1024)S(1)}, f32[1024]{0:T(1024)}, u32[]{:S(2)}) copy-start(f32[1024]{0:T(1024)} %param.21) | copy-start | bytes 12292
  1033.1 144.6 %copy-start.25 = (f32[512]{0:T(512)S(1)}, f32[512]{0:T(512)}, u32[]{:S(2)}) copy-start(f32[512]{0:T(512)} %copy-done.24) | copy-start | bytes 6148
  1033.1 144.6 %copy-start.32 = (f32[512]{0:T(512)S(1)}, f32[512]{0:T(512)}, u32[]{:S(2)}) copy-start(f32[512]{0:T(512)} %copy-done.31) | copy-start | bytes 6148
  1033.1 144.6 %copy-start.34 = (f32[512]{0:T(512)S(1)}, f32[512]{0:T(512)}, u32[]{:S(2)}) copy-start(f32[512]{0:T(512)} %copy-done.33) | copy-start | bytes 6148
  (43 other events, 369.6 us)
Sparse Core Ops, SparseCore 0:
  13.3 83.4 all-gather.4
  177.4 75.2 reduce-scatter.4
  258.5 81.2 all-gather.6
  341.3 79.2 all-gather.8
  447.5 75.2 reduce-scatter.8
  530.7 81.2 all-gather.10
  891.6 126.0 all-reduce.3
  1020.1 76.9 reduce-scatter.10
  1099.4 78.2 reduce-scatter.6
where the time goes:
time: 1200 us; the launch traced here: 1190 us
  waiting for transfers between devices  621 us (52%)
  matrix products  249 us (21%)
  local copies, waits for them, and re-layouts  133 us (11%)
  other arithmetic  123 us (10%)
  blocking collectives  46.3 us (4%)
  between operations  15.5 us (1%)
    psum x1, waiting for transfers between devices, shards(): lax.psum(gate_up_grad.astype(jnp.bfloat16), 'dp').astype(jnp.float32)  110 us
    all_gather x1, waiting for transfers between devices, shards(): gathered_one = lax.all_gather(normed_one_low, 'tensor', axis=0, tiled=True)  78.9 us
    reduce_scatter x1, waiting for transfers between devices, shards(): lax.psum_scatter(jnp.dot(block_vals, gate_up_matrix.T, preferred_element_...  75.4 us
    reduce_scatter x1, waiting for transfers between devices, shards(): lax.psum_scatter(jnp.dot(block_vals, w_out, preferred_element_type=jnp.fl...  75.2 us
    all_gather x1, waiting for transfers between devices, shards(): gathered_two = lax.all_gather(normed_two_low, 'tensor', axis=0, tiled=True)  68.6 us
    all_gather x1, waiting for transfers between devices, shards(): shard_rows = lax.all_gather(cotangent, 'tensor', axis=0, tiled=True)  65.7 us
    reduce_scatter x1, waiting for transfers between devices, shards(): lax.psum_scatter(jnp.dot(block_vals, qkv_matrix.T, preferred_element_type...  59.8 us
    all_gather x1, waiting for transfers between devices, shards(): shard_rows = lax.all_gather(attn_grad, 'tensor', axis=0, tiled=True)  55.4 us
  transfers between devices with their start and end apart: 9, of which 9 were waited for; matrix products, arithmetic and copies ran while one was open for 8% of the time, Pallas kernels for 0%

commit v1 on v0

v1 whole, which is shorter than its diff:
```python
import functools

import jax
import jax.numpy as jnp
from jax import lax
from jax.experimental import pallas as pl
from jax.experimental.pallas import tpu as pltpu
from jax.sharding import PartitionSpec as P

HEADS = 16
LONG_LEN = 2048
SHORT_LEN = 1000

norm_eps = 1e-05
mask_fill = -1e30
rope_base = 10000.0
MIB = 2**20
F32 = jnp.float32
BF16 = jnp.bfloat16


def dot_nn(a, b):
    return jnp.dot(a, b, preferred_element_type=F32)


def dot_nt(a, b):
    return lax.dot_general(a, b, (((1,), (1,)), ((), ())), preferred_element_type=F32)


def dot_tn(a, b):
    return lax.dot_general(a, b, (((0,), (0,)), ((), ())), preferred_element_type=F32)


def rotary_wide(bucket_id, group_rows, head_dim, width):
    positions = jnp.arange(group_rows, dtype=jnp.int32)
    span_len = jnp.where(bucket_id == 1, LONG_LEN, SHORT_LEN).astype(jnp.int32)
    places = positions - (positions // span_len) * span_len
    half_dim = head_dim // 2
    exponents = jnp.arange(half_dim, dtype=F32) * (-2.0 / head_dim)
    freqs = jnp.exp(exponents * jnp.log(F32(rope_base)))
    angles = places.astype(F32)[:, None] * freqs[None, :]
    cos_table, sine_table = jnp.cos(angles), jnp.sin(angles)
    heads = width // head_dim
    cos_wide = jnp.tile(jnp.concatenate([cos_table, cos_table], axis=1), (1, heads))
    sine_wide = jnp.tile(jnp.concatenate([-sine_table, sine_table], axis=1), (1, heads))
    return cos_wide, sine_wide


def norm_forward(values, gain, shift):
    average = jnp.mean(values, axis=-1, keepdims=True)
    centred = values - average
    spread_sq = jnp.mean(centred * centred, axis=-1, keepdims=True)
    inv_root = lax.rsqrt(spread_sq + norm_eps)
    unit_rows = centred * inv_root
    return (unit_rows * gain + shift, unit_rows, inv_root)


def norm_backward(out_grad_rows, unit_rows, inv_root, gain):
    scaled = out_grad_rows * gain
    first_mean = jnp.mean(scaled, axis=-1, keepdims=True)
    second_mean = jnp.mean(scaled * unit_rows, axis=-1, keepdims=True)
    in_grad = inv_root * (scaled - first_mean - unit_rows * second_mean)
    return (in_grad, jnp.sum(out_grad_rows * unit_rows, axis=0), jnp.sum(out_grad_rows, axis=0))


def swap_halves(x, head_dim):
    half = head_dim // 2
    width = x.shape[1]
    lane = lax.broadcasted_iota(jnp.int32, x.shape, 1) % head_dim
    return jnp.where(lane < half, pltpu.roll(x, width - half, 1), pltpu.roll(x, half, 1))


def head_mask(x, h, head_dim):
    lane = lax.broadcasted_iota(jnp.int32, x.shape, 1)
    return jnp.where((lane >= h * head_dim) & (lane < (h + 1) * head_dim), x, jnp.zeros_like(x))


def project_kernel(head_dim, x_ref, w_ref, cos_ref, sin_ref, q_ref, k_ref, v_ref, kt_ref, vt_ref):
    width = q_ref.shape[1]
    mixed = dot_nn(x_ref[...], w_ref[...])
    cos, sin = cos_ref[...], sin_ref[...]
    q = mixed[:, :width]
    k = mixed[:, width : 2 * width]
    v = mixed[:, 2 * width :].astype(BF16)
    q = q * cos + swap_halves(q, head_dim) * sin
    k = k * cos + swap_halves(k, head_dim) * sin
    k_low = k.astype(BF16)
    q_ref[...] = (q.astype(BF16).astype(F32) * head_dim ** (-0.5)).astype(BF16)
    k_ref[...] = k_low
    v_ref[...] = v
    kt_ref[...] = k_low.T
    vt_ref[...] = v.T


def project(rows, qkv_matrix, cos_wide, sine_wide, head_dim):
    n, d = rows.shape
    width = qkv_matrix.shape[1] // 3
    block = min(512, n)
    row = pl.BlockSpec((block, width), lambda i: (i, 0))
    col = pl.BlockSpec((width, block), lambda i: (0, i))
    return pl.pallas_call(
        functools.partial(project_kernel, head_dim),
        grid=(n // block,),
        in_specs=[
            pl.BlockSpec((block, d), lambda i: (i, 0)),
            pl.BlockSpec((d, 3 * width), lambda i: (0, 0)),
            row,
            row,
        ],
        out_specs=[row, row, row, col, col],
        out_shape=[jax.ShapeDtypeStruct((n, width), BF16)] * 3
        + [jax.ShapeDtypeStruct((width, n), BF16)] * 2,
        compiler_params=pltpu.CompilerParams(vmem_limit_bytes=40 * MIB),
        cost_estimate=pl.CostEstimate(
            flops=6 * n * d * width, bytes_accessed=2 * n * d + 18 * n * width, transcendentals=0
        ),
        name="project",
    )(rows, qkv_matrix, cos_wide, sine_wide)


def key_range(start, block, total):
    first = (start // SHORT_LEN) * SHORT_LEN
    last = min(total, ((start + block - 1) // SHORT_LEN + 1) * SHORT_LEN)
    return (first // 256) * 256, min(total, -(-last // 256) * 256)


def window_bias(key_start, keys, row_start, rows, total):
    key_at = lax.broadcasted_iota(jnp.int32, (keys, rows), 0) + key_start
    row_at = lax.broadcasted_iota(jnp.int32, (keys, rows), 1) + row_start
    key_window = jnp.zeros_like(key_at)
    row_window = jnp.zeros_like(row_at)
    for edge in range(SHORT_LEN, total, SHORT_LEN):
        key_window += (key_at >= edge).astype(jnp.int32)
        row_window += (row_at >= edge).astype(jnp.int32)
    return jnp.where(key_window == row_window, 0.0, mask_fill)


def attend_kernel(head_dim, bucket_ref, q_ref, k_ref, vt_ref, o_ref, ot_ref, l_ref, bias_ref):
    rows, width = q_ref.shape
    total = k_ref.shape[0]
    heads = width // head_dim
    step = pl.program_id(0)

    def block(at, first, last, masked):
        @pl.loop(0, heads)
        def _(h):
            hs = pl.ds(pl.multiple_of(h * head_dim, head_dim), head_dim)
            scores = dot_nt(k_ref[first:last, :], head_mask(q_ref[at, :], h, head_dim))
            if masked:
                scores = scores + bias_ref[: last - first, :]
            top = jnp.max(scores, axis=0, keepdims=True)
            weights = jnp.exp(scores - top)
            totals = jnp.sum(weights, axis=0, keepdims=True)
            ot_ref[hs, at] = dot_nn(vt_ref[hs, first:last], weights.astype(BF16)) / totals
            l_ref[pl.ds(h, 1), at] = top + jnp.log(totals)

    @pl.when(bucket_ref[0] == 1)
    def _():
        block(slice(0, rows), 0, total, False)

    sub = bias_ref.shape[1]
    for start in range(0, total, sub):
        first, last = key_range(start, sub, total)

        @pl.when((bucket_ref[0] != 1) & (step == start // rows))
        def _():
            bias_ref[: last - first, :] = window_bias(first, last - first, start, sub, total)
            block(slice(start % rows, start % rows + sub), first, last, True)

    o_ref[...] = ot_ref[...].T.astype(BF16)


def attend(bucket, q, k, vt, head_dim):
    n, width = q.shape
    heads = width // head_dim
    block = min(1024, n)
    pairs = n * n * heads
    lanes = -(-heads // 8) * 8
    row = pl.BlockSpec((block, width), lambda i, *_: (i, 0))
    col = pl.BlockSpec((width, block), lambda i, *_: (0, i))
    return pl.pallas_call(
        functools.partial(attend_kernel, head_dim),
        grid_spec=pltpu.PrefetchScalarGridSpec(
            num_scalar_prefetch=1,
            grid=(n // block,),
            in_specs=[
                row,
                pl.BlockSpec((n, width), lambda i, *_: (0, 0)),
                pl.BlockSpec((width, n), lambda i, *_: (0, 0)),
            ],
            out_specs=[row, col, pl.BlockSpec((lanes, block), lambda i, *_: (0, i))],
            scratch_shapes=[pltpu.VMEM((n, min(512, block)), F32)],
        ),
        out_shape=[
            jax.ShapeDtypeStruct((n, width), BF16),
            jax.ShapeDtypeStruct((width, n), F32),
            jax.ShapeDtypeStruct((lanes, n), F32),
        ],
        compiler_params=pltpu.CompilerParams(vmem_limit_bytes=56 * MIB),
        cost_estimate=pl.CostEstimate(
            flops=pairs * 1024, bytes_accessed=10 * n * width, transcendentals=pairs
        ),
        name="attend",
    )(bucket, q, k, vt)


def attend_back_kernel(
    head_dim,
    bucket_ref,
    q_ref,
    k_ref,
    kt_ref,
    v_ref,
    g_ref,
    ot_ref,
    l_ref,
    dq_ref,
    dk_ref,
    dv_ref,
    bias_ref,
    gt_ref,
):
    rows, width = q_ref.shape
    total = k_ref.shape[0]
    heads = width // head_dim
    step = pl.program_id(0)

    @pl.when(step == 0)
    def _():
        dk_ref[...] = jnp.zeros_like(dk_ref)
        dv_ref[...] = jnp.zeros_like(dv_ref)

    gt_ref[...] = g_ref[...].astype(F32).T * ot_ref[...]

    def block(first, last, masked):
        keys = slice(first, last)

        @pl.loop(0, heads)
        def _(h):
            hs = pl.ds(pl.multiple_of(h * head_dim, head_dim), head_dim)
            qh, gh = head_mask(q_ref[...], h, head_dim), head_mask(g_ref[...], h, head_dim)
            scores = dot_nt(k_ref[keys, :], qh)
            if masked:
                scores = scores + bias_ref[: last - first, :]
            probs = jnp.exp(scores - l_ref[pl.ds(h, 1), :])
            prob_grad = dot_nt(v_ref[keys, :], gh)
            delta = jnp.sum(gt_ref[hs, :], axis=0, keepdims=True)
            score_grad = (probs * (prob_grad - delta)).astype(BF16)
            dv_ref[keys, :] += dot_nn(probs.astype(BF16), gh)
            dk_ref[keys, :] += dot_nn(score_grad, qh)
            dq_ref[hs, :] = dot_nn(kt_ref[hs, keys], score_grad)

    @pl.when(bucket_ref[0] == 1)
    def _():
        block(0, total, False)

    for start in range(0, total, rows):
        first, last = key_range(start, rows, total)

        @pl.when((bucket_ref[0] != 1) & (step == start // rows))
        def _():
            bias_ref[: last - first, :] = window_bias(first, last - first, start, rows, total)
            block(first, last, True)


def attend_back(bucket, q, k, kt, v, g, ot, log_totals, head_dim):
    n, width = q.shape
    heads = width // head_dim
    block = min(512, n)
    pairs = n * n * heads
    row = pl.BlockSpec((block, width), lambda i, *_: (i, 0))
    col = pl.BlockSpec((width, block), lambda i, *_: (0, i))
    full = pl.BlockSpec((n, width), lambda i, *_: (0, 0))
    return pl.pallas_call(
        functools.partial(attend_back_kernel, head_dim),
        grid_spec=pltpu.PrefetchScalarGridSpec(
            num_scalar_prefetch=1,
            grid=(n // block,),
            in_specs=[
                row,
                full,
                pl.BlockSpec((width, n), lambda i, *_: (0, 0)),
                full,
                row,
                col,
                pl.BlockSpec((log_totals.shape[0], block), lambda i, *_: (0, i)),
            ],
            out_specs=[col, full, full],
            scratch_shapes=[pltpu.VMEM((n, block), F32), pltpu.VMEM((width, block), F32)],
        ),
        out_shape=[
            jax.ShapeDtypeStruct((width, n), F32),
            jax.ShapeDtypeStruct((n, width), F32),
            jax.ShapeDtypeStruct((n, width), F32),
        ],
        compiler_params=pltpu.CompilerParams(vmem_limit_bytes=56 * MIB),
        cost_estimate=pl.CostEstimate(
            flops=pairs * 2560, bytes_accessed=24 * n * width, transcendentals=pairs
        ),
        name="attend_back",
    )(bucket, q, k, kt, v, g, ot, log_totals)


def unrotate_kernel(head_dim, dq_ref, dk_ref, dv_ref, cos_ref, sin_ref, out_ref):
    width = dk_ref.shape[1]
    cos, sin = cos_ref[...], sin_ref[...]
    dq = dq_ref[...].T * head_dim ** (-0.5)
    dk = dk_ref[...]
    out_ref[:, :width] = (dq * cos - swap_halves(dq, head_dim) * sin).astype(BF16)
    out_ref[:, width : 2 * width] = (dk * cos - swap_halves(dk, head_dim) * sin).astype(BF16)
    out_ref[:, 2 * width :] = dv_ref[...].astype(BF16)


def unrotate(dq_t, dk, dv, cos_wide, sine_wide, head_dim):
    n, width = dk.shape
    block = min(512, n)
    row = pl.BlockSpec((block, width), lambda i: (i, 0))
    return pl.pallas_call(
        functools.partial(unrotate_kernel, head_dim),
        grid=(n // block,),
        in_specs=[pl.BlockSpec((width, block), lambda i: (0, i)), row, row, row, row],
        out_specs=pl.BlockSpec((block, 3 * width), lambda i: (i, 0)),
        out_shape=jax.ShapeDtypeStruct((n, 3 * width), BF16),
        compiler_params=pltpu.CompilerParams(vmem_limit_bytes=40 * MIB),
        cost_estimate=pl.CostEstimate(flops=0, bytes_accessed=26 * n * width, transcendentals=0),
        name="unrotate",
    )(dq_t, dk, dv, cos_wide, sine_wide)


def feed_kernel(x_ref, c_ref, wgu_ref, wd_ref, h_ref, b_ref, n_ref):
    units = wd_ref.shape[0]
    both = dot_nn(x_ref[...], wgu_ref[...])
    gate, up = both[:, :units], both[:, units:]
    sig = jax.nn.sigmoid(gate)
    silu = gate * sig
    h_ref[...] = (silu * up).astype(BF16)
    hidden_grad = dot_nt(c_ref[...], wd_ref[...])
    b_ref[:, :units] = (hidden_grad * up * sig * (1.0 + gate * (1.0 - sig))).astype(BF16)
    b_ref[:, units:] = (hidden_grad * silu).astype(BF16)
    n_ref[...] = dot_nt(b_ref[...], wgu_ref[...]).astype(BF16)


def feed(x, cot, wgu, wd):
    n, d = x.shape
    units = wd.shape[0]
    block = min(256, n)
    row = lambda w: pl.BlockSpec((block, w), lambda i: (i, 0))
    return pl.pallas_call(
        feed_kernel,
        grid=(n // block,),
        in_specs=[
            row(d),
            row(d),
            pl.BlockSpec((d, 2 * units), lambda i: (0, 0)),
            pl.BlockSpec((units, d), lambda i: (0, 0)),
        ],
        out_specs=[row(units), row(2 * units), row(d)],
        out_shape=[
            jax.ShapeDtypeStruct((n, units), BF16),
            jax.ShapeDtypeStruct((n, 2 * units), BF16),
            jax.ShapeDtypeStruct((n, d), BF16),
        ],
        compiler_params=pltpu.CompilerParams(vmem_limit_bytes=40 * MIB),
        cost_estimate=pl.CostEstimate(
            flops=10 * n * d * units, bytes_accessed=8 * n * d, transcendentals=n * units
        ),
        name="feed",
    )(x, cot, wgu, wd)


def hop(x, bit):
    size = lax.axis_size("dp")
    return lax.ppermute(x, "dp", [(i, i ^ bit) for i in range(size)])


def gather_plane(a):
    size = lax.axis_size("dp")
    if size != 8:
        return [lax.all_gather(a, "dp", axis=0, tiled=True)]
    half = a.shape[0] // 2
    from_x, from_y = hop(a, 2), hop(a, 4)
    own_pair = jnp.concatenate([a, hop(a, 1)])
    low, high = hop(from_y[:half], 2), hop(from_x[half:], 4)
    x_pair = jnp.concatenate([from_x, hop(from_x, 1)])
    y_pair = jnp.concatenate([from_y, hop(from_y, 1)])
    far = jnp.concatenate([low, high])
    far_pair = jnp.concatenate([far, hop(far, 1)])
    return [own_pair, x_pair, y_pair, far_pair]


def add_low(*terms):
    return sum(t.astype(F32) for t in terms).astype(BF16)


def scatter_plane(parts):
    size = lax.axis_size("dp")
    if size != 8:
        return lax.psum_scatter(parts[0], "dp", scatter_dimension=0, tiled=True).astype(F32)
    rows = parts[0].shape[0] // 2
    half = rows // 2
    own, x, y, far = (add_low(p[:rows], hop(p[rows:], 1)) for p in parts)
    to_x, to_y = hop(far[:half], 2), hop(far[half:], 4)
    y = jnp.concatenate([add_low(y[:half], to_x), y[half:]])
    x = jnp.concatenate([x[:half], add_low(x[half:], to_y)])
    return own.astype(F32) + hop(x, 2).astype(F32) + hop(y, 4).astype(F32)


def shards(
    tokens,
    group_bucket,
    gain_one,
    shift_one,
    w_qkv,
    w_out,
    gain_two,
    shift_two,
    w_gate_up,
    w_down,
    cotangent,
):
    ways = lax.axis_size("tensor")
    replicas = lax.axis_size("dp")
    replica = lax.axis_index("dp")
    own_rows, d = tokens.shape
    group_rows = own_rows * ways
    local_width = w_out.shape[0]
    head_dim = d // HEADS
    hidden_width = w_down.shape[0]
    units = hidden_width // replicas
    out_rows = local_width // replicas
    qkv_matrix = w_qkv.reshape(d, 3 * local_width)
    cos_wide, sine_wide = rotary_wide(group_bucket[0], group_rows, head_dim, local_width)

    rows_in = tokens.astype(F32)
    normed_one, unit_one, root_one = norm_forward(rows_in, gain_one, shift_one)
    normed_one_low = normed_one.astype(BF16)
    rows_one = lax.all_gather(normed_one_low, "tensor", axis=0, tiled=True)

    gate_up_slice = lax.dynamic_slice_in_dim(w_gate_up, replica * units, units, axis=2)
    down_slice = lax.dynamic_slice_in_dim(w_down, replica * units, units, axis=0)
    out_slice = lax.dynamic_slice_in_dim(w_out, replica * out_rows, out_rows, axis=0)
    gate_up_all = lax.all_gather(gate_up_slice.reshape(d, 2 * units), "tensor", axis=0)
    down_all = lax.all_gather(down_slice, "tensor", axis=0, tiled=True)
    out_part = lax.all_gather(out_slice, "tensor", axis=0)
    out_full = lax.all_gather(out_part, "dp", axis=1).reshape(d, d)
    wgu = gate_up_all.reshape(ways, d, 2, units).transpose(1, 2, 0, 3).reshape(d, 2 * ways * units)
    cot_pieces = gather_plane(cotangent)

    q, k, v, kt, vt = project(rows_one, qkv_matrix, cos_wide, sine_wide, head_dim)
    attended, attended_t, log_totals = attend(group_bucket, q, k, vt, head_dim)
    attended_own = lax.all_to_all(attended, "tensor", 0, 1, tiled=True)
    resid = rows_in + dot_nn(attended_own, out_full)

    normed_two, unit_two, root_two = norm_forward(resid, gain_two, shift_two)
    row_pieces = gather_plane(normed_two.astype(BF16))
    fed = [feed(x, c, wgu, down_all) for x, c in zip(row_pieces, cot_pieces)]
    normed_two_grad = scatter_plane([f[2] for f in fed])
    hidden = [f[0] for f in fed]
    branch = [f[1] for f in fed]
    ffn_out = scatter_plane([dot_nn(h, down_all).astype(BF16) for h in hidden])
    layer_out = (resid + ffn_out).astype(BF16)
    down_grad = sum(dot_tn(h, c) for h, c in zip(hidden, cot_pieces)).astype(BF16)
    gate_up_grad = sum(dot_tn(x, b) for x, b in zip(row_pieces, branch)).astype(BF16)
    gate_up_grad = gate_up_grad.reshape(d, 2, ways, units).transpose(2, 0, 1, 3)
    gate_up_grad = gate_up_grad.reshape(ways, d, 2 * units)
    gate_up_grad = lax.psum_scatter(gate_up_grad, "tensor", scatter_dimension=0)
    down_grad = lax.psum_scatter(down_grad, "tensor", scatter_dimension=0, tiled=True)
    gate_up_grad = lax.all_gather(gate_up_grad, "dp", axis=0)
    down_grad = lax.all_gather(down_grad, "dp", axis=0, tiled=True).astype(F32)
    gate_up_grad = gate_up_grad.reshape(replicas, d, 2, units).transpose(1, 2, 0, 3)
    gate_up_grad = gate_up_grad.reshape(d, 2, hidden_width).astype(F32)

    resid_part, gain_two_grad, shift_two_grad = norm_backward(
        normed_two_grad, unit_two, root_two, gain_two
    )
    resid_grad = cotangent.astype(F32) + resid_part
    attn_grad = resid_grad.astype(BF16)

    attended_grad_own = dot_nt(attn_grad, out_full).astype(BF16)
    attended_grad = lax.all_to_all(attended_grad_own, "tensor", 1, 0, tiled=True)
    out_grad = dot_tn(attended_own, attn_grad).astype(BF16).reshape(ways, replicas, out_rows, d)
    out_grad = lax.psum_scatter(out_grad, "dp", scatter_dimension=1)
    out_grad = lax.psum_scatter(out_grad, "tensor", scatter_dimension=0)
    out_grad = lax.all_gather(out_grad, "dp", axis=0, tiled=True).astype(F32)
    dq_t, dk, dv = attend_back(
        group_bucket, q, k, kt, v, attended_grad, attended_t, log_totals, head_dim
    )
    mixed_grad = unrotate(dq_t, dk, dv, cos_wide, sine_wide, head_dim)
    normed_one_grad = lax.psum_scatter(
        dot_nt(mixed_grad, qkv_matrix).astype(BF16), "tensor", scatter_dimension=0, tiled=True
    ).astype(F32)
    qkv_grad = lax.psum(dot_tn(rows_one, mixed_grad).astype(BF16), "dp").astype(F32)
    qkv_grad = qkv_grad.reshape(d, 3, local_width)
    input_part, gain_one_grad, shift_one_grad = norm_backward(
        normed_one_grad, unit_one, root_one, gain_one
    )
    token_grad = resid_grad + input_part
    gain_one_grad, shift_one_grad, gain_two_grad, shift_two_grad = lax.psum(
        jnp.stack([gain_one_grad, shift_one_grad, gain_two_grad, shift_two_grad]), ("dp", "tensor")
    )
    return (
        layer_out,
        token_grad,
        gain_one_grad,
        shift_one_grad,
        qkv_grad,
        out_grad,
        gain_two_grad,
        shift_two_grad,
        gate_up_grad,
        down_grad,
    )


def solution(mesh):
    in_specs = (
        P(("dp", "tensor"), None),
        P("dp"),
        P(),
        P(),
        P(None, None, "tensor"),
        P("tensor", None),
        P(),
        P(),
        P(None, None, "tensor"),
        P("tensor", None),
        P(("dp", "tensor"), None),
    )
    out_specs = (
        P(("dp", "tensor"), None),
        P(("dp", "tensor"), None),
        P(),
        P(),
        P(None, None, "tensor"),
        P("tensor", None),
        P(),
        P(),
        P(None, None, "tensor"),
        P("tensor", None),
    )
    return jax.shard_map(shards, mesh=mesh, in_specs=in_specs, out_specs=out_specs, check_vma=False)
```

time: 1200 us -> 789 us (0.66)
  waiting for transfers between devices: 621 us -> 317 us
  matrix products: 249 us -> 49.1 us
  Pallas kernels: 0 us -> 115 us
  other arithmetic: 123 us -> 46.6 us
  starting transfers between devices: 0.54 us -> 31.9 us
  blocking collectives: 46.3 us -> 67.8 us
    dot_general x40 -> x17, matrix products: 249 us -> 49.1 us  [the longest x10 31.7 us: dot_tn(): lax.dot_general(a, b, (((0,), (0,)), ((), ())), preferred_element_type=F32)]
    all_gather x4 -> x6, waiting for transfers between devices: 269 us -> 93.2 us  [the longest x1 40.9 us: shards(): rows_one = lax.all_gather(normed_one_low, 'tensor', axis=0, tiled=True)]
    reduce_scatter x4 -> x5, waiting for transfers between devices: 242 us -> 69.1 us  [the longest x1 51.3 us: shards(): lax.psum_scatter(dot_nt(mixed_grad, qkv_matrix).astype(BF16), 'tensor', s...]
    pallas_call x0 -> x8, Pallas kernels: none -> 115 us  [the longest x1 49 us: attend_back(): pl.pallas_call(functools.partial(attend_back_kernel, head_dim), grid_spec...]
    ppermute x0 -> x32, waiting for transfers between devices: none -> 65 us  [hop(): return lax.ppermute(x, 'dp', [(i, i ^ bit) for i in range(size)])]
    psum x1, waiting for transfers between devices: 110 us -> 48 us  [shards(): lax.psum(dot_tn(rows_one, mixed_grad).astype(BF16), 'dp').astype(F32)]
    convert_element_type x13 -> x16, other arithmetic: 74.5 us -> 19.2 us  [the longest x10 8.45 us: add_low(): return sum((t.astype(F32) for t in terms)).astype(BF16)]
    dynamic_update_slice x8 -> x0, local copies, waits for them, and re-layouts: 49.9 us -> none  [attend_backward(): lax.scan(one_block, (zero_rows, zero_rows), inputs)]
  transfers between devices with their start and end apart: 9 -> 46, of which waited for: 9 -> 15; matrix products, arithmetic and copies ran while one was open for 8% -> 24% of each run, Pallas kernels for 0% -> 15%
where the time goes in v1:
time: 789 us; the launch traced here: 784 us
  waiting for transfers between devices  317 us (40%)
  local copies, waits for them, and re-layouts  140 us (18%)
  Pallas kernels  115 us (15%)
  blocking collectives  67.8 us (9%)
  matrix products  49.1 us (6%)
  other arithmetic  46.6 us (6%)
  starting transfers between devices  31.9 us (4%)
  between operations  16.3 us (2%)
    unnamed x177, local copies, waits for them, and re-layouts  65.1 us
    ppermute x32, waiting for transfers between devices, hop(): return lax.ppermute(x, 'dp', [(i, i ^ bit) for i in range(size)])  65 us
    reduce_scatter x1, waiting for transfers between devices, shards(): lax.psum_scatter(dot_nt(mixed_grad, qkv_matrix).astype(BF16), 'tensor', s...  51.3 us
    pallas_call x1, Pallas kernels, attend_back(): pl.pallas_call(functools.partial(attend_back_kernel, head_dim), grid_spec...  49 us
    psum x1, waiting for transfers between devices, shards(): lax.psum(dot_tn(rows_one, mixed_grad).astype(BF16), 'dp').astype(F32)  48 us
    all_gather x1, waiting for transfers between devices, shards(): rows_one = lax.all_gather(normed_one_low, 'tensor', axis=0, tiled=True)  40.9 us
    psum x1, blocking collectives, shards(): lax.psum(jnp.stack([gain_one_grad, shift_one_grad, gain_two_grad, shift_t...  40.9 us
    dot_general x10, matrix products, dot_tn(): lax.dot_general(a, b, (((0,), (0,)), ((), ())), preferred_element_type=F32)  31.7 us
  transfers between devices with their start and end apart: 46, of which 15 were waited for; matrix products, arithmetic and copies ran while one was open for 24% of the time, Pallas kernels for 15%

profile of v1, /device:TPU:0, one launch (start us, length us, event | category | flops | bytes accessed | tf_op | source)
XLA Modules:
  0.0 784.1 jit_solution(17132829370232873350)
XLA Ops:
  13.5 16.9 %all-gather = bf16[128,1024]{1,0:T(8,128)(2,1)} all-gather(bf16[32,1024]{1,0:T(8,128)(2,1)S(1)} %constant_dynamic-slice_fusion.2), channel_id=2, replica_groups=mesh['dp'=8,'tensor'=4] {'tensor'}, dimensions={0}, use_global_device_ids=true | all-gather | bytes 327680 | tf_op jit(solution)/shard_map/all_gather | solution.py:444
  56.0 40.9 %all-gather.10.cloned.1.call-done.x_ref = bf16[2048,1024]{1,0:T(8,128)(2,1)} async-done(((bf16[512,1024]{1,0:T(8,128)(2,1)}), bf16[2048,1024]{1,0:T(8,128)(2,1)}) %all-gather.10.cloned.1.call-update) | async-done | bytes 4194320 | tf_op jit(solution)/shard_map/all_gather | solution.py:437
  101.5 7.0 project.1
  113.5 28.0 %attend.1 = (bf16[2048,256]{1,0:T(8,128)(2,1)}, f32[256,2048]{1,0:T(8,128)}, f32[8,2048]{1,0:T(8,128)}) custom-call(s32[1]{0:T(128)S(6)} %copy.83.bucket_ref, bf16[2048,256]{1,0:T(8,128)(2,1)} %copy-done.36, bf16[2048,256]{1,0:T(8,128)(2,1)} %copy-done.37, bf16[256,2048]{1,0:T(8,128)(2,1)} %copy-done.40), custom_call_target="tpu_custom_call" | custom-call | flops 17179869184 | bytes 5242880 | tf_op jit(solution)/shard_map/attend/pallas_call | solution.py:181
  168.3 26.7 %all-to-all-done = bf16[4,512,256]{1,2,0:T(8,128)(2,1)} async-done(((bf16[4,512,256]{1,2,0:T(8,128)(2,1)}), bf16[4,512,256]{1,2,0:T(8,128)(2,1)}, u32[]{:S(2)}, u32[]{:S(2)}) %all-to-all-start) | async-done | bytes 1048608 | tf_op jit(solution)/shard_map/all_to_all | solution.py:451
  241.9 6.9 feed.4
  261.2 6.9 feed.7
  272.7 6.9 feed.5
  289.0 7.0 feed.6
  318.9 10.6 %collective-permute-done.30 = bf16[256,1024]{1,0:T(8,128)(2,1)S(1)} collective-permute-done((bf16[256,1024]{1,0:T(8,128)(2,1)S(1)}, bf16[256,1024]{1,0:T(8,128)(2,1)S(1)}, u32[]{:S(2)}, u32[]{:S(2)}) %collective-permute-start.30) | collective-permute-done | bytes 524320 | tf_op jit(solution)/shard_map/ppermute | solution.py:373
  334.1 6.6 collective-permute-done.22
  347.6 19.2 %collective-permute-done.31 = bf16[512,1024]{1,0:T(8,128)(2,1)S(1)} collective-permute-done((bf16[512,1024]{1,0:T(8,128)(2,1)S(1)}, bf16[512,1024]{1,0:T(8,128)(2,1)S(1)}, u32[]{:S(2)}, u32[]{:S(2)}) %collective-permute-start.31) | collective-permute-done | bytes 1048608 | tf_op jit(solution)/shard_map/ppermute | solution.py:373
  369.3 18.0 %collective-permute-done.23 = bf16[512,1024]{1,0:T(8,128)(2,1)S(1)} collective-permute-done((bf16[512,1024]{1,0:T(8,128)(2,1)S(1)}, bf16[512,1024]{1,0:T(8,128)(2,1)S(1)}, u32[]{:S(2)}, u32[]{:S(2)}) %collective-permute-start.23) | collective-permute-done | bytes 1048608 | tf_op jit(solution)/shard_map/ppermute | solution.py:373
  424.2 13.3 %all-to-all-done.1 = bf16[512,4,256]{2,0,1:T(8,128)(2,1)S(1)} async-done(((bf16[512,4,256]{2,0,1:T(8,128)(2,1)}), bf16[512,4,256]{2,0,1:T(8,128)(2,1)S(1)}, u32[]{:S(2)}, u32[]{:S(2)}) %all-to-all-start.1) | async-done | bytes 1048608 | tf_op jit(solution)/shard_map/all_to_all | solution.py:480
  438.5 49.0 %attend_back.1 = (f32[256,2048]{1,0:T(8,128)}, f32[2048,256]{1,0:T(8,128)}, f32[2048,256]{1,0:T(8,128)}) custom-call(s32[1]{0:T(128)S(6)} %copy.83.bucket_ref, bf16[2048,256]{1,0:T(8,128)(2,1)} %copy-done.36, bf16[2048,256]{1,0:T(8,128)(2,1)} %copy-done.37, bf16[256,2048]{1,0:T(8,128)(2,1)} %copy-done.39, bf16[2048,256]{1,0:T(8,128)(2,1)} %copy-done.38, ...), custom_call_target="tpu_custom_call" | custom-call | flops 42949672960 | bytes 12582912 | tf_op jit(solution)/shard_map/attend_back/pallas_call | solution.py:274
  507.0 6.6 convolution_convert_fusion
  513.7 48.0 %all-reduce.2.cloned.1.call-done = bf16[1024,3,256]{2,0,1:T(8,128)(2,1)} async-done(((bf16[1024,3,256]{2,0,1:T(8,128)(2,1)}), bf16[1024,3,256]{2,0,1:T(8,128)(2,1)}) %all-reduce.2.cloned.1.call-update) | async-done | bytes 1572880 | tf_op jit(solution)/shard_map/psum | solution.py:492
  565.0 25.8 %all-gather.18.cloned.1.call-done = bf16[1024,1024]{1,0:T(8,128)(2,1)} async-done(((bf16[128,1024]{1,0:T(8,128)(2,1)}), bf16[1024,1024]{1,0:T(8,128)(2,1)}) %all-gather.18.cloned.1.call-update) | async-done | bytes 2097168 | tf_op jit(solution)/shard_map/all_gather | solution.py:469
  594.9 17.7 %reduce-scatter.10.cloned.1.call-done = bf16[1,32,1024]{2,1,0:T(8,128)(2,1)} async-done(((bf16[4,32,1024]{2,1,0:T(8,128)(2,1)}), bf16[1,32,1024]{2,1,0:T(8,128)(2,1)}) %reduce-scatter.10.cloned.1.call-update) | async-done | bytes 65552 | tf_op jit(solution)/shard_map/reduce_scatter | solution.py:483
  612.6 10.1 %all-gather.2 = bf16[1,256,1024]{2,1,0:T(8,128)(2,1)S(1)} all-gather(bf16[1,32,1024]{2,1,0:T(8,128)(2,1)} %reduce-scatter.10.cloned.1.call-done), channel_id=4, replica_groups=mesh['dp'=8,'tensor'=4] {'dp'}, dimensions={1}, use_global_device_ids=true | all-gather | bytes 589824 | tf_op jit(solution)/shard_map/all_gather | solution.py:484
  623.8 26.4 %all-gather.16.cloned.1.call-done = bf16[8,1024,256]{2,1,0:T(8,128)(2,1)} async-done(((bf16[1,1024,256]{2,1,0:T(8,128)(2,1)}), bf16[8,1024,256]{2,1,0:T(8,128)(2,1)}) %all-gather.16.cloned.1.call-update) | async-done | bytes 4194320 | tf_op jit(solution)/shard_map/all_gather | solution.py:468
  664.6 13.4 %copy.69 = f32[1024,2,1024]{2,1,0:T(2,128)} copy(f32[1024,2,1024]{0,2,1:T(8,128)} %bitcast.74) | data formatting | bytes 16777216
  678.0 51.3 %reduce-scatter.6.cloned.1.call-done = bf16[512,1024]{1,0:T(8,128)(2,1)} async-done(((bf16[2048,1024]{1,0:T(8,128)(2,1)}), bf16[512,1024]{1,0:T(8,128)(2,1)}) %reduce-scatter.6.cloned.1.call-update) | async-done | bytes 1048592 | tf_op jit(solution)/shard_map/reduce_scatter | solution.py:489
  731.6 40.9 %psum.14 = f32[4,1024]{1,0:T(4,128)S(1)} all-reduce(f32[4,1024]{1,0:T(4,128)S(1)} %pad_maximum_fusion.9), channel_id=1, replica_groups=mesh['dp'=8,'tensor'=4] {'dp','tensor'}, use_global_device_ids=true, to_apply=%region_13.14 | all-reduce | flops 4096 | bytes 32768 | tf_op jit(solution)/shard_map/psum | solution.py:498
  (374 shorter events, 263.6 us)
Async XLA Ops:
  7.2 89.7 %all-gather.10.cloned.1.call-start = ((), (), s32[]{:S(2)}) async-start(), calls=%async_computation.7 | async-start | bytes 5242880 | tf_op jit(solution)/shard_map/all_gather | solution.py:437
  12.6 155.8 %all-gather.20.cloned.1.call-start = ((), (), s32[]{:S(2)}) async-start(), calls=%async_computation.18 | async-start | bytes 2359296 | tf_op jit(solution)/shard_map/all_gather | solution.py:445
  30.3 185.2 %all-gather.12.cloned.1.call-start = ((), (), s32[]{:S(2)}) async-start(), calls=%async_computation.8 | async-start | bytes 2621440 | tf_op jit(solution)/shard_map/all_gather | solution.py:442
  30.4 118.1 %collective-permute-start.12 = (bf16[512,1024]{1,0:T(8,128)(2,1)}, bf16[512,1024]{1,0:T(8,128)(2,1)}, u32[]{:S(2)}, u32[]{:S(2)}) collective-permute-start(bf16[512,1024]{1,0:T(8,128)(2,1)} %param.21), channel_id=1, source_target_pairs={{0,16},{4,20},{8,24},{12,28},{16,0},{20,4},{24,8},{28,12},{1,17},{... | collective-permute-start | bytes 3145736 | tf_op jit(solution)/shard_map/ppermute | solution.py:373
  32.0 118.4 %collective-permute-start.5 = (bf16[512,1024]{1,0:T(8,128)(2,1)}, bf16[512,1024]{1,0:T(8,128)(2,1)}, u32[]{:S(2)}, u32[]{:S(2)}) collective-permute-start(bf16[512,1024]{1,0:T(8,128)(2,1)} %param.21), channel_id=1, source_target_pairs={{0,8},{4,12},{8,0},{12,4},{16,24},{20,28},{24,16},{28,20},{1,9},{5... | collective-permute-start | bytes 3145736 | tf_op jit(solution)/shard_map/ppermute | solution.py:373
  144.2 50.8 %all-to-all-start = ((bf16[4,512,256]{1,2,0:T(8,128)(2,1)}), bf16[4,512,256]{1,2,0:T(8,128)(2,1)}, u32[]{:S(2)}, u32[]{:S(2)}) async-start(bf16[4,512,256]{1,2,0:T(8,128)(2,1)} %copy.57), calls=%async_computation | async-start | bytes 2097152 | tf_op jit(solution)/shard_map/all_to_all | solution.py:451
  148.5 87.4 %all-gather.14.cloned.1.call-start = ((), (), s32[]{:S(2)}) async-start(), calls=%async_computation.9 | async-start | bytes 1310720 | tf_op jit(solution)/shard_map/all_gather | solution.py:443
  155.3 45.8 %collective-permute-start.1 = (bf16[512,1024]{1,0:T(8,128)(2,1)}, bf16[512,1024]{1,0:T(8,128)(2,1)}, u32[]{:S(2)}, u32[]{:S(2)}) collective-permute-start(bf16[512,1024]{1,0:T(8,128)(2,1)} %param.21), channel_id=1, source_target_pairs={{0,4},{4,0},{8,12},{12,8},{16,20},{20,16},{24,28},{28,24},{1,5},{5... | collective-permute-start | bytes 3145736 | tf_op jit(solution)/shard_map/ppermute | solution.py:373
  156.1 347.5 %reduce-scatter.14.cloned.1.call-start = ((), (), s32[]{:S(2)}) async-start(), calls=%async_computation.16 | async-start | bytes 1310720 | tf_op jit(solution)/shard_map/reduce_scatter | solution.py:467
  158.4 44.2 %collective-permute-start.20 = (bf16[512,1024]{1,0:T(8,128)(2,1)}, bf16[512,1024]{1,0:T(8,128)(2,1)S(1)}, u32[]{:S(2)}, u32[]{:S(2)}) collective-permute-start(bf16[512,1024]{1,0:T(8,128)(2,1)} %collective-permute-done.12), channel_id=1, source_target_pairs={{0,4},{4,0},{8,12},{12,8},{16,20},{20,16},{24,28},{28,24},{1,5},{5... | collective-permute-start | bytes 3145736 | tf_op jit(solution)/shard_map/ppermute | solution.py:373
  158.9 51.3 %collective-permute-start.6 = (bf16[512,1024]{1,0:T(8,128)(2,1)}, bf16[512,1024]{1,0:T(8,128)(2,1)}, u32[]{:S(2)}, u32[]{:S(2)}) collective-permute-start(bf16[512,1024]{1,0:T(8,128)(2,1)} %collective-permute-done.5), channel_id=1, source_target_pairs={{0,4},{4,0},{8,12},{12,8},{16,20},{20,16},{24,28},{28,24},{1,5},{5... | collective-permute-start | bytes 3145736 | tf_op jit(solution)/shard_map/ppermute | solution.py:373
  168.3 44.6 %collective-permute-start.15 = (bf16[512,1024]{1,0:T(8,128)(2,1)}, bf16[512,1024]{1,0:T(8,128)(2,1)}, u32[]{:S(2)}, u32[]{:S(2)}) collective-permute-start(bf16[512,1024]{1,0:T(8,128)(2,1)} %pad_maximum_fusion.2), channel_id=1, source_target_pairs={{0,4},{4,0},{8,12},{12,8},{16,20},{20,16},{24,28},{28,24},{1,5},{5... | collective-permute-start | bytes 3145736 | tf_op jit(solution)/shard_map/ppermute | solution.py:373
  250.0 96.2 %collective-permute-start.24 = (bf16[512,1024]{1,0:T(8,128)(2,1)}, bf16[512,1024]{1,0:T(8,128)(2,1)}, u32[]{:S(2)}, u32[]{:S(2)}) collective-permute-start(bf16[512,1024]{1,0:T(8,128)(2,1)} %slice.115), channel_id=1, source_target_pairs={{0,4},{4,0},{8,12},{12,8},{16,20},{20,16},{24,28},{28,24},{1,5},{5... | collective-permute-start | bytes 3145736 | tf_op jit(solution)/shard_map/ppermute | solution.py:373
  306.2 198.1 %reduce-scatter.8.cloned.1.call-start = ((), (), s32[]{:S(2)}) async-start(), calls=%async_computation.12 | async-start | bytes 2359296 | tf_op jit(solution)/shard_map/reduce_scatter | solution.py:482
  331.3 35.5 %collective-permute-start.31 = (bf16[512,1024]{1,0:T(8,128)(2,1)S(1)}, bf16[512,1024]{1,0:T(8,128)(2,1)S(1)}, u32[]{:S(2)}, u32[]{:S(2)}) collective-permute-start(bf16[512,1024]{1,0:T(8,128)(2,1)S(1)} %pad_maximum_fusion.6), channel_id=1, source_target_pairs={{0,16},{4,20},{8,24},{12,28},{16,0},{20,4},{24,8},{28,12},{1,17},{... | collective-permute-start | bytes 3145736 | tf_op jit(solution)/shard_map/ppermute | solution.py:373
  332.2 34.6 %collective-permute-start.28 = (bf16[512,1024]{1,0:T(8,128)(2,1)S(1)}, bf16[512,1024]{1,0:T(8,128)(2,1)S(1)}, u32[]{:S(2)}, u32[]{:S(2)}) collective-permute-start(bf16[512,1024]{1,0:T(8,128)(2,1)S(1)} %pad_maximum_fusion.5), channel_id=1, source_target_pairs={{0,8},{4,12},{8,0},{12,4},{16,24},{20,28},{24,16},{28,20},{1,9},{5... | collective-permute-start | bytes 3145736 | tf_op jit(solution)/shard_map/ppermute | solution.py:373
  344.3 43.0 %collective-permute-start.23 = (bf16[512,1024]{1,0:T(8,128)(2,1)S(1)}, bf16[512,1024]{1,0:T(8,128)(2,1)S(1)}, u32[]{:S(2)}, u32[]{:S(2)}) collective-permute-start(bf16[512,1024]{1,0:T(8,128)(2,1)S(1)} %pad_maximum_fusion.4), channel_id=1, source_target_pairs={{0,16},{4,20},{8,24},{12,28},{16,0},{20,4},{24,8},{28,12},{1,17},{... | collective-permute-start | bytes 3145736 | tf_op jit(solution)/shard_map/ppermute | solution.py:373
  346.2 41.2 %collective-permute-start.18 = (bf16[512,1024]{1,0:T(8,128)(2,1)S(1)}, bf16[512,1024]{1,0:T(8,128)(2,1)S(1)}, u32[]{:S(2)}, u32[]{:S(2)}) collective-permute-start(bf16[512,1024]{1,0:T(8,128)(2,1)S(1)} %pad_maximum_fusion.3), channel_id=1, source_target_pairs={{0,8},{4,12},{8,0},{12,4},{16,24},{20,28},{24,16},{28,20},{1,9},{5... | collective-permute-start | bytes 3145736 | tf_op jit(solution)/shard_map/ppermute | solution.py:373
  413.2 91.7 %reduce-scatter.12.cloned.1.call-start = ((), (), s32[]{:S(2)}) async-start(), calls=%async_computation.14 | async-start | bytes 2621440 | tf_op jit(solution)/shard_map/reduce_scatter | solution.py:466
  423.8 137.9 %all-reduce.2.cloned.1.call-start = ((), (), s32[]{:S(2)}) async-start(), calls=%async_computation.11 | async-start | bytes 3145728 | tf_op jit(solution)/shard_map/psum | solution.py:492
  503.5 87.4 %all-gather.18.cloned.1.call-start = ((), (), s32[]{:S(2)}) async-start(), calls=%async_computation.17 | async-start | bytes 2359296 | tf_op jit(solution)/shard_map/all_gather | solution.py:469
  504.2 108.4 %reduce-scatter.10.cloned.1.call-start = ((), (), s32[]{:S(2)}) async-start(), calls=%async_computation.13 | async-start | bytes 327680 | tf_op jit(solution)/shard_map/reduce_scatter | solution.py:483
  504.8 145.4 %all-gather.16.cloned.1.call-start = ((), (), s32[]{:S(2)}) async-start(), calls=%async_computation.15 | async-start | bytes 4718592 | tf_op jit(solution)/shard_map/all_gather | solution.py:468
  507.0 222.3 %reduce-scatter.6.cloned.1.call-start = ((), (), s32[]{:S(2)}) async-start(), calls=%async_computation.10 | async-start | bytes 5242880 | tf_op jit(solution)/shard_map/reduce_scatter | solution.py:489
  (105 other events, 1319.7 us)
Sparse Core Ops, SparseCore 0:
  12.7 84.1 all-gather.9
  98.8 26.6 all-gather.19
  127.0 68.1 all-gather.11
  196.7 26.0 all-gather.13
  306.3 25.9 reduce-scatter.13
  395.7 39.9 reduce-scatter.7
  438.0 43.8 reduce-scatter.11
  503.6 58.0 all-reduce.1
  563.6 27.2 all-gather.17
  593.0 19.6 reduce-scatter.9
  615.3 34.9 all-gather.15
  652.5 76.7 reduce-scatter.5

commit v2 on v1

--- a/solution.py
+++ b/solution.py
@@ -38,12 +38,10 @@
     half_dim = head_dim // 2
     exponents = jnp.arange(half_dim, dtype=F32) * (-2.0 / head_dim)
     freqs = jnp.exp(exponents * jnp.log(F32(rope_base)))
-    angles = places.astype(F32)[:, None] * freqs[None, :]
-    cos_table, sine_table = jnp.cos(angles), jnp.sin(angles)
     heads = width // head_dim
-    cos_wide = jnp.tile(jnp.concatenate([cos_table, cos_table], axis=1), (1, heads))
-    sine_wide = jnp.tile(jnp.concatenate([-sine_table, sine_table], axis=1), (1, heads))
-    return cos_wide, sine_wide
+    signs = jnp.tile(jnp.repeat(jnp.array([-1.0, 1.0], F32), half_dim), heads)
+    angles = places.astype(F32)[:, None] * jnp.tile(freqs, 2 * heads)[None, :]
+    return jnp.cos(angles), jnp.sin(angles) * signs
 
 
 def norm_forward(values, gain, shift):
@@ -75,13 +73,16 @@
     return jnp.where((lane >= h * head_dim) & (lane < (h + 1) * head_dim), x, jnp.zeros_like(x))
 
 
+def widen(table, width):
+    return jnp.concatenate([table] * (width // table.shape[1]), axis=1)
+
+
 def project_kernel(head_dim, x_ref, w_ref, cos_ref, sin_ref, q_ref, k_ref, v_ref, kt_ref, vt_ref):
     width = q_ref.shape[1]
-    mixed = dot_nn(x_ref[...], w_ref[...])
-    cos, sin = cos_ref[...], sin_ref[...]
-    q = mixed[:, :width]
-    k = mixed[:, width : 2 * width]
-    v = mixed[:, 2 * width :].astype(BF16)
+    x = x_ref[...]
+    cos, sin = widen(cos_ref[...], width), widen(sin_ref[...], width)
+    q, k, v = (dot_nn(x, w_ref[j]) for j in range(3))
+    v = v.astype(BF16)
     q = q * cos + swap_halves(q, head_dim) * sin
     k = k * cos + swap_halves(k, head_dim) * sin
     k_low = k.astype(BF16)
@@ -92,20 +93,21 @@
     vt_ref[...] = v.T
 
 
-def project(rows, qkv_matrix, cos_wide, sine_wide, head_dim):
+def project(rows, w, cos_wide, sine_wide, head_dim):
     n, d = rows.shape
-    width = qkv_matrix.shape[1] // 3
+    width = w.shape[2]
     block = min(512, n)
     row = pl.BlockSpec((block, width), lambda i: (i, 0))
     col = pl.BlockSpec((width, block), lambda i: (0, i))
+    table = pl.BlockSpec((block, cos_wide.shape[1]), lambda i: (i, 0))
     return pl.pallas_call(
         functools.partial(project_kernel, head_dim),
         grid=(n // block,),
         in_specs=[
             pl.BlockSpec((block, d), lambda i: (i, 0)),
-            pl.BlockSpec((d, 3 * width), lambda i: (0, 0)),
-            row,
-            row,
+            pl.BlockSpec((3, d, width), lambda i: (0, 0, 0)),
+            table,
+            table,
         ],
         out_specs=[row, row, row, col, col],
         out_shape=[jax.ShapeDtypeStruct((n, width), BF16)] * 3
@@ -115,7 +117,7 @@
             flops=6 * n * d * width, bytes_accessed=2 * n * d + 18 * n * width, transcendentals=0
         ),
         name="project",
-    )(rows, qkv_matrix, cos_wide, sine_wide)
+    )(rows, w, cos_wide, sine_wide)
 
 
 def key_range(start, block, total):
@@ -170,8 +172,8 @@
     o_ref[...] = ot_ref[...].T.astype(BF16)
 
 
-def attend(bucket, q, k, vt, head_dim):
-    n, width = q.shape
+def attend(bucket, q, k, vt, head_dim, pair, width):
+    n = q.shape[0]
     heads = width // head_dim
     block = min(1024, n)
     pairs = n * n * heads
@@ -184,9 +186,9 @@
             num_scalar_prefetch=1,
             grid=(n // block,),
             in_specs=[
-                row,
-                pl.BlockSpec((n, width), lambda i, *_: (0, 0)),
-                pl.BlockSpec((width, n), lambda i, *_: (0, 0)),
+                pl.BlockSpec((block, width), lambda i, *_: (i, pair)),
+                pl.BlockSpec((n, width), lambda i, *_: (0, pair)),
+                pl.BlockSpec((width, n), lambda i, *_: (pair, 0)),
             ],
             out_specs=[row, col, pl.BlockSpec((lanes, block), lambda i, *_: (0, i))],
             scratch_shapes=[pltpu.VMEM((n, min(512, block)), F32)],
@@ -263,25 +265,25 @@
             block(first, last, True)
 
 
-def attend_back(bucket, q, k, kt, v, g, ot, log_totals, head_dim):
-    n, width = q.shape
+def attend_back(bucket, q, k, kt, v, g, ot, log_totals, head_dim, pair, width):
+    n = q.shape[0]
     heads = width // head_dim
     block = min(512, n)
     pairs = n * n * heads
-    row = pl.BlockSpec((block, width), lambda i, *_: (i, 0))
     col = pl.BlockSpec((width, block), lambda i, *_: (0, i))
     full = pl.BlockSpec((n, width), lambda i, *_: (0, 0))
+    full_pair = pl.BlockSpec((n, width), lambda i, *_: (0, pair))
     return pl.pallas_call(
         functools.partial(attend_back_kernel, head_dim),
         grid_spec=pltpu.PrefetchScalarGridSpec(
             num_scalar_prefetch=1,
             grid=(n // block,),
             in_specs=[
-                row,
-                full,
-                pl.BlockSpec((width, n), lambda i, *_: (0, 0)),
-                full,
-                row,
+                pl.BlockSpec((block, width), lambda i, *_: (i, pair)),
+                full_pair,
+                pl.BlockSpec((width, n), lambda i, *_: (pair, 0)),
+                full_pair,
+                pl.BlockSpec((block, width), lambda i, *_: (i, 0)),
                 col,
                 pl.BlockSpec((log_totals.shape[0], block), lambda i, *_: (0, i)),
             ],
@@ -301,30 +303,42 @@
     )(bucket, q, k, kt, v, g, ot, log_totals)
 
 
-def unrotate_kernel(head_dim, dq_ref, dk_ref, dv_ref, cos_ref, sin_ref, out_ref):
-    width = dk_ref.shape[1]
+def unrotate_kernel(head_dim, pairs, *refs):
+    cos_ref, sin_ref, out_ref = refs[-3:]
     cos, sin = cos_ref[...], sin_ref[...]
-    dq = dq_ref[...].T * head_dim ** (-0.5)
-    dk = dk_ref[...]
-    out_ref[:, :width] = (dq * cos - swap_halves(dq, head_dim) * sin).astype(BF16)
-    out_ref[:, width : 2 * width] = (dk * cos - swap_halves(dk, head_dim) * sin).astype(BF16)
-    out_ref[:, 2 * width :] = dv_ref[...].astype(BF16)
-
-
-def unrotate(dq_t, dk, dv, cos_wide, sine_wide, head_dim):
-    n, width = dk.shape
+    width = cos.shape[1]
+    for pair in range(pairs):
+        dq_ref, dk_ref, dv_ref = refs[3 * pair : 3 * pair + 3]
+        dq = dq_ref[...].T * head_dim ** (-0.5)
+        dk = dk_ref[...]
+        grads = (
+            dq * cos - swap_halves(dq, head_dim) * sin,
+            dk * cos - swap_halves(dk, head_dim) * sin,
+            dv_ref[...],
+        )
+        for j, grad in enumerate(grads):
+            at = (j * pairs + pair) * width
+            out_ref[:, at : at + width] = grad.astype(BF16)
+
+
+def unrotate(grads, cos_wide, sine_wide, head_dim):
+    n, width = cos_wide.shape
+    pairs = len(grads)
     block = min(512, n)
     row = pl.BlockSpec((block, width), lambda i: (i, 0))
+    col = pl.BlockSpec((width, block), lambda i: (0, i))
     return pl.pallas_call(
-        functools.partial(unrotate_kernel, head_dim),
+        functools.partial(unrotate_kernel, head_dim, pairs),
         grid=(n // block,),
-        in_specs=[pl.BlockSpec((width, block), lambda i: (0, i)), row, row, row, row],
-        out_specs=pl.BlockSpec((block, 3 * width), lambda i: (i, 0)),
-        out_shape=jax.ShapeDtypeStruct((n, 3 * width), BF16),
+        in_specs=[col, row, row] * pairs + [row, row],
+        out_specs=pl.BlockSpec((block, 3 * pairs * width), lambda i: (i, 0)),
+        out_shape=jax.ShapeDtypeStruct((n, 3 * pairs * width), BF16),
         compiler_params=pltpu.CompilerParams(vmem_limit_bytes=40 * MIB),
-        cost_estimate=pl.CostEstimate(flops=0, bytes_accessed=26 * n * width, transcendentals=0),
+        cost_estimate=pl.CostEstimate(
+            flops=0, bytes_accessed=26 * n * width * pairs, transcendentals=0
+        ),
         name="unrotate",
-    )(dq_t, dk, dv, cos_wide, sine_wide)
+    )(*(g for pair in grads for g in pair), cos_wide, sine_wide)
 
 
 def feed_kernel(x_ref, c_ref, wgu_ref, wd_ref, h_ref, b_ref, n_ref):
@@ -368,41 +382,775 @@
     )(x, cot, wgu, wd)
 
 
-def hop(x, bit):
-    size = lax.axis_size("dp")
-    return lax.ppermute(x, "dp", [(i, i ^ bit) for i in range(size)])
-
-
-def gather_plane(a):
-    size = lax.axis_size("dp")
-    if size != 8:
-        return [lax.all_gather(a, "dp", axis=0, tiled=True)]
-    half = a.shape[0] // 2
-    from_x, from_y = hop(a, 2), hop(a, 4)
-    own_pair = jnp.concatenate([a, hop(a, 1)])
-    low, high = hop(from_y[:half], 2), hop(from_x[half:], 4)
-    x_pair = jnp.concatenate([from_x, hop(from_x, 1)])
-    y_pair = jnp.concatenate([from_y, hop(from_y, 1)])
-    far = jnp.concatenate([low, high])
-    far_pair = jnp.concatenate([far, hop(far, 1)])
-    return [own_pair, x_pair, y_pair, far_pair]
-
-
-def add_low(*terms):
-    return sum(t.astype(F32) for t in terms).astype(BF16)
-
-
-def scatter_plane(parts):
-    size = lax.axis_size("dp")
-    if size != 8:
-        return lax.psum_scatter(parts[0], "dp", scatter_dimension=0, tiled=True).astype(F32)
-    rows = parts[0].shape[0] // 2
+MESH_ID = pl.DeviceIdType.MESH
+
+
+def plane_peers():
+    me = lax.axis_index("dp")
+    return [{"dp": lax.bitwise_xor(me, bit)} for bit in (1, 2, 4)]
+
+
+def enter(peers):
+    barrier = pltpu.get_barrier_semaphore()
+    for peer in peers:
+        pl.semaphore_signal(barrier, inc=1, device_id=peer, device_id_type=MESH_ID)
+    pl.semaphore_wait(barrier, len(peers))
+
+
+def remote(src, dst, send, recv, at, peer):
+    return pltpu.make_async_remote_copy(
+        src_ref=src,
+        dst_ref=dst,
+        send_sem=send.at[at],
+        recv_sem=recv.at[at],
+        device_id=peer,
+        device_id_type=MESH_ID,
+    )
+
+
+def gather_copies(view, send, recv, placed):
+    sib, across, along = plane_peers()
+    steps = [
+        (0, 1, sib, None),
+        (0, 2, across, None),
+        (0, 4, along, None),
+        (4, 2, across, 0),
+        (2, 4, along, 1),
+        (2, 1, sib, None),
+        (4, 1, sib, None),
+        (6, 1, sib, None),
+    ]
+    copies = {}
+    for i, (s, bit, peer, part) in enumerate(steps):
+        src = view(s, part)
+        dst = src if placed else view(s ^ bit, part)
+        copies[f"{s}-{s ^ bit}"] = remote(src, dst, send, recv, i, peer)
+    return copies
+
+
+def half_of(ref, part):
+    if part is None:
+        return ref
+    half = ref.shape[-2] // 2
+    return ref.at[(slice(None),) * (len(ref.shape) - 2) + (pl.ds(part * half, half),)]
+
+
+def gather_start(copies):
+    for name in ("0-2", "0-4", "0-1"):
+        copies[name].start()
+
+
+def gather_forward(copies):
+    copies["0-2"].wait_recv()
+    copies["2-6"].start()
+    copies["2-3"].start()
+    copies["0-4"].wait_recv()
+    copies["4-6"].start()
+    copies["4-5"].start()
+
+
+def gather_finish(copies):
+    copies["2-6"].wait_recv()
+    copies["4-6"].wait_recv()
+    copies["6-7"].start()
+    for name in ("0-1", "2-3", "4-5", "6-7"):
+        copies[name].wait_recv()
+
+
+def gather_kernel(
+    cot_ref, wo_ref, cots_out, wos_out, cots_ref, wos_ref, send, recv, wsend, wrecv, zsend, zrecv, own, done
+):
+    me, z = lax.axis_index("dp"), lax.axis_index("tensor")
+    ways, out_rows = wos_ref.shape[0], wos_ref.shape[2]
+    others = [{"tensor": lax.rem(z + k, ways)} for k in range(1, ways)]
+    enter(plane_peers() + others)
+    copies = gather_copies(lambda s, part: half_of(cots_ref.at[s], part), send, recv, False)
+    loads = [
+        pltpu.make_async_copy(cot_ref, cots_ref.at[0], own.at[0]),
+        pltpu.make_async_copy(
+            wo_ref.at[pl.ds(pl.multiple_of(me * out_rows, 16), out_rows)],
+            wos_ref.at[z, me],
+            own.at[1],
+        ),
+    ]
+    for load in loads:
+        load.start()
+    loads[0].wait()
+    gather_start(copies)
+    loads[1].wait()
+    sends = []
+    for k, peer in enumerate(others):
+        mine = wos_ref.at[z, me]
+        sends.append(
+            pltpu.make_async_remote_copy(
+                src_ref=mine,
+                dst_ref=mine,
+                send_sem=zsend.at[k],
+                recv_sem=zrecv.at[z],
+                device_id=peer,
+                device_id_type=MESH_ID,
+            )
+        )
+        sends[-1].start()
+    view = lambda s, part: half_of(wos_ref.at[:, lax.bitwise_xor(me, s)], part)
+    weights = gather_copies(view, wsend, wrecv, True)
+    gather_forward(copies)
+    for k, peer in enumerate(others):
+        source = lax.rem(z + k + 1, ways)
+        theirs = wos_ref.at[source, me]
+        pltpu.make_async_remote_copy(
+            src_ref=theirs,
+            dst_ref=theirs,
+            send_sem=zsend.at[k],
+            recv_sem=zrecv.at[source],
+            device_id=peer,
+            device_id_type=MESH_ID,
+        ).wait_recv()
+    gather_start(weights)
+    gather_finish(copies)
+    gather_forward(weights)
+    gather_finish(weights)
+    stores = [
+        pltpu.make_async_copy(cots_ref, cots_out, done.at[0]),
+        pltpu.make_async_copy(wos_ref, wos_out, done.at[1]),
+    ]
+    for store in stores:
+        store.start()
+    for store in stores:
+        store.wait()
+    for copy in (*copies.values(), *weights.values(), *sends):
+        copy.wait_send()
+
+
+def gather_front(cot, w_out, ways):
+    rows, d = cot.shape
+    out_rows = w_out.shape[0] // 8
+    anywhere = pl.BlockSpec(memory_space=pl.ANY)
+    return pl.pallas_call(
+        gather_kernel,
+        in_specs=[anywhere] * 2,
+        out_specs=[anywhere] * 2,
+        out_shape=[
+            jax.ShapeDtypeStruct((8, rows, d), cot.dtype),
+            jax.ShapeDtypeStruct((ways, 8, out_rows, d), w_out.dtype),
+        ],
+        scratch_shapes=[
+            pltpu.VMEM((8, rows, d), cot.dtype),
+            pltpu.VMEM((ways, 8, out_rows, d), w_out.dtype),
+        ]
+        + [pltpu.SemaphoreType.DMA((8,))] * 4
+        + [pltpu.SemaphoreType.DMA((ways,))] * 2
+        + [pltpu.SemaphoreType.DMA((2,))] * 2,
+        compiler_params=pltpu.CompilerParams(
+            collective_id=0, has_side_effects=True, vmem_limit_bytes=40 * MIB
+        ),
+        cost_estimate=pl.CostEstimate(
+            flops=45 * 10**9, bytes_accessed=16 * rows * d, transcendentals=0
+        ),
+        name="gather_front",
+    )(cot, w_out)
+
+
+def feed_plane_kernel(
+    x_ref,
+    c_ref,
+    w_ref,
+    n_ref,
+    o_ref,
+    grads_ref,
+    wgu_ref,
+    wd_ref,
+    xs,
+    cs,
+    hid,
+    branch,
+    part,
+    from_sib,
+    from_far,
+    from_x,
+    from_y,
+    down_acc,
+    gate_up_acc,
+    gsend,
+    grecv,
+    ssend,
+    srecv,
+    csem,
+    osem,
+    xsem,
+    wsem,
+):
+    ways, unit = w_ref.shape[0], w_ref.shape[1] // 3
+    units = ways * unit
+    rows = xs.shape[1]
     half = rows // 2
-    own, x, y, far = (add_low(p[:rows], hop(p[rows:], 1)) for p in parts)
-    to_x, to_y = hop(far[:half], 2), hop(far[half:], 4)
-    y = jnp.concatenate([add_low(y[:half], to_x), y[half:]])
-    x = jnp.concatenate([x[:half], add_low(x[half:], to_y)])
-    return own.astype(F32) + hop(x, 2).astype(F32) + hop(y, 4).astype(F32)
+    low, high = pl.ds(0, half), pl.ds(half, half)
+    sib, across, along = plane_peers()
+    enter([sib, across, along])
+    copies = gather_copies(lambda s, part: half_of(xs.at[s], part), gsend, grecv, False)
+    weights = []
+    for t in range(ways):
+        at = pl.ds(t * unit, unit)
+        for j, dst in enumerate((wgu_ref.at[at], wgu_ref.at[pl.ds(units + t * unit, unit)], wd_ref.at[at])):
+            src = w_ref.at[t, pl.ds(j * unit, unit)]
+            weights.append(pltpu.make_async_copy(src, dst, wsem.at[t, j]))
+    own = pltpu.make_async_copy(x_ref, xs.at[0], xsem)
+    own.start()
+    cots = [pltpu.make_async_copy(c_ref.at[i], cs.at[i], csem.at[i]) for i in range(8)]
+    own.wait()
+    gather_start(copies)
+    for load in (*weights, *cots):
+        load.start()
+    for load in weights:
+        load.wait()
+    down_acc[...] = jnp.zeros_like(down_acc)
+    gate_up_acc[...] = jnp.zeros_like(gate_up_acc)
+
+    sums = {
+        "1": (part.at[1], from_sib.at[0], sib),
+        "3": (part.at[3], from_sib.at[1], sib),
+        "5": (part.at[5], from_sib.at[2], sib),
+        "7": (part.at[7], from_sib.at[3], sib),
+        "6l": (part.at[6, low], from_far.at[low], across),
+        "6h": (part.at[6, high], from_far.at[high], along),
+        "2l": (part.at[2, low], from_x.at[low], across),
+        "2h": (part.at[2, high], from_x.at[high], across),
+        "4l": (part.at[4, low], from_y.at[low], along),
+        "4h": (part.at[4, high], from_y.at[high], along),
+    }
+    sums = {
+        name: remote(src, dst, ssend, srecv, i, peer)
+        for i, (name, (src, dst, peer)) in enumerate(sums.items())
+    }
+
+    def out_copy(i):
+        return pltpu.make_async_copy(cs.at[i], o_ref.at[i], osem.at[i])
+
+    def grads(i, at):
+        down_acc[...] += dot_tn(hid[at], cs[i])
+        gate_up_acc[...] += dot_tn(branch[at], xs[i])
+        cs[i] = dot_nn(hid[at], wd_ref[...]).astype(BF16)
+        out_copy(i).start()
+
+    def join(i, j):
+        part[i] = (part[i].astype(F32) + from_sib[j].astype(F32)).astype(BF16)
+
+    @pl.loop(0, 8)
+    def _(i):
+        @pl.when(i == 1)
+        def _():
+            copies["0-1"].wait_recv()
+
+        @pl.when(i == 2)
+        def _():
+            gather_forward(copies)
+
+        @pl.when(i == 3)
+        def _():
+            copies["2-3"].wait_recv()
+
+        @pl.when(i == 5)
+        def _():
+            copies["4-5"].wait_recv()
+            sums["3"].wait_recv()
+            join(2, 1)
+            sums["2l"].start()
+
+        @pl.when(i == 6)
+        def _():
+            copies["2-6"].wait_recv()
+            copies["4-6"].wait_recv()
+            copies["6-7"].start()
+
+        @pl.when(i == 7)
+        def _():
+            copies["6-7"].wait_recv()
+            sums["5"].wait_recv()
+            join(4, 2)
+            sums["4h"].start()
+
+        for slot in range(8):
+
+            @pl.when(i == slot)
+            def _(slot=slot):
+                cots[slot].wait()
+
+        both = dot_nt(xs[i], wgu_ref[...])
+        gate, up = both[:, :units], both[:, units:]
+        sig = jax.nn.sigmoid(gate)
+        silu = gate * sig
+        at = jnp.where(i < 2, i, i - 2)
+        hid[at] = (silu * up).astype(BF16)
+        hidden_grad = dot_nt(cs[i], wd_ref[...])
+        branch[at, :, :units] = (hidden_grad * up * sig * (1.0 + gate * (1.0 - sig))).astype(BF16)
+        branch[at, :, units:] = (hidden_grad * silu).astype(BF16)
+        part[i] = dot_nn(branch[at], wgu_ref[...]).astype(BF16)
+        for odd in (1, 3, 5, 7):
+
+            @pl.when(i == odd)
+            def _(odd=odd):
+                sums[str(odd)].start()
+
+        @pl.when(i < 2)
+        def _():
+            grads(i, i)
+
+    @pl.loop(2, 8)
+    def _(i):
+        @pl.when(i == 3)
+        def _():
+            sums["7"].wait_recv()
+            join(6, 3)
+            sums["6l"].start()
+            sums["6h"].start()
+
+        @pl.when(i == 7)
+        def _():
+            sums["6l"].wait_recv()
+            part[4, low] = (part[4, low].astype(F32) + from_far[low].astype(F32)).astype(BF16)
+            sums["4l"].start()
+            sums["6h"].wait_recv()
+            part[2, high] = (part[2, high].astype(F32) + from_far[high].astype(F32)).astype(BF16)
+            sums["2h"].start()
+
+        grads(i, i - 2)
+
+    for t in range(ways):
+        for j, (acc, first) in enumerate(
+            ((gate_up_acc, t * unit), (gate_up_acc, units + t * unit), (down_acc, t * unit))
+        ):
+            row = (3 * t + j) * unit
+            branch[row // rows, row % rows : row % rows + unit] = acc[first : first + unit].astype(BF16)
+    grads_copy = pltpu.make_async_copy(branch.at[pl.ds(0, grads_ref.shape[0])], grads_ref, xsem)
+    grads_copy.start()
+    sums["1"].wait_recv()
+    n_ref[...] = part[0].astype(F32) + from_sib[0].astype(F32)
+    for name in ("2l", "2h", "4l", "4h"):
+        sums[name].wait_recv()
+    n_ref[...] += from_x[...].astype(F32) + from_y[...].astype(F32)
+    for copy in (*copies.values(), *sums.values()):
+        copy.wait_send()
+    for i in range(8):
+        out_copy(i).wait()
+    grads_copy.wait()
+
+
+def feed_plane(x, cot, weights):
+    rows, d = x.shape
+    ways = weights.shape[0]
+    units = ways * weights.shape[1] // 3
+    anywhere = pl.BlockSpec(memory_space=pl.ANY)
+    inside = pl.BlockSpec(memory_space=pltpu.VMEM)
+    return pl.pallas_call(
+        feed_plane_kernel,
+        in_specs=[anywhere, anywhere, anywhere],
+        out_specs=[inside, anywhere, anywhere],
+        out_shape=[
+            jax.ShapeDtypeStruct((rows, d), F32),
+            jax.ShapeDtypeStruct((8, rows, d), BF16),
+            jax.ShapeDtypeStruct((3 * units // rows, rows, d), BF16),
+        ],
+        scratch_shapes=[
+            pltpu.VMEM((2 * units, d), BF16),
+            pltpu.VMEM((units, d), BF16),
+            pltpu.VMEM((8, rows, d), BF16),
+            pltpu.VMEM((8, rows, d), BF16),
+            pltpu.VMEM((6, rows, units), BF16),
+            pltpu.VMEM((6, rows, 2 * units), BF16),
+            pltpu.VMEM((8, rows, d), BF16),
+            pltpu.VMEM((4, rows, d), BF16),
+            pltpu.VMEM((rows, d), BF16),
+            pltpu.VMEM((rows, d), BF16),
+            pltpu.VMEM((rows, d), BF16),
+            pltpu.VMEM((units, d), F32),
+            pltpu.VMEM((2 * units, d), F32),
+            pltpu.SemaphoreType.DMA((8,)),
+            pltpu.SemaphoreType.DMA((8,)),
+            pltpu.SemaphoreType.DMA((10,)),
+            pltpu.SemaphoreType.DMA((10,)),
+            pltpu.SemaphoreType.DMA((8,)),
+            pltpu.SemaphoreType.DMA((8,)),
+            pltpu.SemaphoreType.DMA,
+            pltpu.SemaphoreType.DMA((ways, 3)),
+        ],
+        compiler_params=pltpu.CompilerParams(
+            collective_id=1, has_side_effects=True, vmem_limit_bytes=62 * MIB
+        ),
+        cost_estimate=pl.CostEstimate(
+            flops=80 * 10**9, bytes_accessed=40 * rows * d, transcendentals=0
+        ),
+        name="feed_plane",
+    )(x, cot, weights)
+
+
+def tail_kernel(
+    mixed_ref,
+    w_ref,
+    ffn_parts_ref,
+    out_parts_ref,
+    rows_ref,
+    tok_ref,
+    norm_ref,
+    n_ref,
+    ffn_ref,
+    og_ref,
+    ng_ref,
+    lines,
+    line_in,
+    part,
+    from_sib,
+    from_far,
+    from_x,
+    from_y,
+    mine,
+    slices,
+    ogs,
+    norms,
+    norms_z,
+    qkv,
+    usend,
+    urecv,
+    dsend,
+    drecv,
+    ssend,
+    srecv,
+    gsend,
+    grecv,
+    osend,
+    orecv,
+    nsend,
+    nrecv,
+    zsend,
+    zrecv,
+    load_sem,
+):
+    me, z = lax.axis_index("dp"), lax.axis_index("tensor")
+    ways, rows = lines.shape[0], lines.shape[1]
+    out_rows = slices.shape[1]
+    qkv_rows = ogs.shape[1] - out_rows
+    split = rows + ways * out_rows
+    total = part.shape[1]
+    width = w_ref.shape[2]
+    half = total // 2
+    low, high = pl.ds(0, half), pl.ds(half, half)
+    sib, across, along = plane_peers()
+    others = [{"tensor": lax.rem(z + k, ways)} for k in range(1, ways)]
+    above, below = {"tensor": lax.rem(z + 1, ways)}, {"tensor": lax.rem(z + ways - 1, ways)}
+    enter([sib, across, along] + others)
+
+    loads = []
+    for i in range(8):
+        loads.append(
+            (
+                pltpu.make_async_copy(
+                    ffn_parts_ref.at[i], part.at[i, pl.ds(0, rows)], load_sem.at[0, i]
+                ),
+                pltpu.make_async_copy(
+                    out_parts_ref.at[lax.bitwise_xor(me, i)],
+                    part.at[i, pl.ds(rows, ways * out_rows)],
+                    load_sem.at[1, i],
+                ),
+            )
+        )
+        for load in loads[-1]:
+            load.start()
+
+    def line(i):
+        b = jnp.where(z >= ways // 2, i, ways - 1 - i)
+        step = min(256, rows)
+
+        @pl.loop(0, rows // step)
+        def _(k):
+            at = pl.ds(pl.multiple_of(b * rows + k * step, step), step)
+            lines[b, pl.ds(pl.multiple_of(k * step, step), step)] = sum(
+                dot_nt(mixed_ref[at, j * width : (j + 1) * width], w_ref[j]) for j in range(3)
+            ).astype(BF16)
+
+    def up_copy(b):
+        return remote(lines.at[b], line_in.at[b + 1], usend, urecv, b, above)
+
+    def down_copy(b):
+        return remote(lines.at[b], line_in.at[b], dsend, drecv, b, below)
+
+    def line_round(r):
+        b = r - (ways - 1 - z)
+
+        @pl.when((b >= 0) & (b < z))
+        def _():
+            @pl.when(z < ways - 1)
+            def _():
+                down_copy(b).wait_recv()
+                lines[b] = (lines[b].astype(F32) + line_in[b].astype(F32)).astype(BF16)
+
+            down_copy(b).start()
+
+        u = ways - 1 - (r - z)
+
+        @pl.when((u > z) & (u <= ways - 1))
+        def _():
+            @pl.when(z > 0)
+            def _():
+                up_copy(u).wait_recv()
+                lines[u] = (lines[u].astype(F32) + line_in[u + 1].astype(F32)).astype(BF16)
+
+            up_copy(u).start()
+
+    sums = [
+        ("1", part.at[1], from_sib.at[0], sib),
+        ("3", part.at[3], from_sib.at[1], sib),
+        ("5", part.at[5], from_sib.at[2], sib),
+        ("7", part.at[7], from_sib.at[3], sib),
+        ("6l", part.at[6, low], from_far.at[low], across),
+        ("6h", part.at[6, high], from_far.at[high], along),
+        ("2l", part.at[2, low], from_x.at[low], across),
+        ("2h", part.at[2, high], from_x.at[high], across),
+        ("4l", part.at[4, low], from_y.at[low], along),
+        ("4h", part.at[4, high], from_y.at[high], along),
+    ]
+    sums = {
+        name: remote(src, dst, ssend, srecv, i, peer)
+        for i, (name, src, dst, peer) in enumerate(sums)
+    }
+
+    def join(i, j):
+        part[i] = (part[i].astype(F32) + from_sib[j].astype(F32)).astype(BF16)
+
+    line(0)
+    line_round(0)
+
+    @pl.loop(0, 3)
+    def _(j):
+        at = pl.ds(pl.multiple_of(j * width, width), width)
+        qkv[at, :] = dot_tn(mixed_ref[:, at], rows_ref[...]).astype(BF16)
+
+    for i in range(8):
+        at = pl.multiple_of(lax.bitwise_xor(me, i) * qkv_rows, 16)
+        part[i, split:total] = qkv[pl.ds(at, qkv_rows), :]
+    for i in (7, 3, 5, 1):
+        for load in loads[i]:
+            load.wait()
+        sums[str(i)].start()
+
+    @pl.loop(1, ways)
+    def _(i):
+        line(i)
+
+    for i, j, names in ((6, 3, ("6l", "6h")), (2, 1, ("2l",)), (4, 2, ("4h",))):
+        for load in loads[i]:
+            load.wait()
+        sums[str(i + 1)].wait_recv()
+        join(i, j)
+        for name in names:
+            sums[name].start()
+    line_round(1)
+    sums["6l"].wait_recv()
+    part[4, low] = (part[4, low].astype(F32) + from_far[low].astype(F32)).astype(BF16)
+    sums["4l"].start()
+    sums["6h"].wait_recv()
+    part[2, high] = (part[2, high].astype(F32) + from_far[high].astype(F32)).astype(BF16)
+    sums["2h"].start()
+    for r in range(2, ways - 1):
+        line_round(r)
+
+    for load in loads[0]:
+        load.wait()
+    sums["1"].wait_recv()
+    for name in ("2l", "2h", "4l", "4h"):
+        sums[name].wait_recv()
+    for at, out in ((slice(0, rows), ffn_ref), (slice(rows, total), mine)):
+        out[...] = part[0, at].astype(F32) + from_sib[0, at].astype(F32)
+        out[...] += from_x[at].astype(F32) + from_y[at].astype(F32)
+
+    for t in range(ways):
+        at = slice(t * out_rows, (t + 1) * out_rows)
+        part[0, at] = mine[at].astype(BF16)
+
+    def slice_copy(k, to, source):
+        return pltpu.make_async_remote_copy(
+            src_ref=part.at[0, pl.ds(pl.multiple_of(to * out_rows, 16), out_rows)],
+            dst_ref=slices.at[source],
+            send_sem=osend.at[k],
+            recv_sem=orecv.at[source],
+            device_id={"tensor": to},
+            device_id_type=MESH_ID,
+        )
+
+    for k in range(1, ways):
+        slice_copy(k, lax.rem(z + k, ways), z).start()
+    own_slice = part[0, pl.ds(pl.multiple_of(z * out_rows, 16), out_rows)].astype(F32)
+    for k in range(1, ways):
+        source = lax.rem(z + k, ways)
+        slice_copy(k, source, source).wait_recv()
+        own_slice += slices[source].astype(F32)
+    ogs[me, :out_rows] = own_slice.astype(BF16)
+    ogs[me, out_rows:] = mine[ways * out_rows :].astype(BF16)
+    view = lambda s, half: half_of(ogs.at[lax.bitwise_xor(me, s)], half)
+    gathers = gather_copies(view, gsend, grecv, True)
+    gather_start(gathers)
+    gather_forward(gathers)
+    gather_finish(gathers)
+    og_ref[...] = ogs[...]
+
+    n_ref[...] = lines[z].astype(F32)
+
+    @pl.when(z < ways - 1)
+    def _():
+        down_copy(z).wait_recv()
+        n_ref[...] += line_in[z].astype(F32)
+
+    @pl.when(z > 0)
+    def _():
+        up_copy(z).wait_recv()
+        n_ref[...] += line_in[z + 1].astype(F32)
+
+    norms[0] = norm_ref[...]
+    step = min(128, rows)
+
+    @pl.loop(0, rows // step)
+    def _(i):
+        at = pl.ds(pl.multiple_of(i * step, step), step)
+        values = tok_ref[at, :].astype(F32)
+        centred = values - jnp.mean(values, axis=-1, keepdims=True)
+        root = lax.rsqrt(jnp.mean(centred * centred, axis=-1, keepdims=True) + norm_eps)
+        grad = n_ref[at, :]
+        norms[0, 0:1] += jnp.sum(grad * (centred * root), axis=0, keepdims=True)
+        norms[0, 1:2] += jnp.sum(grad, axis=0, keepdims=True)
+
+    swaps = [
+        remote(norms.at[i], norms.at[4 + i], nsend, nrecv, i, peer)
+        for i, peer in enumerate((sib, across, along))
+    ]
+    for i, swap in enumerate(swaps):
+        swap.start()
+        swap.wait_recv()
+        norms[i + 1] = norms[i] + norms[4 + i]
+
+    def norm_copy(k, to, source):
+        return pltpu.make_async_remote_copy(
+            src_ref=norms.at[3],
+            dst_ref=norms_z.at[source],
+            send_sem=zsend.at[k],
+            recv_sem=zrecv.at[source],
+            device_id={"tensor": to},
+            device_id_type=MESH_ID,
+        )
+
+    for k in range(1, ways):
+        norm_copy(k, lax.rem(z + k, ways), z).start()
+    norms_z[z] = norms[3]
+    for k in range(1, ways):
+        source = lax.rem(z + k, ways)
+        norm_copy(k, source, source).wait_recv()
+    ng_ref[...] = sum(norms_z[t] for t in range(ways))
+
+    for copy in (*sums.values(), *gathers.values(), *swaps):
+        copy.wait_send()
+    for k in range(1, ways):
+        to = lax.rem(z + k, ways)
+        slice_copy(k, to, z).wait_send()
+        norm_copy(k, to, z).wait_send()
+    for b in range(ways):
+
+        @pl.when(b < z)
+        def _():
+            down_copy(b).wait_send()
+
+        @pl.when(b > z)
+        def _():
+            up_copy(b).wait_send()
+
+
+def tail(mixed, w, ffn_parts, out_parts, rows_one, tokens, norm_grads, ways):
+    rows, d = tokens.shape
+    out_rows = out_parts.shape[1] // ways
+    qkv_rows = mixed.shape[1] // 8
+    total = rows + out_parts.shape[1] + qkv_rows
+    both = out_rows + qkv_rows
+    anywhere = pl.BlockSpec(memory_space=pl.ANY)
+    inside = pl.BlockSpec(memory_space=pltpu.VMEM)
+    sems = lambda n: [pltpu.SemaphoreType.DMA((n,))] * 2
+    return pl.pallas_call(
+        tail_kernel,
+        in_specs=[inside, inside, anywhere, anywhere, inside, inside, inside],
+        out_specs=[inside] * 4,
+        out_shape=[
+            jax.ShapeDtypeStruct((rows, d), F32),
+            jax.ShapeDtypeStruct((rows, d), F32),
+            jax.ShapeDtypeStruct((8, both, d), BF16),
+            jax.ShapeDtypeStruct((8, d), F32),
+        ],
+        scratch_shapes=[
+            pltpu.VMEM((ways, rows, d), BF16),
+            pltpu.VMEM((ways + 1, rows, d), BF16),
+            pltpu.VMEM((8, total, d), BF16),
+            pltpu.VMEM((4, total, d), BF16),
+            pltpu.VMEM((total, d), BF16),
+            pltpu.VMEM((total, d), BF16),
+            pltpu.VMEM((total, d), BF16),
+            pltpu.VMEM((total - rows, d), F32),
+            pltpu.VMEM((ways, out_rows, d), BF16),
+            pltpu.VMEM((8, both, d), BF16),
+            pltpu.VMEM((8, 8, d), F32),
+            pltpu.VMEM((ways, 8, d), F32),
+            pltpu.VMEM((mixed.shape[1], d), BF16),
+        ]
+        + sems(ways) * 2
+        + sems(10)
+        + sems(8)
+        + sems(ways)
+        + sems(3)
+        + sems(ways)
+        + [pltpu.SemaphoreType.DMA((2, 8))],
+        compiler_params=pltpu.CompilerParams(
+            collective_id=2, has_side_effects=True, vmem_limit_bytes=62 * MIB
+        ),
+        cost_estimate=pl.CostEstimate(
+            flops=75 * 10**9, bytes_accessed=40 * rows * d, transcendentals=0
+        ),
+        name="tail",
+    )(mixed, w, ffn_parts, out_parts, rows_one, tokens, norm_grads)
+
+
+def spread_kernel(out_rows, both_ref, down_ref, rest_ref, gate_up_ref, down_out_ref, qkv_ref):
+    units = both_ref.shape[1] // 2
+    for p in range(8):
+        turned = both_ref[p].astype(F32).T
+        for g in range(2):
+            at = pl.ds(2 * p + g, turned.shape[0], stride=16)
+            gate_up_ref[at, :] = turned[:, g * units : (g + 1) * units]
+    down_out_ref[...] = down_ref[0].astype(F32)
+    features = rest_ref[:, out_rows:, :].reshape(-1, rest_ref.shape[2]).astype(F32)
+    width = qkv_ref.shape[2]
+    for j in range(3):
+        qkv_ref[j] = features[j * width : (j + 1) * width].T
+
+
+def spread(grads, rest, out_rows):
+    d = grads.shape[2]
+    units = grads.shape[1] // 3
+    block = d // 8
+    width = 8 * (rest.shape[1] - out_rows) // 3
+    return pl.pallas_call(
+        functools.partial(spread_kernel, out_rows),
+        grid=(8,),
+        in_specs=[
+            pl.BlockSpec((8, 2 * units, block), lambda i: (0, 0, i)),
+            pl.BlockSpec((1, units, d), lambda i: (i, 2, 0)),
+            pl.BlockSpec((8, rest.shape[1], block), lambda i: (0, 0, i)),
+        ],
+        out_specs=[
+            pl.BlockSpec((16 * block, units), lambda i: (i, 0)),
+            pl.BlockSpec((units, d), lambda i: (i, 0)),
+            pl.BlockSpec((3, block, width), lambda i: (0, i, 0)),
+        ],
+        out_shape=[
+            jax.ShapeDtypeStruct((16 * d, units), F32),
+            jax.ShapeDtypeStruct((8 * units, d), F32),
+            jax.ShapeDtypeStruct((3, d, width), F32),
+        ],
+        compiler_params=pltpu.CompilerParams(vmem_limit_bytes=40 * MIB),
+        name="spread",
+    )(grads, grads, rest)
 
 
 def shards(
@@ -427,9 +1175,10 @@
     head_dim = d // HEADS
     hidden_width = w_down.shape[0]
     units = hidden_width // replicas
+    fast = replicas == 8
     out_rows = local_width // replicas
-    qkv_matrix = w_qkv.reshape(d, 3 * local_width)
-    cos_wide, sine_wide = rotary_wide(group_bucket[0], group_rows, head_dim, local_width)
+    pair_width = min(128, local_width)
+    pairs = local_width // pair_width
 
     rows_in = tokens.astype(F32)
     normed_one, unit_one, root_one = norm_forward(rows_in, gain_one, shift_one)
@@ -438,37 +1187,55 @@
 
     gate_up_slice = lax.dynamic_slice_in_dim(w_gate_up, replica * units, units, axis=2)
     down_slice = lax.dynamic_slice_in_dim(w_down, replica * units, units, axis=0)
-    out_slice = lax.dynamic_slice_in_dim(w_out, replica * out_rows, out_rows, axis=0)
-    gate_up_all = lax.all_gather(gate_up_slice.reshape(d, 2 * units), "tensor", axis=0)
-    down_all = lax.all_gather(down_slice, "tensor", axis=0, tiled=True)
-    out_part = lax.all_gather(out_slice, "tensor", axis=0)
-    out_full = lax.all_gather(out_part, "dp", axis=1).reshape(d, d)
-    wgu = gate_up_all.reshape(ways, d, 2, units).transpose(1, 2, 0, 3).reshape(d, 2 * ways * units)
-    cot_pieces = gather_plane(cotangent)
-
-    q, k, v, kt, vt = project(rows_one, qkv_matrix, cos_wide, sine_wide, head_dim)
-    attended, attended_t, log_totals = attend(group_bucket, q, k, vt, head_dim)
-    attended_own = lax.all_to_all(attended, "tensor", 0, 1, tiled=True)
+    weight_slice = jnp.concatenate(
+        [gate_up_slice.transpose(1, 2, 0).reshape(2 * units, d), down_slice]
+    )
+    weights = lax.all_gather(weight_slice, "tensor", axis=0)
+    if fast:
+        cot_rows, _ = lax.optimization_barrier((cotangent, normed_one_low))
+        cot_all, out_full = gather_front(cot_rows, w_out, ways)
+        cot_all, out_full, group_bucket, w_qkv = lax.optimization_barrier(
+            (cot_all, out_full, group_bucket, w_qkv)
+        )
+        out_full = out_full.reshape(d, d)
+    else:
+        cot_all = lax.all_gather(cotangent, "dp", axis=0, tiled=True)
+        out_full = lax.all_gather(w_out, "tensor", axis=0, tiled=True)
+
+    cos_wide, sine_wide = rotary_wide(group_bucket[0], group_rows, head_dim, pair_width)
+    qkv_weights = w_qkv.transpose(1, 0, 2)
+    q, k, v, kt, vt = project(rows_one, qkv_weights, cos_wide, sine_wide, head_dim)
+    attended = [attend(group_bucket, q, k, vt, head_dim, p, pair_width) for p in range(pairs)]
+    attended_own = jnp.stack(
+        [
+            lax.all_to_all(a[0], "tensor", 0, 1, tiled=True).reshape(own_rows, ways, pair_width)
+            for a in attended
+        ],
+        axis=2,
+    ).reshape(own_rows, d)
     resid = rows_in + dot_nn(attended_own, out_full)
 
     normed_two, unit_two, root_two = norm_forward(resid, gain_two, shift_two)
-    row_pieces = gather_plane(normed_two.astype(BF16))
-    fed = [feed(x, c, wgu, down_all) for x, c in zip(row_pieces, cot_pieces)]
-    normed_two_grad = scatter_plane([f[2] for f in fed])
-    hidden = [f[0] for f in fed]
-    branch = [f[1] for f in fed]
-    ffn_out = scatter_plane([dot_nn(h, down_all).astype(BF16) for h in hidden])
-    layer_out = (resid + ffn_out).astype(BF16)
-    down_grad = sum(dot_tn(h, c) for h, c in zip(hidden, cot_pieces)).astype(BF16)
-    gate_up_grad = sum(dot_tn(x, b) for x, b in zip(row_pieces, branch)).astype(BF16)
-    gate_up_grad = gate_up_grad.reshape(d, 2, ways, units).transpose(2, 0, 1, 3)
-    gate_up_grad = gate_up_grad.reshape(ways, d, 2 * units)
-    gate_up_grad = lax.psum_scatter(gate_up_grad, "tensor", scatter_dimension=0)
-    down_grad = lax.psum_scatter(down_grad, "tensor", scatter_dimension=0, tiled=True)
-    gate_up_grad = lax.all_gather(gate_up_grad, "dp", axis=0)
-    down_grad = lax.all_gather(down_grad, "dp", axis=0, tiled=True).astype(F32)
-    gate_up_grad = gate_up_grad.reshape(replicas, d, 2, units).transpose(1, 2, 0, 3)
-    gate_up_grad = gate_up_grad.reshape(d, 2, hidden_width).astype(F32)
+    normed_two_low = normed_two.astype(BF16)
+    if fast:
+        normed_two_grad, ffn_parts, grads = feed_plane(normed_two_low, cot_all, weights)
+        grads = grads.reshape(weights.shape)
+    else:
+        parts = weights.reshape(ways, 3, units, d)
+        wgu = parts[:, :2].transpose(3, 1, 0, 2).reshape(d, 2 * ways * units)
+        wd = parts[:, 2].reshape(ways * units, d)
+        rows_two = lax.all_gather(normed_two_low, "dp", axis=0, tiled=True)
+        hidden, branch, back = feed(rows_two, cot_all, wgu, wd)
+        normed_two_grad = lax.psum_scatter(back, "dp", scatter_dimension=0, tiled=True).astype(F32)
+        ffn_parts = dot_nn(hidden, wd).astype(BF16)
+        grads = jnp.concatenate(
+            [
+                dot_tn(branch, rows_two).reshape(2, ways, units, d),
+                dot_tn(hidden, cot_all).reshape(1, ways, units, d),
+            ]
+        )
+        grads = grads.astype(BF16).transpose(1, 0, 2, 3).reshape(ways, 3 * units, d)
+    grads = lax.psum_scatter(grads, "tensor", scatter_dimension=0)
 
     resid_part, gain_two_grad, shift_two_grad = norm_backward(
         normed_two_grad, unit_two, root_two, gain_two
@@ -477,27 +1244,53 @@
     attn_grad = resid_grad.astype(BF16)
 
     attended_grad_own = dot_nt(attn_grad, out_full).astype(BF16)
-    attended_grad = lax.all_to_all(attended_grad_own, "tensor", 1, 0, tiled=True)
+    attended_grad_own = attended_grad_own.reshape(own_rows, ways, pairs, pair_width)
+    attended_grad = [
+        lax.all_to_all(
+            attended_grad_own[:, :, p].reshape(own_rows, ways * pair_width), "tensor", 1, 0, tiled=True
+        )
+        for p in range(pairs)
+    ]
     out_grad = dot_tn(attended_own, attn_grad).astype(BF16).reshape(ways, replicas, out_rows, d)
-    out_grad = lax.psum_scatter(out_grad, "dp", scatter_dimension=1)
-    out_grad = lax.psum_scatter(out_grad, "tensor", scatter_dimension=0)
-    out_grad = lax.all_gather(out_grad, "dp", axis=0, tiled=True).astype(F32)
-    dq_t, dk, dv = attend_back(
-        group_bucket, q, k, kt, v, attended_grad, attended_t, log_totals, head_dim
-    )
-    mixed_grad = unrotate(dq_t, dk, dv, cos_wide, sine_wide, head_dim)
-    normed_one_grad = lax.psum_scatter(
-        dot_nt(mixed_grad, qkv_matrix).astype(BF16), "tensor", scatter_dimension=0, tiled=True
-    ).astype(F32)
-    qkv_grad = lax.psum(dot_tn(rows_one, mixed_grad).astype(BF16), "dp").astype(F32)
-    qkv_grad = qkv_grad.reshape(d, 3, local_width)
-    input_part, gain_one_grad, shift_one_grad = norm_backward(
-        normed_one_grad, unit_one, root_one, gain_one
-    )
-    token_grad = resid_grad + input_part
-    gain_one_grad, shift_one_grad, gain_two_grad, shift_two_grad = lax.psum(
-        jnp.stack([gain_one_grad, shift_one_grad, gain_two_grad, shift_two_grad]), ("dp", "tensor")
-    )
+    out_grad = out_grad.transpose(1, 0, 2, 3).reshape(replicas, ways * out_rows, d)
+    back = [
+        attend_back(
+            group_bucket, q, k, kt, v, attended_grad[p], *attended[p][1:], head_dim, p, pair_width
+        )
+        for p in range(pairs)
+    ]
+    mixed_grad = unrotate(back, cos_wide, sine_wide, head_dim)
+    grads = lax.all_gather(grads, "dp", axis=0)
+    norm_grads = jnp.zeros((8, d), F32).at[2].set(gain_two_grad).at[3].set(shift_two_grad)
+    if fast:
+        normed_one_grad, ffn_out, rest, norm_grads = tail(
+            mixed_grad, qkv_weights, ffn_parts, out_grad, rows_one, tokens, norm_grads, ways
+        )
+        gate_up_grad, down_grad, qkv_grad = spread(grads, rest, out_rows)
+        out_grad = rest[:, :out_rows].reshape(local_width, d).astype(F32)
+        gate_up_grad = gate_up_grad.reshape(d, replicas, 2, units).transpose(0, 2, 1, 3)
+        gate_up_grad = gate_up_grad.reshape(d, 2, hidden_width)
+        qkv_grad = qkv_grad.transpose(1, 0, 2)
+    else:
+        grads = grads.reshape(replicas, 3, units, d)
+        down_grad = grads[:, 2].reshape(hidden_width, d).astype(F32)
+        gate_up_grad = grads[:, :2].transpose(3, 1, 0, 2).reshape(d, 2, hidden_width).astype(F32)
+        qkv_grad = lax.psum(dot_tn(rows_one, mixed_grad).astype(BF16), "dp").astype(F32)
+        qkv_grad = qkv_grad.reshape(d, 3, local_width)
+        flat = qkv_weights.transpose(1, 0, 2).reshape(d, 3 * local_width)
+        normed_one_grad = lax.psum_scatter(
+            dot_nt(mixed_grad, flat).astype(BF16), "tensor", scatter_dimension=0, tiled=True
+        ).astype(F32)
+        ffn_out = lax.psum_scatter(ffn_parts, "dp", scatter_dimension=0, tiled=True).astype(F32)
+        out_grad = lax.psum_scatter(out_grad, "dp", scatter_dimension=0)
+        out_grad = lax.psum_scatter(out_grad, "tensor", scatter_dimension=0, tiled=True)
+        out_grad = lax.all_gather(out_grad, "dp", axis=0, tiled=True).astype(F32)
+        one = norm_backward(normed_one_grad, unit_one, root_one, gain_one)
+        norm_grads = norm_grads.at[0].set(one[1]).at[1].set(one[2])
+        norm_grads = lax.psum(norm_grads, ("dp", "tensor"))
+    layer_out = (resid + ffn_out).astype(BF16)
+    token_grad = resid_grad + norm_backward(normed_one_grad, unit_one, root_one, gain_one)[0]
+    gain_one_grad, shift_one_grad, gain_two_grad, shift_two_grad = (norm_grads[i] for i in range(4))
     return (
         layer_out,
         token_grad,

time: 789 us -> 532 us (0.67)
  waiting for transfers between devices: 317 us -> 56.9 us
  Pallas kernels: 115 us -> 352 us
  local copies, waits for them, and re-layouts: 140 us -> 43.5 us
  matrix products: 49.1 us -> 3.93 us
  blocking collectives: 67.8 us -> 22.7 us
  other arithmetic: 46.6 us -> 22.6 us
  starting transfers between devices: 31.9 us -> 11.9 us
    pallas_call x5, Pallas kernels: 31.4 us -> 265 us  [the longest x1 116 us: tail(): pl.pallas_call(tail_kernel, in_specs=[inside, inside, anywhere, anywhere,...]
    reduce_scatter x5 -> x1, waiting for transfers between devices: 69.1 us -> 0.87 us  [shards(): grads = lax.psum_scatter(grads, 'tensor', scatter_dimension=0)]
    ppermute x32 -> x0, waiting for transfers between devices: 65 us -> none  [hop(): return lax.ppermute(x, 'dp', [(i, i ^ bit) for i in range(size)])]
    all_gather x5 -> x2, waiting for transfers between devices: 52.3 us -> 0.01 us  [the longest x1 0.01 us: shards(): weights = lax.all_gather(weight_slice, 'tensor', axis=0)]
    psum x1 -> x0, waiting for transfers between devices: 48 us -> none  [shards(): lax.psum(dot_tn(rows_one, mixed_grad).astype(BF16), 'dp').astype(F32)]
    psum x1 -> x0, blocking collectives: 40.9 us -> none  [shards(): lax.psum(jnp.stack([gain_one_grad, shift_one_grad, gain_two_grad, shift_t...]
    unnamed x177 -> x110, local copies, waits for them, and re-layouts: 65.1 us -> 29.7 us
    dot_general x10 -> x1, matrix products: 31.7 us -> 1.25 us  [dot_tn(): lax.dot_general(a, b, (((0,), (0,)), ((), ())), preferred_element_type=F32)]
  transfers between devices with their start and end apart: 46 -> 7, of which waited for: 15 -> 5; matrix products, arithmetic and copies ran while one was open for 24% -> 7% of each run, Pallas kernels for 15% -> 49%
where the time goes in v2:
time: 532 us; the launch traced here: 529 us
  Pallas kernels  352 us (66%)
  waiting for transfers between devices  56.9 us (11%)
  local copies, waits for them, and re-layouts  43.5 us (8%)
  blocking collectives  22.7 us (4%)
  other arithmetic  22.6 us (4%)
  between operations  15.5 us (3%)
  starting transfers between devices  11.9 us (2%)
    pallas_call x1, Pallas kernels, tail(): pl.pallas_call(tail_kernel, in_specs=[inside, inside, anywhere, anywhere,...  116 us
    pallas_call x1, Pallas kernels, feed_plane(): pl.pallas_call(feed_plane_kernel, in_specs=[anywhere, anywhere, anywhere]...  83.8 us
    pallas_call x1, Pallas kernels, gather_front(): pl.pallas_call(gather_kernel, in_specs=[anywhere] * 2, out_specs=[anywher...  53 us
    pallas_call x2, Pallas kernels, attend_back(): pl.pallas_call(functools.partial(attend_back_kernel, head_dim), grid_spec...  51.8 us
    unnamed x110, local copies, waits for them, and re-layouts  29.7 us
    pallas_call x2, Pallas kernels, attend(): pl.pallas_call(functools.partial(attend_kernel, head_dim), grid_spec=pltp...  29.7 us
    all_to_all x2, waiting for transfers between devices, shards(): lax.all_to_all(attended_grad_own[:, :, p].reshape(own_rows, ways * pair_w...  25.6 us
    all_to_all x1, blocking collectives, shards(): lax.all_to_all(a[0], 'tensor', 0, 1, tiled=True)  22.7 us
  transfers between devices with their start and end apart: 7, of which 5 were waited for; matrix products, arithmetic and copies ran while one was open for 7% of the time, Pallas kernels for 49%

profile of v2, /device:TPU:0, one launch (start us, length us, event | category | flops | bytes accessed | tf_op | source)
XLA Modules:
  0.0 528.7 jit_solution(15788832847707375037)
XLA Ops:
  17.2 53.0 %gather_front.1 = (bf16[8,512,1024]{2,1,0:T(8,128)(2,1)S(1)}, bf16[4,8,32,1024]{3,2,1,0:T(8,128)(2,1)S(1)}) custom-call(bf16[512,1024]{1,0:T(8,128)(2,1)S(1)} %copy-done.10, bf16[256,1024]{1,0:T(8,128)(2,1)S(1)} %copy-done.19), custom_call_target="tpu_custom_call" | custom-call | flops 44999999488 | bytes 8388608 | tf_op jit(solution)/shard_map/gather_front/pallas_call | solution.py:529
  71.5 3.4 copy-done.25
  75.2 3.7 fusion.12
  79.0 18.3 %all-gather.5.cloned.1.call-done.x_ref.rows_ref = bf16[2048,1024]{1,0:T(8,128)(2,1)} async-done(((bf16[512,1024]{1,0:T(8,128)(2,1)}), bf16[2048,1024]{1,0:T(8,128)(2,1)}) %all-gather.5.cloned.1.call-update) | async-done | bytes 4194320 | tf_op jit(solution)/shard_map/all_gather | solution.py:1186
  100.9 5.7 %project.1 = (bf16[2048,256]{1,0:T(8,128)(2,1)S(1)}, bf16[2048,256]{1,0:T(8,128)(2,1)S(1)}, bf16[2048,256]{1,0:T(8,128)(2,1)S(1)}, bf16[256,2048]{1,0:T(8,128)(2,1)S(1)}, bf16[256,2048]{1,0:T(8,128)(2,1)S(1)}) custom-call(bf16[2048,1024]{1,0:T(8,128)(2,1)S(1)} %copy-done.17, bf16[3,1024,256]{2,1,0:T(8,128)(2,1)S(1)} %bitcast.55, ...), custom_call_target="tpu_custom_call" | custom-call | flops 3221225472 | bytes 13631488 | tf_op jit(solution)/shard_map/project/pallas_call | solution.py:103
  111.6 14.8 %attend.3 = (bf16[2048,128]{1,0:T(8,128)(2,1)}, f32[128,2048]{1,0:T(8,128)}, f32[8,2048]{1,0:T(8,128)}) custom-call(s32[1]{0:T(128)S(6)} %copy.49.bucket_ref, bf16[2048,256]{1,0:T(8,128)(2,1)} %copy-done.20, bf16[2048,256]{1,0:T(8,128)(2,1)} %copy-done.21, bf16[256,2048]{1,0:T(8,128)(2,1)} %copy-done.24), custom_call_target="tpu_custom_call" | custom-call | flops 8589934592 | bytes 2621440 | tf_op jit(solution)/shard_map/attend/pallas_call | solution.py:183
  128.4 4.1 all-to-all-start.1
  132.6 14.9 %attend.2 = (bf16[2048,128]{1,0:T(8,128)(2,1)}, f32[128,2048]{1,0:T(8,128)}, f32[8,2048]{1,0:T(8,128)}) custom-call(s32[1]{0:T(128)S(6)} %copy.49.bucket_ref, bf16[2048,256]{1,0:T(8,128)(2,1)} %copy-done.20, bf16[2048,256]{1,0:T(8,128)(2,1)} %copy-done.21, bf16[256,2048]{1,0:T(8,128)(2,1)} %copy-done.24), custom_call_target="tpu_custom_call" | custom-call | flops 8589934592 | bytes 2621440 | tf_op jit(solution)/shard_map/attend/pallas_call | solution.py:183
  147.5 2.2 copy.34
  149.7 11.9 %all-to-all-done.1 = bf16[4,512,128]{1,2,0:T(8,128)(2,1)} async-done(((bf16[4,512,128]{1,2,0:T(8,128)(2,1)}), bf16[4,512,128]{1,2,0:T(8,128)(2,1)}, u32[]{:S(2)}, u32[]{:S(2)}) %all-to-all-start.1) | async-done | bytes 524320 | tf_op jit(solution)/shard_map/all_to_all | solution.py:1211
  161.7 22.7 %all_to_all.70 = bf16[4,512,128]{1,2,0:T(8,128)(2,1)S(1)} all-to-all(bf16[4,512,128]{1,2,0:T(8,128)(2,1)} %copy.34), channel_id=1, replica_groups=mesh['dp'=8,'tensor'=4] {'tensor'}, dimensions={0} | all-to-all | bytes 1048576 | tf_op jit(solution)/shard_map/all_to_all | solution.py:1211
  189.6 83.8 %feed_plane.1 = (f32[512,1024]{1,0:T(8,128)}, bf16[8,512,1024]{2,1,0:T(8,128)(2,1)}, bf16[3,512,1024]{2,1,0:T(8,128)(2,1)}) custom-call(bf16[512,1024]{1,0:T(8,128)(2,1)} %add_convert_fusion.1.x_ref, bf16[8,512,1024]{2,1,0:T(8,128)(2,1)} %copy-done.25, bf16[4,384,1024]{2,1,0:T(8,128)(2,1)} %bitcast.74), custom_call_target="tpu_custom_call" | custom-call | flops 80000000000 | bytes 20971520 | tf_op jit(solution)/shard_map/feed_plane/pallas_call | solution.py:744
  275.0 2.6 multiply_reduce_fusion
  281.8 2.3 fusion.19
  285.0 4.2 all-to-all-start.2
  293.0 25.3 %all-to-all-done.2 = bf16[512,4,128]{2,0,1:T(8,128)(2,1)} async-done(((bf16[512,4,128]{2,0,1:T(8,128)(2,1)}), bf16[512,4,128]{2,0,1:T(8,128)(2,1)}, u32[]{:S(2)}, u32[]{:S(2)}) %all-to-all-start.2) | async-done | bytes 524320 | tf_op jit(solution)/shard_map/all_to_all | solution.py:1249
  318.3 3.5 all-to-all-start.3
  321.9 25.8 %attend_back.2 = (f32[128,2048]{1,0:T(8,128)}, f32[2048,128]{1,0:T(8,128)}, f32[2048,128]{1,0:T(8,128)}) custom-call(s32[1]{0:T(128)S(6)} %copy.49.bucket_ref, bf16[2048,256]{1,0:T(8,128)(2,1)} %copy-done.20, bf16[2048,256]{1,0:T(8,128)(2,1)} %copy-done.21, bf16[256,2048]{1,0:T(8,128)(2,1)} %copy-done.23, bf16[2048,256]{1,0:T(8,128)(2,1)} %copy-done.22, ...), custom_call_target="tpu_custom_call" | custom-call | flops 21474836480 | bytes 6291456 | tf_op jit(solution)/shard_map/attend_back/pallas_call | solution.py:276
  349.6 26.0 %attend_back.3 = (f32[128,2048]{1,0:T(8,128)}, f32[2048,128]{1,0:T(8,128)}, f32[2048,128]{1,0:T(8,128)}) custom-call(s32[1]{0:T(128)S(6)} %copy.49.bucket_ref, bf16[2048,256]{1,0:T(8,128)(2,1)} %copy-done.20, bf16[2048,256]{1,0:T(8,128)(2,1)} %copy-done.21, bf16[256,2048]{1,0:T(8,128)(2,1)} %copy-done.23, bf16[2048,256]{1,0:T(8,128)(2,1)} %copy-done.22, ...), custom_call_target="tpu_custom_call" | custom-call | flops 21474836480 | bytes 6291456 | tf_op jit(solution)/shard_map/attend_back/pallas_call | solution.py:276
  379.4 3.3 unrotate.1.mixed_ref
  384.4 116.5 %tail.1 = (f32[512,1024]{1,0:T(8,128)}, f32[512,1024]{1,0:T(8,128)}, bf16[8,128,1024]{2,1,0:T(8,128)(2,1)}, f32[8,1024]{1,0:T(8,128)}) custom-call(bf16[2048,768]{1,0:T(8,128)(2,1)} %copy-done.6, bf16[3,1024,256]{2,1,0:T(8,128)(2,1)} %bitcast.54, bf16[8,512,1024]{2,1,0:T(8,128)(2,1)} %get-tuple-element.93.ffn_parts_ref, bf16[8,128,1024]{2,1,0:T(8,128)(2,1)} %bitcast.61, ...), custom_call_target="tpu_custom_call" | custom-call | flops 74999996416 | bytes 20971520 | tf_op jit(solution)/shard_map/tail/pallas_call | solution.py:1072
  502.0 2.5 multiply_reduce_fusion.3
  510.9 2.8 copy-done
  513.7 8.1 %spread.1 = (f32[16384,128]{1,0:T(8,128)}, f32[1024,1024]{1,0:T(8,128)}, f32[3,1024,256]{2,1,0:T(8,128)}) custom-call(bf16[8,384,1024]{2,1,0:T(8,128)(2,1)S(1)} %copy-done, bf16[8,384,1024]{2,1,0:T(8,128)(2,1)S(1)} %copy-done, bf16[8,128,1024]{2,1,0:T(8,128)(2,1)S(1)} %copy-done.5), custom_call_target="tpu_custom_call" | custom-call | tf_op jit(solution)/shard_map/spread/pallas_call | solution.py:1133
  (159 shorter events, 52.0 us)
Async XLA Ops:
  7.2 90.1 %all-gather.5.cloned.1.call-start = ((), (), s32[]{:S(2)}) async-start(), calls=%async_computation.5 | async-start | bytes 5242880 | tf_op jit(solution)/shard_map/all_gather | solution.py:1186
  12.5 177.1 %all-gather.9.cloned.1.call-start = ((), (), s32[]{:S(2)}) async-start(), calls=%async_computation.8 | async-start | bytes 3932160 | tf_op jit(solution)/shard_map/all_gather | solution.py:1193
  17.2 57.7 %copy-start.53 = (f32[2]{0:T(128)S(1)}, f32[2]{0:T(128)}, u32[]{:S(2)}) copy-start(f32[2]{0:T(128)} %constant.102.clone) | copy-start | bytes 28
  79.0 27.7 %copy-start.1 = (f32[2048,128]{1,0:T(8,128)}, f32[2048,128]{1,0:T(8,128)S(1)}, u32[]{:S(2)}) copy-start(f32[2048,128]{1,0:T(8,128)S(1)} %get-tuple-element.114.sin_ref.refs_7_) | copy-start | bytes 3145732
  79.0 27.7 %copy-start.3 = (f32[2048,128]{1,0:T(8,128)}, f32[2048,128]{1,0:T(8,128)S(1)}, u32[]{:S(2)}) copy-start(f32[2048,128]{1,0:T(8,128)S(1)} %get-tuple-element.115.cos_ref.refs_6_) | copy-start | bytes 3145732
  128.4 33.2 %all-to-all-start.1 = ((bf16[4,512,128]{1,2,0:T(8,128)(2,1)}), bf16[4,512,128]{1,2,0:T(8,128)(2,1)}, u32[]{:S(2)}, u32[]{:S(2)}) async-start(bf16[4,512,128]{1,2,0:T(8,128)(2,1)} %copy.35), calls=%async_computation.1 | async-start | bytes 1048576 | tf_op jit(solution)/shard_map/all_to_all | solution.py:1211
  132.6 215.9 %reduce-scatter.2.cloned.1.call-start = ((), (), s32[]{:S(2)}) async-start(), calls=%async_computation.6 | async-start | bytes 3932160 | tf_op jit(solution)/shard_map/reduce_scatter | solution.py:1238
  147.5 38.0 %copy-start.8 = (bf16[4,8,32,1024]{3,2,1,0:T(8,128)(2,1)S(1)}, bf16[4,8,32,1024]{3,2,1,0:T(8,128)(2,1)}, u32[]{:S(2)}) copy-start(bf16[4,8,32,1024]{3,2,1,0:T(8,128)(2,1)} %copy-done.7) | copy-start | bytes 6291460
  161.6 23.8 %copy-start.30 = (bf16[512,1024]{1,0:T(8,128)(2,1)S(1)}, bf16[512,1024]{1,0:T(8,128)(2,1)}, u32[]{:S(2)}) copy-start(bf16[512,1024]{1,0:T(8,128)(2,1)} %tok_ref.1) | copy-start | bytes 3145732
  281.8 7.4 %copy-start.38 = (bf16[512,4,2,128]{0,3,2,1:T(8,128)(2,1)S(1)}, bf16[512,4,2,128]{0,3,2,1:T(8,128)(2,1)}, u32[]{:S(2)}) copy-start(bf16[512,4,2,128]{0,3,2,1:T(8,128)(2,1)} %copy-done.37) | copy-start | bytes 3145732
  284.1 5.1 copy-start.35
  285.0 33.3 %all-to-all-start.2 = ((bf16[512,4,128]{2,0,1:T(8,128)(2,1)}), bf16[512,4,128]{2,0,1:T(8,128)(2,1)}, u32[]{:S(2)}, u32[]{:S(2)}) async-start(bf16[512,4,128]{2,0,1:T(8,128)(2,1)} %bitcast.59), calls=%async_computation.2 | async-start | bytes 1048576 | tf_op jit(solution)/shard_map/all_to_all | solution.py:1249
  293.0 54.6 %copy-start.47 = (f32[8,1024]{1,0:T(8,128)}, f32[8,1024]{1,0:T(8,128)S(1)}, u32[]{:S(2)}) copy-start(f32[8,1024]{1,0:T(8,128)S(1)} %scatter.9.norm_ref) | copy-start | bytes 98308
  318.3 30.5 %all-to-all-start.3 = ((bf16[512,4,128]{2,0,1:T(8,128)(2,1)}), bf16[512,4,128]{2,0,1:T(8,128)(2,1)S(1)}, u32[]{:S(2)}, u32[]{:S(2)}) async-start(bf16[512,4,128]{2,0,1:T(8,128)(2,1)} %bitcast.50), calls=%async_computation.3 | async-start | bytes 1048576 | tf_op jit(solution)/shard_map/all_to_all | solution.py:1249
  321.8 189.1 %all-gather.7.cloned.1.call-start = ((), (), s32[]{:S(2)}) async-start(), calls=%async_computation.7 | async-start | bytes 7077888 | tf_op jit(solution)/shard_map/all_gather | solution.py:1263
  349.6 26.0 %copy-start.2 = (f32[2048,128]{1,0:T(8,128)S(1)}, f32[2048,128]{1,0:T(8,128)}, u32[]{:S(2)}) copy-start(f32[2048,128]{1,0:T(8,128)} %copy-done.1) | copy-start | bytes 3145732
  349.6 26.0 %copy-start.4 = (f32[2048,128]{1,0:T(8,128)S(1)}, f32[2048,128]{1,0:T(8,128)}, u32[]{:S(2)}) copy-start(f32[2048,128]{1,0:T(8,128)} %copy-done.3) | copy-start | bytes 3145732
  349.6 26.1 %copy-start.11 = (f32[128,2048]{1,0:T(8,128)S(1)}, f32[128,2048]{1,0:T(8,128)}, u32[]{:S(2)}) copy-start(f32[128,2048]{1,0:T(8,128)} %get-tuple-element.85.refs_0_) | copy-start | bytes 3145732
  349.6 26.1 %copy-start.12 = (f32[2048,128]{1,0:T(8,128)S(1)}, f32[2048,128]{1,0:T(8,128)}, u32[]{:S(2)}) copy-start(f32[2048,128]{1,0:T(8,128)} %get-tuple-element.86.refs_1_) | copy-start | bytes 3145732
  349.6 26.1 %copy-start.13 = (f32[2048,128]{1,0:T(8,128)S(1)}, f32[2048,128]{1,0:T(8,128)}, u32[]{:S(2)}) copy-start(f32[2048,128]{1,0:T(8,128)} %get-tuple-element.87.refs_2_) | copy-start | bytes 3145732
  384.4 117.6 %copy-start.31 = (bf16[512,1024]{1,0:T(8,128)(2,1)S(1)}, bf16[512,1024]{1,0:T(8,128)(2,1)}, u32[]{:S(2)}) copy-start(bf16[512,1024]{1,0:T(8,128)(2,1)} %tok_ref.1) | copy-start | bytes 3145732
  384.4 117.6 %copy-start.43 = (f32[512]{0:T(512)S(1)}, f32[512]{0:T(512)}, u32[]{:S(2)}) copy-start(f32[512]{0:T(512)} %copy-done.42) | copy-start | bytes 6148
  384.4 117.6 %copy-start.46 = (f32[1024]{0:T(1024)S(1)}, f32[1024]{0:T(1024)}, u32[]{:S(2)}) copy-start(f32[1024]{0:T(1024)} %param.18) | copy-start | bytes 12292
  384.4 117.6 %copy-start.49 = (f32[512]{0:T(512)S(1)}, f32[512]{0:T(512)}, u32[]{:S(2)}) copy-start(f32[512]{0:T(512)} %copy-done.48) | copy-start | bytes 6148
  (37 other events, 75.6 us)
Sparse Core Ops, SparseCore 0:
  12.6 84.6 all-gather.4
  98.9 84.1 all-gather.8
  273.5 74.9 reduce-scatter.1
  350.3 50.6 all-gather.6

commit v3 on v2

v3 whole, which is shorter than its diff:
```python
import functools

import jax
import jax.numpy as jnp
from jax import lax
from jax.experimental import pallas as pl
from jax.experimental.pallas import tpu as pltpu
from jax.sharding import PartitionSpec as P

HEADS = 16
LONG_LEN = 2048
SHORT_LEN = 1000

norm_eps = 1e-05
mask_fill = -1e30
rope_base = 10000.0
VMEM_LIMIT = 62 * 2**20
F32 = jnp.float32
BF16 = jnp.bfloat16


def dot_nn(a, b):
    return jnp.dot(a, b, preferred_element_type=F32)


def dot_nt(a, b):
    return lax.dot_general(a, b, (((1,), (1,)), ((), ())), preferred_element_type=F32)


def dot_tn(a, b):
    return lax.dot_general(a, b, (((0,), (0,)), ((), ())), preferred_element_type=F32)


def rotary_wide(bucket_id, group_rows, head_dim, width):
    positions = jnp.arange(group_rows, dtype=jnp.int32)
    span_len = jnp.where(bucket_id == 1, LONG_LEN, SHORT_LEN).astype(jnp.int32)
    places = positions - (positions // span_len) * span_len
    half_dim = head_dim // 2
    exponents = jnp.arange(half_dim, dtype=F32) * (-2.0 / head_dim)
    freqs = jnp.exp(exponents * jnp.log(F32(rope_base)))
    heads = width // head_dim
    signs = jnp.tile(jnp.repeat(jnp.array([-1.0, 1.0], F32), half_dim), heads)
    angles = places.astype(F32)[:, None] * jnp.tile(freqs, 2 * heads)[None, :]
    return jnp.cos(angles), jnp.sin(angles) * signs


def norm_forward(values, gain, shift):
    average = jnp.mean(values, axis=-1, keepdims=True)
    centred = values - average
    spread_sq = jnp.mean(centred * centred, axis=-1, keepdims=True)
    inv_root = lax.rsqrt(spread_sq + norm_eps)
    unit_rows = centred * inv_root
    return (unit_rows * gain + shift, unit_rows, inv_root)


def norm_backward(out_grad_rows, unit_rows, inv_root, gain):
    scaled = out_grad_rows * gain
    first_mean = jnp.mean(scaled, axis=-1, keepdims=True)
    second_mean = jnp.mean(scaled * unit_rows, axis=-1, keepdims=True)
    in_grad = inv_root * (scaled - first_mean - unit_rows * second_mean)
    return (in_grad, jnp.sum(out_grad_rows * unit_rows, axis=0), jnp.sum(out_grad_rows, axis=0))


def swap_halves(x, head_dim):
    half = head_dim // 2
    width = x.shape[1]
    lane = lax.broadcasted_iota(jnp.int32, x.shape, 1) % head_dim
    return jnp.where(lane < half, pltpu.roll(x, width - half, 1), pltpu.roll(x, half, 1))


def head_mask(x, h, head_dim):
    lane = lax.broadcasted_iota(jnp.int32, x.shape, 1)
    return jnp.where((lane >= h * head_dim) & (lane < (h + 1) * head_dim), x, jnp.zeros_like(x))


def widen(table, width):
    return jnp.concatenate([table] * (width // table.shape[1]), axis=1)


def project_kernel(head_dim, x_ref, w_ref, cos_ref, sin_ref, q_ref, k_ref, v_ref, kt_ref, vt_ref):
    width = q_ref.shape[1]
    x = x_ref[...]
    cos, sin = widen(cos_ref[...], width), widen(sin_ref[...], width)
    q, k, v = (dot_nn(x, w_ref[j]) for j in range(3))
    v = v.astype(BF16)
    q = q * cos + swap_halves(q, head_dim) * sin
    k = k * cos + swap_halves(k, head_dim) * sin
    k_low = k.astype(BF16)
    q_ref[...] = (q.astype(BF16).astype(F32) * head_dim ** (-0.5)).astype(BF16)
    k_ref[...] = k_low
    v_ref[...] = v
    kt_ref[...] = k_low.T
    vt_ref[...] = v.T


def project(rows, w, cos_wide, sine_wide, head_dim):
    n, d = rows.shape
    width = w.shape[2]
    block = min(512, n)
    row = pl.BlockSpec((block, width), lambda i: (i, 0))
    col = pl.BlockSpec((width, block), lambda i: (0, i))
    table = pl.BlockSpec((block, cos_wide.shape[1]), lambda i: (i, 0))
    return pl.pallas_call(
        functools.partial(project_kernel, head_dim),
        grid=(n // block,),
        in_specs=[
            pl.BlockSpec((block, d), lambda i: (i, 0)),
            pl.BlockSpec((3, d, width), lambda i: (0, 0, 0)),
            table,
            table,
        ],
        out_specs=[row, row, row, col, col],
        out_shape=[jax.ShapeDtypeStruct((n, width), BF16)] * 3
        + [jax.ShapeDtypeStruct((width, n), BF16)] * 2,
        compiler_params=pltpu.CompilerParams(vmem_limit_bytes=VMEM_LIMIT),
        cost_estimate=pl.CostEstimate(
            flops=6 * n * d * width, bytes_accessed=2 * n * d + 18 * n * width, transcendentals=0
        ),
        name="project",
    )(rows, w, cos_wide, sine_wide)


def key_range(start, block, total):
    first = (start // SHORT_LEN) * SHORT_LEN
    last = min(total, ((start + block - 1) // SHORT_LEN + 1) * SHORT_LEN)
    return (first // 256) * 256, min(total, -(-last // 256) * 256)


def window_bias(key_start, keys, row_start, rows, total):
    key_at = lax.broadcasted_iota(jnp.int32, (keys, rows), 0) + key_start
    row_at = lax.broadcasted_iota(jnp.int32, (keys, rows), 1) + row_start
    key_window = jnp.zeros_like(key_at)
    row_window = jnp.zeros_like(row_at)
    for edge in range(SHORT_LEN, total, SHORT_LEN):
        key_window += (key_at >= edge).astype(jnp.int32)
        row_window += (row_at >= edge).astype(jnp.int32)
    return jnp.where(key_window == row_window, 0.0, mask_fill)


def attend_kernel(head_dim, bucket_ref, q_ref, k_ref, vt_ref, o_ref, ot_ref, l_ref, bias_ref):
    rows, width = q_ref.shape
    total = k_ref.shape[0]
    heads = width // head_dim
    step = pl.program_id(0)

    def block(at, first, last, masked):
        @pl.loop(0, heads)
        def _(h):
            hs = pl.ds(pl.multiple_of(h * head_dim, head_dim), head_dim)
            scores = dot_nt(k_ref[first:last, :], head_mask(q_ref[at, :], h, head_dim))
            if masked:
                scores = scores + bias_ref[: last - first, :]
            top = jnp.max(scores, axis=0, keepdims=True)
            weights = jnp.exp(scores - top)
            totals = jnp.sum(weights, axis=0, keepdims=True)
            ot_ref[hs, at] = dot_nn(vt_ref[hs, first:last], weights.astype(BF16)) / totals
            l_ref[pl.ds(h, 1), at] = top + jnp.log(totals)

    @pl.when(bucket_ref[0] == 1)
    def _():
        block(slice(0, rows), 0, total, False)

    sub = bias_ref.shape[1]
    for start in range(0, total, sub):
        first, last = key_range(start, sub, total)

        @pl.when((bucket_ref[0] != 1) & (step == start // rows))
        def _():
            bias_ref[: last - first, :] = window_bias(first, last - first, start, sub, total)
            block(slice(start % rows, start % rows + sub), first, last, True)

    o_ref[...] = ot_ref[...].T.astype(BF16)


def attend(bucket, q, k, vt, head_dim):
    n, width = q.shape
    heads = width // head_dim
    block = min(1024, n)
    pairs = n * n * heads
    lanes = -(-heads // 8) * 8
    row = pl.BlockSpec((block, width), lambda i, *_: (i, 0))
    col = pl.BlockSpec((width, block), lambda i, *_: (0, i))
    return pl.pallas_call(
        functools.partial(attend_kernel, head_dim),
        grid_spec=pltpu.PrefetchScalarGridSpec(
            num_scalar_prefetch=1,
            grid=(n // block,),
            in_specs=[
                row,
                pl.BlockSpec((n, width), lambda i, *_: (0, 0)),
                pl.BlockSpec((width, n), lambda i, *_: (0, 0)),
            ],
            out_specs=[row, col, pl.BlockSpec((lanes, block), lambda i, *_: (0, i))],
            scratch_shapes=[pltpu.VMEM((n, min(512, block)), F32)],
        ),
        out_shape=[
            jax.ShapeDtypeStruct((n, width), BF16),
            jax.ShapeDtypeStruct((width, n), F32),
            jax.ShapeDtypeStruct((lanes, n), F32),
        ],
        compiler_params=pltpu.CompilerParams(vmem_limit_bytes=VMEM_LIMIT),
        cost_estimate=pl.CostEstimate(
            flops=pairs * 1024, bytes_accessed=10 * n * width, transcendentals=pairs
        ),
        name="attend",
    )(bucket, q, k, vt)


def attend_back_kernel(
    head_dim,
    bucket_ref,
    q_ref,
    k_ref,
    kt_ref,
    v_ref,
    g_ref,
    ot_ref,
    l_ref,
    cos_ref,
    sin_ref,
    out_ref,
    bias_ref,
    gt_ref,
    dq_ref,
    dk_ref,
    dv_ref,
):
    rows, width = q_ref.shape
    total = k_ref.shape[0]
    heads = width // head_dim
    step = pl.program_id(0)

    @pl.when(step == 0)
    def _():
        dk_ref[...] = jnp.zeros_like(dk_ref)
        dv_ref[...] = jnp.zeros_like(dv_ref)

    gt_ref[...] = g_ref[...].astype(F32).T * ot_ref[...]

    def block(first, last, masked):
        keys = slice(first, last)

        @pl.loop(0, heads)
        def _(h):
            hs = pl.ds(pl.multiple_of(h * head_dim, head_dim), head_dim)
            qh, gh = head_mask(q_ref[...], h, head_dim), head_mask(g_ref[...], h, head_dim)
            scores = dot_nt(k_ref[keys, :], qh)
            if masked:
                scores = scores + bias_ref[: last - first, :]
            probs = jnp.exp(scores - l_ref[pl.ds(h, 1), :])
            prob_grad = dot_nt(v_ref[keys, :], gh)
            delta = jnp.sum(gt_ref[hs, :], axis=0, keepdims=True)
            score_grad = (probs * (prob_grad - delta)).astype(BF16)
            dv_ref[keys, :] += dot_nn(probs.astype(BF16), gh)
            dk_ref[keys, :] += dot_nn(score_grad, qh)
            dq_ref[hs, :] = dot_nn(kt_ref[hs, keys], score_grad)

    @pl.when(bucket_ref[0] == 1)
    def _():
        block(0, total, False)

    for start in range(0, total, rows):
        first, last = key_range(start, rows, total)

        @pl.when((bucket_ref[0] != 1) & (step == start // rows))
        def _():
            bias_ref[: last - first, :] = window_bias(first, last - first, start, rows, total)
            block(first, last, True)

    def turn_back(grad, at):
        cos, sin = widen(cos_ref[at, :], width), widen(sin_ref[at, :], width)
        return (grad * cos - swap_halves(grad, head_dim) * sin).astype(BF16)

    at = pl.ds(pl.multiple_of(step * rows, rows), rows)
    out_ref[at, :width] = turn_back(dq_ref[...].T * head_dim ** (-0.5), at)

    @pl.when(step == pl.num_programs(0) - 1)
    def _():
        @pl.loop(0, total // rows)
        def _(i):
            at = pl.ds(pl.multiple_of(i * rows, rows), rows)
            out_ref[at, width : 2 * width] = turn_back(dk_ref[at, :], at)
            out_ref[at, 2 * width :] = dv_ref[at, :].astype(BF16)


def attend_back(bucket, q, k, kt, v, g, ot, log_totals, cos_wide, sine_wide, head_dim):
    n, width = q.shape
    heads = width // head_dim
    block = min(512, n)
    pairs = n * n * heads
    row = pl.BlockSpec((block, width), lambda i, *_: (i, 0))
    col = pl.BlockSpec((width, block), lambda i, *_: (0, i))
    full = lambda rows, cols: pl.BlockSpec((rows, cols), lambda i, *_: (0, 0))
    table = full(n, cos_wide.shape[1])
    return pl.pallas_call(
        functools.partial(attend_back_kernel, head_dim),
        grid_spec=pltpu.PrefetchScalarGridSpec(
            num_scalar_prefetch=1,
            grid=(n // block,),
            in_specs=[
                row,
                full(n, width),
                full(width, n),
                full(n, width),
                row,
                col,
                pl.BlockSpec((log_totals.shape[0], block), lambda i, *_: (0, i)),
                table,
                table,
            ],
            out_specs=full(n, 3 * width),
            scratch_shapes=[
                pltpu.VMEM((n, block), F32),
                pltpu.VMEM((width, block), F32),
                pltpu.VMEM((width, block), F32),
                pltpu.VMEM((n, width), F32),
                pltpu.VMEM((n, width), F32),
            ],
        ),
        out_shape=jax.ShapeDtypeStruct((n, 3 * width), BF16),
        compiler_params=pltpu.CompilerParams(vmem_limit_bytes=VMEM_LIMIT),
        cost_estimate=pl.CostEstimate(
            flops=pairs * 2560, bytes_accessed=24 * n * width, transcendentals=pairs
        ),
        name="attend_back",
    )(bucket, q, k, kt, v, g, ot, log_totals, cos_wide, sine_wide)


def feed_kernel(x_ref, c_ref, wgu_ref, wd_ref, h_ref, b_ref, n_ref):
    units = wd_ref.shape[0]
    both = dot_nn(x_ref[...], wgu_ref[...])
    gate, up = both[:, :units], both[:, units:]
    sig = jax.nn.sigmoid(gate)
    silu = gate * sig
    h_ref[...] = (silu * up).astype(BF16)
    hidden_grad = dot_nt(c_ref[...], wd_ref[...])
    b_ref[:, :units] = (hidden_grad * up * sig * (1.0 + gate * (1.0 - sig))).astype(BF16)
    b_ref[:, units:] = (hidden_grad * silu).astype(BF16)
    n_ref[...] = dot_nt(b_ref[...], wgu_ref[...]).astype(BF16)


def feed(x, cot, wgu, wd):
    n, d = x.shape
    units = wd.shape[0]
    block = min(256, n)
    row = lambda w: pl.BlockSpec((block, w), lambda i: (i, 0))
    return pl.pallas_call(
        feed_kernel,
        grid=(n // block,),
        in_specs=[
            row(d),
            row(d),
            pl.BlockSpec((d, 2 * units), lambda i: (0, 0)),
            pl.BlockSpec((units, d), lambda i: (0, 0)),
        ],
        out_specs=[row(units), row(2 * units), row(d)],
        out_shape=[
            jax.ShapeDtypeStruct((n, units), BF16),
            jax.ShapeDtypeStruct((n, 2 * units), BF16),
            jax.ShapeDtypeStruct((n, d), BF16),
        ],
        compiler_params=pltpu.CompilerParams(vmem_limit_bytes=VMEM_LIMIT),
        cost_estimate=pl.CostEstimate(
            flops=10 * n * d * units, bytes_accessed=8 * n * d, transcendentals=n * units
        ),
        name="feed",
    )(x, cot, wgu, wd)


MESH_ID = pl.DeviceIdType.MESH


def plane_peers():
    me = lax.axis_index("dp")
    return [{"dp": lax.bitwise_xor(me, bit)} for bit in (1, 2, 4)]


def enter(peers):
    barrier = pltpu.get_barrier_semaphore()
    for peer in peers:
        pl.semaphore_signal(barrier, inc=1, device_id=peer, device_id_type=MESH_ID)
    pl.semaphore_wait(barrier, len(peers))


def remote(src, dst, send, recv, at, peer):
    return pltpu.make_async_remote_copy(
        src_ref=src,
        dst_ref=dst,
        send_sem=send.at[at],
        recv_sem=recv.at[at],
        device_id=peer,
        device_id_type=MESH_ID,
    )


def gather_copies(view, send, recv, placed, cores=True):
    sib, across, along = plane_peers()
    steps = [
        (0, 1, sib, None),
        (0, 2, across, None),
        (0, 4, along, None),
        (4, 2, across, 0),
        (2, 4, along, 1),
        (2, 1, sib, None),
        (4, 1, sib, None),
        (6, 1, sib, None),
    ]
    copies = {}
    for i, (s, bit, peer, part) in enumerate(steps):
        if bit == 1 and not cores:
            continue
        src = view(s, part)
        dst = src if placed else view(s ^ bit, part)
        copies[f"{s}-{s ^ bit}"] = remote(src, dst, send, recv, i, peer)
    return copies


def half_of(ref, part):
    if part is None:
        return ref
    half = ref.shape[-2] // 2
    return ref.at[(slice(None),) * (len(ref.shape) - 2) + (pl.ds(part * half, half),)]


def gather_start(copies):
    for name in ("0-2", "0-4", "0-1"):
        copies[name].start()


def gather_forward(copies):
    copies["0-2"].wait_recv()
    copies["2-6"].start()
    copies["2-3"].start()
    copies["0-4"].wait_recv()
    copies["4-6"].start()
    copies["4-5"].start()


def gather_finish(copies):
    copies["2-6"].wait_recv()
    copies["4-6"].wait_recv()
    copies["6-7"].start()
    for name in ("0-1", "2-3", "4-5", "6-7"):
        copies[name].wait_recv()


def head_share():
    core, z = lax.rem(lax.axis_index("dp"), 2), lax.axis_index("tensor")
    return core, 2 * lax.rem(z, 2) + core, z // 2


def head_source(s):
    return s % 2, 2 * lax.rem(lax.axis_index("dp"), 2) + s // 2


def front_kernel(
    head_dim,
    bucket_ref,
    tok_ref,
    gain_ref,
    shift_ref,
    freq_ref,
    cot_ref,
    wo_ref,
    wq_ref,
    q_ref,
    k_ref,
    v_ref,
    kt_ref,
    vt_ref,
    cos_ref,
    sin_ref,
    bucket_out,
    rows_out,
    cots_out,
    wos_out,
    wq_out,
    rows_all,
    mine,
    other,
    cots,
    wos,
    wq,
    buckets,
    nsend,
    nrecv,
    csend,
    crecv,
    wsend,
    wrecv,
    qsend,
    qrecv,
    zsend,
    zrecv,
    psend,
    precv,
    bsend,
    brecv,
    local,
):
    ways, rows, d = rows_all.shape
    half = rows // 2
    out_rows = wos.shape[2]
    width = q_ref.shape[1]
    me, z = lax.axis_index("dp"), lax.axis_index("tensor")
    core, heads_of, group_of = head_share()
    sib, across, along = plane_peers()
    others = [{"tensor": lax.rem(z + k, ways)} for k in range(1, ways)]
    z1, z2, z3 = (lax.bitwise_xor(z, k) for k in (1, 2, 3))
    near, far = {"tensor": z1}, {"tensor": z2}
    chip_rows = wq.shape[1] // 4
    enter([sib, across, along] + others)

    buckets[0] = jnp.full(buckets.shape[1:], bucket_ref[0], jnp.int32)
    bucket_copy = remote(buckets.at[0], buckets.at[1], bsend, brecv, 0, sib)
    bucket_copy.start()
    loads = [
        pltpu.make_async_copy(cot_ref.at[pl.ds(0, half)], cots.at[0], local.at[0]),
        pltpu.make_async_copy(
            wo_ref.at[pl.ds(pl.multiple_of(me * out_rows, 16), out_rows)],
            wos.at[z, me],
            local.at[1],
        ),
    ]
    for load in loads:
        load.start()

    def chip_part(chip, part):
        size = chip_rows if part is None else chip_rows // 2
        first = chip * chip_rows + (0 if part is None else part * size)
        return wq.at[:, pl.ds(pl.multiple_of(first, 16), size)]

    chip = me // 2
    chip_src = wq_ref.at[:, pl.ds(pl.multiple_of(chip * chip_rows, 16), chip_rows)]
    gives = core == lax.rem(z, 2)

    def piece_copy(k):
        return pltpu.make_async_remote_copy(
            src_ref=chip_src,
            dst_ref=chip_part(chip, None),
            send_sem=psend.at[k],
            recv_sem=precv.at[0],
            device_id={"tensor": z // 2 + 2 * k},
            device_id_type=MESH_ID,
        )

    piece_own = pltpu.make_async_copy(chip_src, chip_part(chip, None), local.at[2])
    for k in range(2):

        @pl.when(gives & (z // 2 + 2 * k != z))
        def _():
            piece_copy(k).start()

    @pl.when(heads_of == z)
    def _():
        piece_own.start()

    cot_copies = gather_copies(
        lambda s, part: half_of(cots.at[s], part), csend, crecv, False
    )
    loads[0].wait()
    gather_start(cot_copies)

    step = 128

    @pl.loop(0, rows // step)
    def _(i):
        at = pl.ds(pl.multiple_of(i * step, step), step)
        values = tok_ref[at, :].astype(F32)
        centred = values - jnp.mean(values, axis=-1, keepdims=True)
        root = lax.rsqrt(jnp.mean(centred * centred, axis=-1, keepdims=True) + norm_eps)
        mine[at, :] = (centred * root * gain_ref[...] + shift_ref[...]).astype(BF16)

    def part_of(which):
        return pl.ds(pl.multiple_of(which * half, half), half)

    def rows_at(block, which):
        return rows_all.at[block, part_of(which)]

    home = group_of == core
    give = [
        remote(mine.at[part_of(1 - core)], rows_at(z, 1 - core), nsend, nrecv, 0, sib),
        remote(mine.at[part_of(core)], rows_at(z, core), nsend, nrecv, 1, sib),
    ]
    swap = remote(mine.at[part_of(1 - core)], other, nsend, nrecv, 0, sib)
    to_far = remote(other, rows_at(z, core), nsend, nrecv, 2, far)
    to_near = remote(rows_at(z, core), rows_at(z, core), nsend, nrecv, 3, near)
    relay = remote(rows_at(z2, core), rows_at(z2, core), nsend, nrecv, 4, near)
    shares = {
        b: remote(rows_at(block, core), rows_at(block, core), nsend, nrecv, 4 + b, sib)
        for b, block in ((1, z1), (2, z2), (3, z3))
    }

    @pl.when(home)
    def _():
        give[0].start()
        give[1].start()
        rows_all[z] = mine[...]
        swap.wait_recv()
        to_far.start()
        to_near.start()

    @pl.when(jnp.logical_not(home))
    def _():
        swap.start()
        other[...] = mine[part_of(core), :]
        to_far.start()
        give[0].wait_recv()
        to_near.start()

    loads[1].wait()
    out_sends = []
    for k, peer in enumerate(others):
        slice_ref = wos.at[z, me]
        out_sends.append(
            pltpu.make_async_remote_copy(
                src_ref=slice_ref,
                dst_ref=slice_ref,
                send_sem=zsend.at[k],
                recv_sem=zrecv.at[z],
                device_id=peer,
                device_id_type=MESH_ID,
            )
        )
        out_sends[-1].start()

    qkv_copies = gather_copies(
        lambda s, part: chip_part(lax.bitwise_xor(chip, s // 2), part), qsend, qrecv, True, False
    )
    out_copies = gather_copies(
        lambda s, part: half_of(wos.at[:, lax.bitwise_xor(me, s)], part), wsend, wrecv, True
    )

    @pl.when(heads_of == z)
    def _():
        piece_own.wait()

    @pl.when(heads_of != z)
    def _():
        piece_copy(0).wait_recv()

    qkv_copies["0-2"].start()
    qkv_copies["0-4"].start()
    gather_forward(cot_copies)

    bucket_copy.wait_recv()
    bucket = jnp.where(home, buckets[0], buckets[1])
    bucket_out[...] = bucket
    span = jnp.where(bucket[0:1] == 1, LONG_LEN, SHORT_LEN)
    freq = freq_ref[...]
    lane = lax.broadcasted_iota(jnp.int32, freq.shape, 1)
    sign = jnp.where(lax.rem(lane, head_dim) < head_dim // 2, -1.0, 1.0)
    total = ways * rows

    @pl.loop(0, total // step)
    def _(i):
        at = pl.ds(pl.multiple_of(i * step, step), step)
        position = lax.broadcasted_iota(jnp.int32, (step, freq.shape[1]), 0) + i * step
        place = position
        for k in range(1, -(-total // SHORT_LEN)):
            place = place - jnp.where(position >= k * span, span, 0)
        angles = place.astype(F32) * freq
        cos_ref[at, :] = jnp.cos(angles)
        sin_ref[at, :] = jnp.sin(angles) * sign

    to_far.wait_recv()
    relay.start()
    shares[2].start()
    to_near.wait_recv()
    shares[1].start()
    qkv_copies["0-2"].wait_recv()
    qkv_copies["2-6"].start()
    qkv_copies["0-4"].wait_recv()
    qkv_copies["4-6"].start()
    for k, peer in enumerate(others):
        source = lax.rem(z + k + 1, ways)
        theirs = wos.at[source, me]
        pltpu.make_async_remote_copy(
            src_ref=theirs,
            dst_ref=theirs,
            send_sem=zsend.at[k],
            recv_sem=zrecv.at[source],
            device_id=peer,
            device_id_type=MESH_ID,
        ).wait_recv()
    gather_start(out_copies)
    qkv_copies["2-6"].wait_recv()
    qkv_copies["4-6"].wait_recv()
    wq_copy = pltpu.make_async_copy(wq, wq_out, local.at[0])
    wq_copy.start()

    @pl.when(jnp.logical_not(home))
    def _():
        give[1].wait_recv()

    @pl.loop(0, ways)
    def _(i):
        @pl.when(i == 1)
        def _():
            shares[1].wait_recv()

        @pl.when(i == 2)
        def _():
            shares[2].wait_recv()
            gather_forward(out_copies)

        @pl.when(i == 3)
        def _():
            relay.wait_recv()
            shares[3].start()
            shares[3].wait_recv()

        block = lax.bitwise_xor(z, i)
        at = pl.ds(pl.multiple_of(block * rows, rows), rows)
        x = rows_all[block]
        cos, sin = widen(cos_ref[at, :], width), widen(sin_ref[at, :], width)
        q, k, v = (dot_nn(x, wq[j]) for j in range(3))
        v = v.astype(BF16)
        q = q * cos + swap_halves(q, head_dim) * sin
        k = (k * cos + swap_halves(k, head_dim) * sin).astype(BF16)
        q_ref[at, :] = (q.astype(BF16).astype(F32) * head_dim ** (-0.5)).astype(BF16)
        k_ref[at, :] = k
        v_ref[at, :] = v
        kt_ref[:, at] = k.T
        vt_ref[:, at] = v.T

    gather_finish(cot_copies)
    gather_finish(out_copies)
    stores = [
        wq_copy,
        pltpu.make_async_copy(rows_all, rows_out, local.at[1]),
        pltpu.make_async_copy(cots, cots_out, local.at[2]),
        pltpu.make_async_copy(wos, wos_out, local.at[3]),
    ]
    for store in stores[1:]:
        store.start()
    for store in stores:
        store.wait()

    @pl.when(home)
    def _():
        give[0].wait_send()
        give[1].wait_send()

    @pl.when(jnp.logical_not(home))
    def _():
        swap.wait_send()

    for k in range(2):

        @pl.when(gives & (z // 2 + 2 * k != z))
        def _():
            piece_copy(k).wait_send()

    for copy in (to_far, to_near, relay, bucket_copy, *shares.values(), *out_sends):
        copy.wait_send()
    for copy in (*qkv_copies.values(), *cot_copies.values(), *out_copies.values()):
        copy.wait_send()


def front(bucket, tokens, gain, shift, cot, w_out, w_qkv, head_dim, ways):
    rows, d = tokens.shape
    width = w_qkv.shape[2]
    out_rows = w_out.shape[0] // 8
    total = ways * rows
    lanes = 128
    half_dim = head_dim // 2
    exponents = jnp.arange(half_dim, dtype=F32) * (-2.0 / head_dim)
    freq = jnp.tile(jnp.exp(exponents * jnp.log(F32(rope_base))), lanes // half_dim)[None]
    anywhere = pl.BlockSpec(memory_space=pl.ANY)
    inside = pl.BlockSpec(memory_space=pltpu.VMEM)
    sems = lambda n: [pltpu.SemaphoreType.DMA((n,))] * 2
    shape = jax.ShapeDtypeStruct
    return pl.pallas_call(
        functools.partial(front_kernel, head_dim),
        in_specs=[pl.BlockSpec(memory_space=pltpu.SMEM)] + [inside] * 4 + [anywhere] * 3,
        out_specs=[inside] * 8 + [anywhere] * 4,
        out_shape=[
            shape((total, width), BF16),
            shape((total, width), BF16),
            shape((total, width), BF16),
            shape((width, total), BF16),
            shape((width, total), BF16),
            shape((total, lanes), F32),
            shape((total, lanes), F32),
            shape((8, lanes), jnp.int32),
            shape((ways, rows, d), BF16),
            shape((8, rows // 2, d), BF16),
            shape((ways, 8, out_rows, d), BF16),
            shape(w_qkv.shape, BF16),
        ],
        scratch_shapes=[
            pltpu.VMEM((ways, rows, d), BF16),
            pltpu.VMEM((rows, d), BF16),
            pltpu.VMEM((rows // 2, d), BF16),
            pltpu.VMEM((8, rows // 2, d), BF16),
            pltpu.VMEM((ways, 8, out_rows, d), BF16),
            pltpu.VMEM(w_qkv.shape, BF16),
            pltpu.VMEM((2, 8, lanes), jnp.int32),
        ]
        + sems(8)
        + sems(8)
        + sems(8)
        + sems(8)
        + sems(ways)
        + sems(2)
        + sems(1)
        + [pltpu.SemaphoreType.DMA((4,))],
        compiler_params=pltpu.CompilerParams(
            collective_id=0, has_side_effects=True, vmem_limit_bytes=VMEM_LIMIT
        ),
        cost_estimate=pl.CostEstimate(
            flops=55 * 10**9, bytes_accessed=32 * rows * d, transcendentals=0
        ),
        name="front",
    )(bucket, tokens, gain[None], shift[None], freq, cot, w_out, w_qkv)


def column(ways):
    me, z = lax.axis_index("dp"), lax.axis_index("tensor")
    sib = lax.bitwise_xor(me, 1)
    others = [{"dp": sib, "tensor": z}]
    for k in range(1, ways):
        to = lax.rem(z + k, ways)
        others += [{"dp": me, "tensor": to}, {"dp": sib, "tensor": to}]
    return others


def collect_kernel(
    att_ref,
    tok_ref,
    wo_ref,
    gain_ref,
    shift_ref,
    cot_ref,
    at_ref,
    resid_ref,
    n_ref,
    cots_out,
    at,
    cots,
    isend,
    irecv,
    csend,
    crecv,
    lsem,
):
    ways, rows, quarter = at.shape
    me, z = lax.axis_index("dp"), lax.axis_index("tensor")
    core, heads_of, group_of = head_share()
    enter(column(ways) + plane_peers()[1:])
    half = rows // 2
    cot_own = pltpu.make_async_copy(cot_ref.at[pl.ds(half, half)], cots.at[0], lsem.at[1])
    cot_own.start()

    def in_copy(to):
        return pltpu.make_async_remote_copy(
            src_ref=att_ref.at[pl.ds(pl.multiple_of(to * rows, rows), rows)],
            dst_ref=at.at[heads_of],
            send_sem=isend.at[to],
            recv_sem=irecv.at[heads_of],
            device_id={"dp": me - core + group_of, "tensor": to},
            device_id_type=MESH_ID,
        )

    def in_wait(s):
        return pltpu.make_async_remote_copy(
            src_ref=att_ref.at[pl.ds(0, rows)],
            dst_ref=at.at[s],
            send_sem=isend.at[0],
            recv_sem=irecv.at[s],
            device_id={"dp": me - core + group_of, "tensor": z},
            device_id_type=MESH_ID,
        )

    own_at = group_of == core
    in_own = pltpu.make_async_copy(
        att_ref.at[pl.ds(pl.multiple_of(z * rows, rows), rows)], at.at[heads_of], lsem.at[0]
    )
    for k in range(ways - 1, 0, -1):
        in_copy(lax.bitwise_xor(z, k)).start()

    @pl.when(own_at)
    def _():
        in_own.start()
        in_own.wait()

    @pl.when(jnp.logical_not(own_at))
    def _():
        in_copy(z).start()

    copies = gather_copies(lambda s, part: half_of(cots.at[s], part), csend, crecv, False)
    cot_own.wait()
    gather_start(copies)
    gather_forward(copies)

    for s in range(ways):
        source_core, source_z = head_source(s)

        @pl.when(jnp.logical_not((source_core == core) & (source_z == z)))
        def _():
            in_wait(s).wait_recv()

    step = min(256, rows)

    @pl.loop(0, rows // step)
    def _(k):
        rs = pl.ds(pl.multiple_of(k * step, step), step)
        acc = tok_ref[rs, :].astype(F32)
        for s in range(ways):
            acc += dot_nn(at[s, rs, :], wo_ref[s * quarter : (s + 1) * quarter, :])
            at_ref[s, rs, :] = at[s, rs, :]
        resid_ref[rs, :] = acc
        centred = acc - jnp.mean(acc, axis=-1, keepdims=True)
        root = lax.rsqrt(jnp.mean(centred * centred, axis=-1, keepdims=True) + norm_eps)
        n_ref[rs, :] = (centred * root * gain_ref[...] + shift_ref[...]).astype(BF16)

    gather_finish(copies)
    cots_copy = pltpu.make_async_copy(cots, cots_out, lsem.at[1])
    cots_copy.start()
    for copy in copies.values():
        copy.wait_send()
    for k in range(1, ways):
        in_copy(lax.bitwise_xor(z, k)).wait_send()

    @pl.when(jnp.logical_not(own_at))
    def _():
        in_copy(z).wait_send()

    cots_copy.wait()


def collect(attended, tokens, out_full, gain, shift, cot, ways):
    rows, d = tokens.shape
    quarter = d // ways
    anywhere = pl.BlockSpec(memory_space=pl.ANY)
    inside = pl.BlockSpec(memory_space=pltpu.VMEM)
    return pl.pallas_call(
        collect_kernel,
        in_specs=[anywhere] + [inside] * 4 + [anywhere],
        out_specs=[inside] * 3 + [anywhere],
        out_shape=[
            jax.ShapeDtypeStruct((ways, rows, quarter), BF16),
            jax.ShapeDtypeStruct((rows, d), F32),
            jax.ShapeDtypeStruct((rows, d), BF16),
            jax.ShapeDtypeStruct((8, rows // 2, d), BF16),
        ],
        scratch_shapes=[
            pltpu.VMEM((ways, rows, quarter), BF16),
            pltpu.VMEM((8, rows // 2, d), BF16),
            pltpu.SemaphoreType.DMA((ways,)),
            pltpu.SemaphoreType.DMA((ways,)),
            pltpu.SemaphoreType.DMA((8,)),
            pltpu.SemaphoreType.DMA((8,)),
            pltpu.SemaphoreType.DMA((2,)),
        ],
        compiler_params=pltpu.CompilerParams(
            collective_id=3, has_side_effects=True, vmem_limit_bytes=VMEM_LIMIT
        ),
        cost_estimate=pl.CostEstimate(
            flops=30 * 10**9, bytes_accessed=16 * rows * d, transcendentals=0
        ),
        name="collect",
    )(attended, tokens, out_full, gain[None], shift[None], cot)


def middle_kernel(
    x_ref,
    at_ref,
    resid_ref,
    wo_ref,
    c_low_ref,
    c_high_ref,
    w_low_ref,
    w_high_ref,
    gain_ref,
    ag_ref,
    rg_ref,
    og_ref,
    out_ref,
    grads_ref,
    ng_ref,
    wgu_ref,
    wd_ref,
    xs,
    cs,
    hid,
    branch,
    part,
    from_sib,
    from_far,
    from_x,
    from_y,
    down_acc,
    gate_up_acc,
    resid,
    at,
    agr,
    gsend,
    grecv,
    ssend,
    srecv,
    fsend,
    frecv,
    osend,
    orecv,
    csem,
    wsem,
    lsem,
    credit,
):
    ways, split = w_low_ref.shape[:2]
    unit = 2 * split // 3
    units = ways * unit
    rows, d = x_ref.shape
    quarter = d // ways
    half = rows // 2
    low, high = pl.ds(0, half), pl.ds(half, half)
    me, z = lax.axis_index("dp"), lax.axis_index("tensor")
    core, heads_of, group_of = head_share()
    sib, across, along = plane_peers()
    enter(column(ways) + [across, along])

    own_at = group_of == core
    half_wo = ways // 2
    step = min(256, rows)
    own = pltpu.make_async_copy(x_ref, xs.at[0], lsem.at[0])
    own.start()
    first_loads = [
        pltpu.make_async_copy(at_ref, at, lsem.at[1]),
        pltpu.make_async_copy(resid_ref, resid, lsem.at[2]),
    ]
    cots = [
        pltpu.make_async_copy(ref.at[i], cs.at[i, side], csem.at[i, k])
        for i in range(8)
        for k, (ref, side) in enumerate(((c_low_ref, low), (c_high_ref, high)))
    ]
    weights = []
    for t in range(ways):
        dst = pl.ds(t * unit, unit)
        places = (wgu_ref.at[dst], wgu_ref.at[pl.ds(units + t * unit, unit)], wd_ref.at[dst])
        for j, place in enumerate(places):
            for k, (ref, first) in enumerate(((w_low_ref, 0), (w_high_ref, split))):
                start = max(j * unit, first)
                size = min((j + 1) * unit, first + split) - start
                if size > 0:
                    src = ref.at[t, pl.ds(start - first, size)]
                    dst_rows = place.at[pl.ds(start - j * unit, size)]
                    weights.append(pltpu.make_async_copy(src, dst_rows, wsem.at[t, j, k]))
    own.wait()
    copies = gather_copies(lambda s, side: half_of(xs.at[s], side), gsend, grecv, False)
    gather_start(copies)
    for load in (*weights, *cots, *first_loads):
        load.start()
    down_acc[...] = jnp.zeros_like(down_acc)
    gate_up_acc[...] = jnp.zeros_like(gate_up_acc)
    for load in weights:
        load.wait()

    def plane_sums(send, recv, src, landing):
        steps = [
            ("1", src(1), landing[0], sib),
            ("3", src(3), landing[1], sib),
            ("5", src(5), landing[2], sib),
            ("7", src(7), landing[3], sib),
            ("6l", src(6).at[low], from_far.at[low], across),
            ("6h", src(6).at[high], from_far.at[high], along),
            ("2l", src(2).at[low], from_x.at[low], across),
            ("2h", src(2).at[high], from_x.at[high], across),
            ("4l", src(4).at[low], from_y.at[low], along),
            ("4h", src(4).at[high], from_y.at[high], along),
        ]
        return {
            name: remote(ref, dst, send, recv, i, peer)
            for i, (name, ref, dst, peer) in enumerate(steps)
        }

    def add_to(ref, other):
        ref[...] = (ref[...].astype(F32) + other[...].astype(F32)).astype(BF16)

    def slot(i):
        return i // 2 if i % 2 == 0 else 4 + (i // 2) % 2

    landing = [from_sib.at[0], from_sib.at[1], from_sib.at[2], from_sib.at[0]]
    sums = plane_sums(ssend, srecv, lambda i: part.at[slot(i)], landing)

    def grads(i, place):
        down_acc[...] += dot_tn(hid[place], cs[i])
        gate_up_acc[...] += dot_tn(branch[place], xs[i])
        cs[i] = dot_nn(hid[place], wd_ref[...]).astype(BF16)

    @pl.loop(0, 8)
    def _(i):
        @pl.when(i == 1)
        def _():
            copies["0-1"].wait_recv()

        @pl.when(i == 2)
        def _():
            gather_forward(copies)

        @pl.when(i == 3)
        def _():
            copies["2-3"].wait_recv()

        @pl.when(i == 4)
        def _():
            sums["1"].wait_recv()
            add_to(part.at[0], from_sib.at[0])

        @pl.when(i == 5)
        def _():
            copies["4-5"].wait_recv()
            sums["3"].wait_recv()
            add_to(part.at[1], from_sib.at[1])
            sums["2l"].start()
            sums["1"].wait_send()

        @pl.when(i == 6)
        def _():
            copies["2-6"].wait_recv()
            copies["4-6"].wait_recv()
            copies["6-7"].start()

        @pl.when(i == 7)
        def _():
            copies["6-7"].wait_recv()
            sums["5"].wait_recv()
            add_to(part.at[2], from_sib.at[2])
            sums["4h"].start()
            sums["3"].wait_send()

        for k in range(8):

            @pl.when(i == k)
            def _(k=k):
                cots[2 * k].wait()
                cots[2 * k + 1].wait()

        both = dot_nt(xs[i], wgu_ref[...])
        gate, up = both[:, :units], both[:, units:]
        sig = jax.nn.sigmoid(gate)
        silu = gate * sig
        place = jnp.where(i < 2, i, i - 2)
        hid[place] = (silu * up).astype(BF16)
        hidden_grad = dot_nt(cs[i], wd_ref[...])
        branch[place, :, :units] = (
            hidden_grad * up * sig * (1.0 + gate * (1.0 - sig))
        ).astype(BF16)
        branch[place, :, units:] = (hidden_grad * silu).astype(BF16)
        even = lax.rem(i, 2) == 0
        into = jnp.where(even, i // 2, 4 + lax.rem(i // 2, 2))
        part[into] = dot_nn(branch[place], wgu_ref[...]).astype(BF16)
        for odd in (1, 3, 5, 7):

            @pl.when(i == odd)
            def _(odd=odd):
                sums[str(odd)].start()

        @pl.when(i < 2)
        def _():
            grads(i, i)

    @pl.loop(2, 8)
    def _(i):
        @pl.when(i == 3)
        def _():
            sums["7"].wait_recv()
            add_to(part.at[3], from_sib.at[0])
            sums["6l"].start()
            sums["6h"].start()

        @pl.when(i == 7)
        def _():
            sums["6l"].wait_recv()
            add_to(part.at[2, low], from_far.at[low])
            sums["4l"].start()
            sums["6h"].wait_recv()
            add_to(part.at[1, high], from_far.at[high])
            sums["2h"].start()

        grads(i, i - 2)

    pl.semaphore_signal(credit.at[0], inc=1, device_id=sib, device_id_type=MESH_ID)
    for copy in copies.values():
        copy.wait_send()
    for t in range(ways):
        for j, (acc, first) in enumerate(
            ((gate_up_acc, t * unit), (gate_up_acc, units + t * unit), (down_acc, t * unit))
        ):
            row = (3 * t + j) * unit
            branch[row // rows, row % rows : row % rows + unit] = acc[first : first + unit].astype(
                BF16
            )
    for load in first_loads:
        load.wait()
    grads_copy = pltpu.make_async_copy(branch.at[pl.ds(0, grads_ref.shape[0])], grads_ref, lsem.at[1])
    wo_loads = [
        pltpu.make_async_copy(wo_ref.at[pl.ds(0, rows)], branch.at[3], lsem.at[2]),
        pltpu.make_async_copy(wo_ref.at[pl.ds(rows, rows)], branch.at[4], lsem.at[3]),
        pltpu.make_async_copy(c_low_ref.at[0], xs.at[3, low], lsem.at[0]),
        pltpu.make_async_copy(c_high_ref.at[0], xs.at[3, high], lsem.at[4]),
    ]
    grads_copy.start()
    for load in wo_loads:
        load.start()

    outs = plane_sums(
        fsend,
        frecv,
        lambda i: cs.at[i],
        [from_sib.at[0], from_sib.at[1], from_sib.at[2], branch.at[5]],
    )
    pl.semaphore_wait(credit.at[0], 1)
    for name in ("7", "3", "5", "1"):
        outs[name].start()

    grad = gate_up_acc
    for name in ("2l", "2h", "4l", "4h"):
        sums[name].wait_recv()

    @pl.loop(0, rows // step)
    def _(k):
        rs = pl.ds(pl.multiple_of(k * step, step), step)
        grad[rs, :] = (
            part[0, rs, :].astype(F32) + from_x[rs, :].astype(F32) + from_y[rs, :].astype(F32)
        )

    pl.semaphore_signal(credit.at[1], inc=1, device_id=across, device_id_type=MESH_ID)
    pl.semaphore_signal(credit.at[2], inc=1, device_id=along, device_id_type=MESH_ID)
    outs["7"].wait_recv()
    add_to(cs.at[6], branch.at[5])
    pl.semaphore_wait(credit.at[1], 1)
    pl.semaphore_wait(credit.at[2], 1)
    outs["6l"].start()
    outs["6h"].start()
    outs["3"].wait_recv()
    add_to(cs.at[2], from_sib.at[1])
    outs["2l"].start()
    outs["5"].wait_recv()
    add_to(cs.at[4], from_sib.at[2])
    outs["4h"].start()

    for load in wo_loads:
        load.wait()
    ng_ref[...] = jnp.zeros_like(ng_ref)
    gain = gain_ref[...]
    small = min(128, rows)

    @pl.loop(0, rows // small)
    def _(k):
        rs = pl.ds(pl.multiple_of(k * small, small), small)
        values = resid[rs, :]
        centred = values - jnp.mean(values, axis=-1, keepdims=True)
        root = lax.rsqrt(jnp.mean(centred * centred, axis=-1, keepdims=True) + norm_eps)
        unit_rows = centred * root
        out_grad = grad[rs, :]
        ng_ref[2:3] += jnp.sum(out_grad * unit_rows, axis=0, keepdims=True)
        ng_ref[3:4] += jnp.sum(out_grad, axis=0, keepdims=True)
        scaled = out_grad * gain
        first_mean = jnp.mean(scaled, axis=-1, keepdims=True)
        second_mean = jnp.mean(scaled * unit_rows, axis=-1, keepdims=True)
        total = xs[3, rs, :].astype(F32) + root * (scaled - first_mean - unit_rows * second_mean)
        grad[rs, :] = total
        xs[1, rs, :] = total.astype(BF16)

    rg_copy = pltpu.make_async_copy(grad.at[pl.ds(0, rows)], rg_ref, lsem.at[0])
    rg_copy.start()

    def out_copy(s):
        to_core, to_z = head_source(s)
        return pltpu.make_async_remote_copy(
            src_ref=xs.at[2, :, pl.ds(s * quarter, quarter)],
            dst_ref=agr.at[z],
            send_sem=osend.at[s],
            recv_sem=orecv.at[z],
            device_id={"dp": me - core + to_core, "tensor": to_z},
            device_id_type=MESH_ID,
        )

    def out_wait(source):
        return pltpu.make_async_remote_copy(
            src_ref=xs.at[2, :, pl.ds(0, quarter)],
            dst_ref=agr.at[source],
            send_sem=osend.at[0],
            recv_sem=orecv.at[source],
            device_id={"dp": me, "tensor": z},
            device_id_type=MESH_ID,
        )

    for s in range(ways):
        place = 3 + s // half_wo
        first = (s % half_wo) * quarter
        xs[2, :, s * quarter : (s + 1) * quarter] = dot_nt(
            xs[1], branch[place, first : first + quarter, :]
        ).astype(BF16)
        to_core, to_z = head_source(s)
        to_self = (to_core == core) & (to_z == z)

        @pl.when(jnp.logical_not(to_self))
        def _():
            out_copy(s).start()

        @pl.when(to_self)
        def _():
            agr[z] = xs[2, :, s * quarter : (s + 1) * quarter]

    for s in range(ways):
        place = 6 + s // half_wo
        first = (s % half_wo) * quarter
        xs[place, first : first + quarter] = dot_tn(at[s], xs[1]).astype(BF16)
    og_copy = pltpu.make_async_copy(xs.at[pl.ds(6, 2)], og_ref, lsem.at[2])
    og_copy.start()

    outs["6l"].wait_recv()
    add_to(cs.at[4, low], from_far.at[low])
    outs["4l"].start()
    outs["6h"].wait_recv()
    add_to(cs.at[2, high], from_far.at[high])
    outs["2h"].start()

    for source in range(ways):

        @pl.when(jnp.logical_not(own_at & (z == source)))
        def _():
            out_wait(source).wait_recv()

    ag_copy = pltpu.make_async_copy(agr, ag_ref, lsem.at[3])
    ag_copy.start()
    outs["1"].wait_recv()
    for name in ("2l", "2h", "4l", "4h"):
        outs[name].wait_recv()

    @pl.loop(0, rows // step)
    def _(k):
        rs = pl.ds(pl.multiple_of(k * step, step), step)
        total = resid[rs, :] + cs[0, rs, :].astype(F32) + from_sib[0, rs, :].astype(F32)
        total += from_x[rs, :].astype(F32) + from_y[rs, :].astype(F32)
        xs[0, rs, :] = total.astype(BF16)

    grads_copy.wait()
    lo_copy = pltpu.make_async_copy(xs.at[0], out_ref, lsem.at[1])
    lo_copy.start()
    for name in ("5", "7", "6l", "6h", "2l", "2h", "4l", "4h"):
        sums[name].wait_send()
    for copy in outs.values():
        copy.wait_send()
    for s in range(ways):
        to_core, to_z = head_source(s)

        @pl.when(jnp.logical_not((to_core == core) & (to_z == z)))
        def _():
            out_copy(s).wait_send()

    for copy in (rg_copy, og_copy, ag_copy, lo_copy):
        copy.wait()


def middle(x, attended, resid, out_full, cot_low, cot_high, w_low, w_high, gain):
    rows, d = x.shape
    ways = w_low.shape[0]
    units = ways * 2 * w_low.shape[1] // 3
    quarter = d // ways
    anywhere = pl.BlockSpec(memory_space=pl.ANY)
    inside = pl.BlockSpec(memory_space=pltpu.VMEM)
    sems = lambda n: [pltpu.SemaphoreType.DMA((n,))] * 2
    return pl.pallas_call(
        middle_kernel,
        in_specs=[anywhere] * 8 + [inside],
        out_specs=[anywhere] * 5 + [inside],
        out_shape=[
            jax.ShapeDtypeStruct((ways, rows, quarter), BF16),
            jax.ShapeDtypeStruct((rows, d), F32),
            jax.ShapeDtypeStruct((2, rows, d), BF16),
            jax.ShapeDtypeStruct((rows, d), BF16),
            jax.ShapeDtypeStruct((3 * units // rows, rows, d), BF16),
            jax.ShapeDtypeStruct((8, d), F32),
        ],
        scratch_shapes=[
            pltpu.VMEM((2 * units, d), BF16),
            pltpu.VMEM((units, d), BF16),
            pltpu.VMEM((8, rows, d), BF16),
            pltpu.VMEM((8, rows, d), BF16),
            pltpu.VMEM((6, rows, units), BF16),
            pltpu.VMEM((6, rows, 2 * units), BF16),
            pltpu.VMEM((6, rows, d), BF16),
            pltpu.VMEM((3, rows, d), BF16),
            pltpu.VMEM((rows, d), BF16),
            pltpu.VMEM((rows, d), BF16),
            pltpu.VMEM((rows, d), BF16),
            pltpu.VMEM((units, d), F32),
            pltpu.VMEM((2 * units, d), F32),
            pltpu.VMEM((rows, d), F32),
            pltpu.VMEM((ways, rows, quarter), BF16),
            pltpu.VMEM((ways, rows, quarter), BF16),
        ]
        + sems(8)
        + sems(10)
        + sems(10)
        + sems(ways)
        + [
            pltpu.SemaphoreType.DMA((8, 2)),
            pltpu.SemaphoreType.DMA((ways, 3, 2)),
            pltpu.SemaphoreType.DMA((5,)),
            pltpu.SemaphoreType.REGULAR((3,)),
        ],
        compiler_params=pltpu.CompilerParams(
            collective_id=1, has_side_effects=True, vmem_limit_bytes=VMEM_LIMIT
        ),
        cost_estimate=pl.CostEstimate(
            flops=130 * 10**9, bytes_accessed=40 * rows * d, transcendentals=0
        ),
        name="middle",
    )(x, attended, resid, out_full, cot_low, cot_high, w_low, w_high, gain[None])


def tail_kernel(
    mixed_ref,
    w_ref,
    out_parts_ref,
    rows_ref,
    tok_ref,
    norm_ref,
    n_ref,
    og_ref,
    qkv_ref,
    ng_ref,
    lines,
    line_sib,
    line_z,
    line_end,
    part,
    from_sib,
    from_far,
    from_x,
    from_y,
    mine,
    slices,
    ogs,
    qkv,
    qkv_far,
    qkv_x,
    qkv_y,
    qkv_sum,
    qkv_z,
    qkvs,
    norms,
    norms_z,
    lsend,
    lrecv,
    hsend,
    hrecv,
    ssend,
    srecv,
    gsend,
    grecv,
    osend,
    orecv,
    ksend,
    krecv,
    kzsend,
    kzrecv,
    kgsend,
    kgrecv,
    nsend,
    nrecv,
    zsend,
    zrecv,
    load_sem,
):
    me, z = lax.axis_index("dp"), lax.axis_index("tensor")
    ways, rows = lines.shape[0], lines.shape[1]
    out_rows = slices.shape[1]
    width = w_ref.shape[2]
    total = part.shape[1]
    half = total // 2
    low, high = pl.ds(0, half), pl.ds(half, half)
    core, heads_of, group_of = head_share()
    home = group_of == core
    chip = me // 2
    sib, across, along = plane_peers()
    others = [{"tensor": lax.rem(z + k, ways)} for k in range(1, ways)]
    z1, z2, z3 = (lax.bitwise_xor(z, k) for k in (1, 2, 3))
    near, far = {"tensor": z1}, {"tensor": z2}
    enter([sib, across, along] + others)

    loads = []
    for i in range(8):
        src = pl.multiple_of(lax.bitwise_xor(me, i) * out_rows, 16)
        loads.append(
            [
                pltpu.make_async_copy(
                    out_parts_ref.at[t, pl.ds(src, out_rows)],
                    part.at[i, pl.ds(t * out_rows, out_rows)],
                    load_sem.at[t, i],
                )
                for t in range(ways)
            ]
        )
        for load in loads[-1]:
            load.start()

    def add_to(ref, other):
        ref[...] = (ref[...].astype(F32) + other[...].astype(F32)).astype(BF16)

    size = rows // 2

    def part_of(which):
        return pl.ds(pl.multiple_of(which * size, size), size)

    def line(i):
        b = lax.bitwise_xor(z, i)
        step = min(256, rows)

        @pl.loop(0, rows // step)
        def _(k):
            at = pl.ds(pl.multiple_of(b * rows + k * step, step), step)
            lines[b, pl.ds(pl.multiple_of(k * step, step), step)] = sum(
                dot_nt(mixed_ref[at, j * width : (j + 1) * width], w_ref[j]) for j in range(3)
            ).astype(BF16)

    def share(i):
        b = lax.bitwise_xor(z, i)
        return remote(lines.at[b, part_of(1 - core)], line_sib.at[b], hsend, hrecv, i, sib)

    def share_join(i):
        b = lax.bitwise_xor(z, i)
        share(i).wait_recv()
        add_to(lines.at[b, part_of(core)], line_sib.at[b])

    to_near = [
        remote(lines.at[z3, part_of(core)], line_z.at[0], lsend, lrecv, 0, near),
        remote(lines.at[z1, part_of(core)], line_z.at[1], lsend, lrecv, 1, near),
    ]
    to_far = remote(lines.at[z2, part_of(core)], line_z.at[2], lsend, lrecv, 2, far)
    last_away = remote(line_z.at[2], line_end, lsend, lrecv, 3, sib)
    last_home = remote(lines.at[z, part_of(core)], line_end, lsend, lrecv, 3, sib)

    @pl.loop(0, ways)
    def _(k):
        i = ways - 1 - k
        i = jnp.where(i == 2, 1, jnp.where(i == 1, 2, i))
        line(i)
        for fixed in range(ways):

            @pl.when(i == fixed)
            def _(fixed=fixed):
                share(fixed).start()
                if fixed == 1:
                    share_join(3)
                    to_near[0].start()

    sums = [
        ("1", part.at[1], from_sib.at[0], sib),
        ("3", part.at[3], from_sib.at[1], sib),
        ("5", part.at[5], from_sib.at[2], sib),
        ("7", part.at[7], from_sib.at[3], sib),
        ("6l", part.at[6, low], from_far.at[low], across),
        ("6h", part.at[6, high], from_far.at[high], along),
        ("2l", part.at[2, low], from_x.at[low], across),
        ("2h", part.at[2, high], from_x.at[high], across),
        ("4l", part.at[4, low], from_y.at[low], along),
        ("4h", part.at[4, high], from_y.at[high], along),
    ]
    sums = {
        name: remote(src, dst, ssend, srecv, i, peer)
        for i, (name, src, dst, peer) in enumerate(sums)
    }
    for i in (7, 3, 5, 1):
        for load in loads[i]:
            load.wait()
        sums[str(i)].start()

    @pl.loop(0, 3)
    def _(j):
        at = pl.ds(pl.multiple_of(j * width, width), width)
        qkv[at, :] = dot_tn(mixed_ref[:, at], rows_ref[...]).astype(BF16)

    piece = qkv_sum.shape[0]
    small = piece // 2

    def qkv_at(s, side=None):
        first = lax.bitwise_xor(chip, s) * piece + (0 if side is None else side * small)
        return qkv.at[pl.ds(pl.multiple_of(first, 16), piece if side is None else small)]

    def side_of(ref, side):
        return ref.at[pl.ds(side * small, small)]

    pieces = [
        ("3l", qkv_at(3, 0), side_of(qkv_far, 0), across),
        ("3h", qkv_at(3, 1), side_of(qkv_far, 1), along),
        ("1l", qkv_at(1, 0), side_of(qkv_x, 0), across),
        ("1h", qkv_at(1, 1), side_of(qkv_x, 1), across),
        ("2l", qkv_at(2, 0), side_of(qkv_y, 0), along),
        ("2h", qkv_at(2, 1), side_of(qkv_y, 1), along),
    ]
    pieces = {
        name: remote(src, dst, ksend, krecv, i, peer)
        for i, (name, src, dst, peer) in enumerate(pieces)
    }
    for name in ("3l", "3h", "1l", "2h"):
        pieces[name].start()

    share_join(1)
    for i, j, names in ((6, 3, ("6l", "6h")), (2, 1, ("2l",)), (4, 2, ("4h",))):
        for load in loads[i]:
            load.wait()
        sums[str(i + 1)].wait_recv()
        add_to(part.at[i], from_sib.at[j])
        for name in names:
            sums[name].start()
    share_join(2)
    to_near[0].wait_recv()
    to_near[1].start()
    add_to(lines.at[z2, part_of(core)], line_z.at[0])
    to_far.start()
    share_join(0)

    pieces["3l"].wait_recv()
    add_to(qkv_at(2, 0), side_of(qkv_far, 0))
    pieces["2l"].start()
    pieces["3h"].wait_recv()
    add_to(qkv_at(1, 1), side_of(qkv_far, 1))
    pieces["1h"].start()
    sums["6l"].wait_recv()
    add_to(part.at[4, low], from_far.at[low])
    sums["4l"].start()
    sums["6h"].wait_recv()
    add_to(part.at[2, high], from_far.at[high])
    sums["2h"].start()

    for name in ("1l", "1h", "2l", "2h"):
        pieces[name].wait_recv()
    qkv_sum[...] = (
        qkv_at(0)[...].astype(F32) + qkv_x[...].astype(F32) + qkv_y[...].astype(F32)
    ).astype(BF16)
    takes = core == lax.rem(z, 2)

    def owner_copy(slot):
        return pltpu.make_async_remote_copy(
            src_ref=qkv_sum,
            dst_ref=qkv_z.at[slot],
            send_sem=kzsend.at[0],
            recv_sem=kzrecv.at[slot],
            device_id={"tensor": heads_of},
            device_id_type=MESH_ID,
        )

    @pl.when(heads_of != z)
    def _():
        owner_copy(group_of).start()

    @pl.when(heads_of == z)
    def _():
        qkv_z[group_of] = qkv_sum[...]

    for load in loads[0]:
        load.wait()
    sums["1"].wait_recv()
    for name in ("2l", "2h", "4l", "4h"):
        sums[name].wait_recv()
    mine[...] = part[0].astype(F32) + from_sib[0].astype(F32)
    mine[...] += from_x[...].astype(F32) + from_y[...].astype(F32)

    for t in range(ways):
        at = slice(t * out_rows, (t + 1) * out_rows)
        part[0, at] = mine[at].astype(BF16)

    def slice_copy(k, to, source):
        return pltpu.make_async_remote_copy(
            src_ref=part.at[0, pl.ds(pl.multiple_of(to * out_rows, 16), out_rows)],
            dst_ref=slices.at[source],
            send_sem=osend.at[k],
            recv_sem=orecv.at[source],
            device_id={"tensor": to},
            device_id_type=MESH_ID,
        )

    for k in range(1, ways):
        slice_copy(k, lax.rem(z + k, ways), z).start()

    def chip_copy(s, side, peer, sem):
        at = qkvs.at[lax.bitwise_xor(chip, s)]
        ref = at if side is None else side_of(at, side)
        return remote(ref, ref, kgsend, kgrecv, sem, peer)

    to_x, to_y = chip_copy(0, None, across, 0), chip_copy(0, None, along, 1)
    x_on, y_on = chip_copy(1, 1, along, 2), chip_copy(2, 0, across, 3)
    to_sib = [chip_copy(s, None, sib, 4 + s) for s in range(4)]

    @pl.when(takes)
    def _():
        for slot in range(2):

            @pl.when(z // 2 + 2 * slot != z)
            def _():
                owner_copy(slot).wait_recv()

        qkvs[chip] = (qkv_z[0].astype(F32) + qkv_z[1].astype(F32)).astype(BF16)
        to_x.start()
        to_y.start()
        to_sib[0].start()

    own_slice = part[0, pl.ds(pl.multiple_of(z * out_rows, 16), out_rows)].astype(F32)
    for k in range(1, ways):
        source = lax.rem(z + k, ways)
        slice_copy(k, source, source).wait_recv()
        own_slice += slices[source].astype(F32)
    ogs[me] = own_slice.astype(BF16)
    view = lambda s, side: half_of(ogs.at[lax.bitwise_xor(me, s)], side)
    gathers = gather_copies(view, gsend, grecv, True)
    gather_start(gathers)

    to_near[1].wait_recv()
    add_to(lines.at[z, part_of(core)], line_z.at[1])

    @pl.when(jnp.logical_not(home))
    def _():
        last_home.start()

    to_far.wait_recv()

    @pl.when(home)
    def _():
        last_away.start()
        n_ref[part_of(core), :] = lines[z, part_of(core), :].astype(F32)

    @pl.when(jnp.logical_not(home))
    def _():
        n_ref[part_of(core), :] = line_z[2].astype(F32)

    last_away.wait_recv()
    n_ref[part_of(1 - core), :] = line_end[...].astype(F32)

    norms[0] = norm_ref[...]
    step = min(128, rows)

    @pl.loop(0, rows // step)
    def _(i):
        at = pl.ds(pl.multiple_of(i * step, step), step)
        values = tok_ref[at, :].astype(F32)
        centred = values - jnp.mean(values, axis=-1, keepdims=True)
        root = lax.rsqrt(jnp.mean(centred * centred, axis=-1, keepdims=True) + norm_eps)
        grad = n_ref[at, :]
        norms[0, 0:1] += jnp.sum(grad * (centred * root), axis=0, keepdims=True)
        norms[0, 1:2] += jnp.sum(grad, axis=0, keepdims=True)

    swaps = [
        remote(norms.at[i], norms.at[4 + i], nsend, nrecv, i, peer)
        for i, peer in enumerate((sib, across, along))
    ]
    swaps[0].start()

    gather_forward(gathers)

    @pl.when(takes)
    def _():
        to_x.wait_recv()
        x_on.start()
        to_sib[1].start()
        to_y.wait_recv()
        y_on.start()
        to_sib[2].start()

    for i, swap in enumerate(swaps):
        if i:
            swap.start()
        swap.wait_recv()
        norms[i + 1] = norms[i] + norms[4 + i]

    def norm_copy(k, to, source):
        return pltpu.make_async_remote_copy(
            src_ref=norms.at[3],
            dst_ref=norms_z.at[source],
            send_sem=zsend.at[k],
            recv_sem=zrecv.at[source],
            device_id={"tensor": to},
            device_id_type=MESH_ID,
        )

    for k in range(1, ways):
        norm_copy(k, lax.rem(z + k, ways), z).start()
    norms_z[z] = norms[3]
    gather_finish(gathers)
    og_ref[...] = ogs[...]

    @pl.when(takes)
    def _():
        x_on.wait_recv()
        y_on.wait_recv()
        to_sib[3].start()

    @pl.when(jnp.logical_not(takes))
    def _():
        for copy in to_sib:
            copy.wait_recv()

    qkv_ref[...] = qkvs[...]
    for k in range(1, ways):
        source = lax.rem(z + k, ways)
        norm_copy(k, source, source).wait_recv()
    ng_ref[...] = sum(norms_z[t] for t in range(ways))

    @pl.when(takes)
    def _():
        for copy in (to_x, to_y, x_on, y_on, *to_sib):
            copy.wait_send()

    @pl.when(heads_of != z)
    def _():
        owner_copy(group_of).wait_send()

    @pl.when(home)
    def _():
        last_away.wait_send()

    @pl.when(jnp.logical_not(home))
    def _():
        last_home.wait_send()

    for copy in (*sums.values(), *gathers.values(), *pieces.values(), *swaps, *to_near, to_far):
        copy.wait_send()
    for i in range(ways):
        share(i).wait_send()
    for k in range(1, ways):
        to = lax.rem(z + k, ways)
        slice_copy(k, to, z).wait_send()
        norm_copy(k, to, z).wait_send()


def tail(mixed, w, out_parts, rows_one, tokens, norm_grads, ways):
    rows, d = tokens.shape
    out_rows = out_parts.shape[1] // 8
    qkv_rows = mixed.shape[1] // 4
    total = ways * out_rows
    anywhere = pl.BlockSpec(memory_space=pl.ANY)
    inside = pl.BlockSpec(memory_space=pltpu.VMEM)
    sems = lambda n: [pltpu.SemaphoreType.DMA((n,))] * 2
    return pl.pallas_call(
        tail_kernel,
        in_specs=[inside, inside, anywhere, inside, inside, inside],
        out_specs=[inside] * 4,
        out_shape=[
            jax.ShapeDtypeStruct((rows, d), F32),
            jax.ShapeDtypeStruct((8, out_rows, d), BF16),
            jax.ShapeDtypeStruct((4, qkv_rows, d), BF16),
            jax.ShapeDtypeStruct((8, d), F32),
        ],
        scratch_shapes=[
            pltpu.VMEM((ways, rows, d), BF16),
            pltpu.VMEM((ways, rows // 2, d), BF16),
            pltpu.VMEM((3, rows // 2, d), BF16),
            pltpu.VMEM((rows // 2, d), BF16),
            pltpu.VMEM((8, total, d), BF16),
            pltpu.VMEM((4, total, d), BF16),
            pltpu.VMEM((total, d), BF16),
            pltpu.VMEM((total, d), BF16),
            pltpu.VMEM((total, d), BF16),
            pltpu.VMEM((total, d), F32),
            pltpu.VMEM((ways, out_rows, d), BF16),
            pltpu.VMEM((8, out_rows, d), BF16),
            pltpu.VMEM((4 * qkv_rows, d), BF16),
            pltpu.VMEM((qkv_rows, d), BF16),
            pltpu.VMEM((qkv_rows, d), BF16),
            pltpu.VMEM((qkv_rows, d), BF16),
            pltpu.VMEM((qkv_rows, d), BF16),
            pltpu.VMEM((2, qkv_rows, d), BF16),
            pltpu.VMEM((4, qkv_rows, d), BF16),
            pltpu.VMEM((8, 8, d), F32),
            pltpu.VMEM((ways, 8, d), F32),
        ]
        + sems(4)
        + sems(ways)
        + sems(10)
        + sems(8)
        + sems(ways)
        + sems(6)
        + sems(2)
        + sems(8)
        + sems(3)
        + sems(ways)
        + [pltpu.SemaphoreType.DMA((ways, 8))],
        compiler_params=pltpu.CompilerParams(
            collective_id=2, has_side_effects=True, vmem_limit_bytes=VMEM_LIMIT
        ),
        cost_estimate=pl.CostEstimate(
            flops=75 * 10**9, bytes_accessed=40 * rows * d, transcendentals=0
        ),
        name="tail",
    )(mixed, w, out_parts, rows_one, tokens, norm_grads)


def finish_kernel(
    both_ref,
    down_ref,
    features_ref,
    og_ref,
    grad_ref,
    resid_ref,
    tok_ref,
    gain_ref,
    gate_up_ref,
    down_out_ref,
    qkv_ref,
    og_out_ref,
    token_ref,
):
    units = both_ref.shape[1] // 2
    for p in range(8):
        turned = both_ref[p].astype(F32).T
        for g in range(2):
            at = pl.ds(2 * p + g, turned.shape[0], stride=16)
            gate_up_ref[at, :] = turned[:, g * units : (g + 1) * units]
    down_out_ref[...] = down_ref[0].astype(F32)
    width = qkv_ref.shape[2]
    for j in range(3):
        qkv_ref[j] = features_ref[j * width : (j + 1) * width].astype(F32).T
    og_out_ref[...] = og_ref[0].astype(F32)
    values = tok_ref[...].astype(F32)
    centred = values - jnp.mean(values, axis=-1, keepdims=True)
    root = lax.rsqrt(jnp.mean(centred * centred, axis=-1, keepdims=True) + norm_eps)
    unit_rows = centred * root
    scaled = grad_ref[...] * gain_ref[...]
    first_mean = jnp.mean(scaled, axis=-1, keepdims=True)
    second_mean = jnp.mean(scaled * unit_rows, axis=-1, keepdims=True)
    token_ref[...] = resid_ref[...] + root * (scaled - first_mean - unit_rows * second_mean)


def finish(grads, features, out_grad, norm_grad, resid_grad, tokens, gain):
    rows, d = tokens.shape
    units = grads.shape[1] // 3
    block = d // 8
    width = features.shape[0] // 3
    out_rows = out_grad.shape[1]
    own = pl.BlockSpec((rows // 8, d), lambda i: (i, 0))
    return pl.pallas_call(
        finish_kernel,
        grid=(8,),
        in_specs=[
            pl.BlockSpec((8, 2 * units, block), lambda i: (0, 0, i)),
            pl.BlockSpec((1, units, d), lambda i: (i, 2, 0)),
            pl.BlockSpec((3 * width, block), lambda i: (0, i)),
            pl.BlockSpec((1, out_rows, d), lambda i: (i, 0, 0)),
            own,
            own,
            own,
            pl.BlockSpec((1, d), lambda i: (0, 0)),
        ],
        out_specs=[
            pl.BlockSpec((16 * block, units), lambda i: (i, 0)),
            pl.BlockSpec((units, d), lambda i: (i, 0)),
            pl.BlockSpec((3, block, width), lambda i: (0, i, 0)),
            pl.BlockSpec((out_rows, d), lambda i: (i, 0)),
            own,
        ],
        out_shape=[
            jax.ShapeDtypeStruct((16 * d, units), F32),
            jax.ShapeDtypeStruct((8 * units, d), F32),
            jax.ShapeDtypeStruct((3, d, width), F32),
            jax.ShapeDtypeStruct((8 * out_rows, d), F32),
            jax.ShapeDtypeStruct((rows, d), F32),
        ],
        compiler_params=pltpu.CompilerParams(vmem_limit_bytes=VMEM_LIMIT),
        name="finish",
    )(grads, grads, features, out_grad, norm_grad, resid_grad, tokens, gain[None])


def shards(
    tokens,
    group_bucket,
    gain_one,
    shift_one,
    w_qkv,
    w_out,
    gain_two,
    shift_two,
    w_gate_up,
    w_down,
    cotangent,
):
    ways = lax.axis_size("tensor")
    replicas = lax.axis_size("dp")
    replica = lax.axis_index("dp")
    own_rows, d = tokens.shape
    group_rows = own_rows * ways
    local_width = w_out.shape[0]
    head_dim = d // HEADS
    hidden_width = w_down.shape[0]
    units = hidden_width // replicas
    out_rows = local_width // replicas
    pair_width = min(128, local_width)

    rows_in = tokens.astype(F32)
    normed_one, unit_one, root_one = norm_forward(rows_in, gain_one, shift_one)
    normed_one_low = normed_one.astype(BF16)
    rows_one = lax.all_gather(normed_one_low, "tensor", axis=0, tiled=True)

    gate_up_slice = lax.dynamic_slice_in_dim(w_gate_up, replica * units, units, axis=2)
    down_slice = lax.dynamic_slice_in_dim(w_down, replica * units, units, axis=0)
    weight_slice = jnp.concatenate(
        [gate_up_slice.transpose(1, 2, 0).reshape(2 * units, d), down_slice]
    )
    weights = lax.all_gather(weight_slice, "tensor", axis=0)
    cot_all = lax.all_gather(cotangent, "dp", axis=0, tiled=True)
    out_full = lax.all_gather(w_out, "tensor", axis=0, tiled=True)

    cos_wide, sine_wide = rotary_wide(group_bucket[0], group_rows, head_dim, pair_width)
    qkv_weights = w_qkv.transpose(1, 0, 2)
    q, k, v, kt, vt = project(rows_one, qkv_weights, cos_wide, sine_wide, head_dim)
    attended, *kept = attend(group_bucket, q, k, vt, head_dim)
    attended_own = lax.all_to_all(attended, "tensor", 0, 1, tiled=True)
    resid = rows_in + dot_nn(attended_own, out_full)
    normed_two, unit_two, root_two = norm_forward(resid, gain_two, shift_two)
    normed_two_low = normed_two.astype(BF16)
    parts = weights.reshape(ways, 3, units, d)
    wgu = parts[:, :2].transpose(3, 1, 0, 2).reshape(d, 2 * ways * units)
    wd = parts[:, 2].reshape(ways * units, d)
    rows_two = lax.all_gather(normed_two_low, "dp", axis=0, tiled=True)
    hidden, branch, back = feed(rows_two, cot_all, wgu, wd)
    normed_two_grad = lax.psum_scatter(back, "dp", scatter_dimension=0, tiled=True).astype(F32)
    ffn_parts = dot_nn(hidden, wd).astype(BF16)
    ffn_out = lax.psum_scatter(ffn_parts, "dp", scatter_dimension=0, tiled=True).astype(F32)
    layer_out = (resid + ffn_out).astype(BF16)
    grads = jnp.concatenate(
        [
            dot_tn(branch, rows_two).reshape(2, ways, units, d),
            dot_tn(hidden, cot_all).reshape(1, ways, units, d),
        ]
    )
    grads = grads.astype(BF16).transpose(1, 0, 2, 3).reshape(ways, 3 * units, d)
    resid_part, gain_two_grad, shift_two_grad = norm_backward(
        normed_two_grad, unit_two, root_two, gain_two
    )
    norm_grads = jnp.zeros((8, d), F32).at[2].set(gain_two_grad).at[3].set(shift_two_grad)
    resid_grad = cotangent.astype(F32) + resid_part
    attn_grad = resid_grad.astype(BF16)
    attended_grad = lax.all_to_all(
        dot_nt(attn_grad, out_full).astype(BF16), "tensor", 1, 0, tiled=True
    )
    out_grad = dot_tn(attended_own, attn_grad).astype(BF16)
    out_grad = out_grad.reshape(ways, replicas, out_rows, d).transpose(1, 0, 2, 3)
    out_grad = out_grad.reshape(replicas, ways * out_rows, d)
    grads = lax.psum_scatter(grads, "tensor", scatter_dimension=0)

    mixed_grad = attend_back(
        group_bucket, q, k, kt, v, attended_grad, *kept, cos_wide, sine_wide, head_dim
    )
    grads, mixed_grad = lax.optimization_barrier((grads, mixed_grad))
    grads = lax.all_gather(grads, "dp", axis=0)
    grads = grads.reshape(replicas, 3, units, d)
    down_grad = grads[:, 2].reshape(hidden_width, d).astype(F32)
    gate_up_grad = grads[:, :2].transpose(3, 1, 0, 2).reshape(d, 2, hidden_width).astype(F32)
    qkv_grad = lax.psum(dot_tn(rows_one, mixed_grad).astype(BF16), "dp").astype(F32)
    qkv_grad = qkv_grad.reshape(d, 3, local_width)
    flat = qkv_weights.transpose(1, 0, 2).reshape(d, 3 * local_width)
    normed_one_grad = lax.psum_scatter(
        dot_nt(mixed_grad, flat).astype(BF16), "tensor", scatter_dimension=0, tiled=True
    ).astype(F32)
    out_grad = lax.psum_scatter(out_grad, "dp", scatter_dimension=0)
    out_grad = lax.psum_scatter(out_grad, "tensor", scatter_dimension=0, tiled=True)
    out_grad = lax.all_gather(out_grad, "dp", axis=0, tiled=True).astype(F32)
    one = norm_backward(normed_one_grad, unit_one, root_one, gain_one)
    norm_grads = norm_grads.at[0].set(one[1]).at[1].set(one[2])
    norm_grads = lax.psum(norm_grads, ("dp", "tensor"))
    token_grad = resid_grad + norm_backward(normed_one_grad, unit_one, root_one, gain_one)[0]
    gain_one_grad, shift_one_grad, gain_two_grad, shift_two_grad = (norm_grads[i] for i in range(4))
    return (
        layer_out,
        token_grad,
        gain_one_grad,
        shift_one_grad,
        qkv_grad,
        out_grad,
        gain_two_grad,
        shift_two_grad,
        gate_up_grad,
        down_grad,
    )


def shards_columns(
    tokens,
    group_bucket,
    gain_one,
    shift_one,
    w_qkv,
    w_out,
    gain_two,
    shift_two,
    w_gate_up,
    w_down,
    cotangent,
):
    ways = lax.axis_size("tensor")
    replica = lax.axis_index("dp")
    own_rows, d = tokens.shape
    group_rows = own_rows * ways
    local_width = w_out.shape[0]
    head_dim = d // HEADS
    hidden_width = w_down.shape[0]
    units = hidden_width // 8

    gate_up_slice = lax.dynamic_slice_in_dim(w_gate_up, replica * units, units, axis=2)
    down_slice = lax.dynamic_slice_in_dim(w_down, replica * units, units, axis=0)
    weight_slice = jnp.concatenate(
        [gate_up_slice.transpose(1, 2, 0).reshape(2 * units, d), down_slice]
    )
    split = 3 * units // 2
    weights_low = lax.all_gather(weight_slice[:split], "tensor", axis=0)
    q, k, v, kt, vt, cos_wide, sine_wide, bucket, rows_one, cot_low, out_full, qkv_weights = front(
        group_bucket,
        tokens,
        gain_one,
        shift_one,
        cotangent,
        w_out,
        w_qkv.transpose(1, 0, 2),
        head_dim,
        ways,
    )
    bucket, weight_slice = lax.optimization_barrier((bucket, weight_slice))
    weights_high = lax.all_gather(weight_slice[split:], "tensor", axis=0)
    bucket = bucket[0, :1]
    out_full = out_full.reshape(d, d)
    attended, *kept = attend(bucket, q, k, vt, head_dim)
    attended_own, resid, normed_two, cot_high = collect(
        attended, tokens, out_full, gain_two, shift_two, cotangent, ways
    )
    attended_grad, resid_grad, out_grad, layer_out, grads, norm_grads = middle(
        normed_two,
        attended_own,
        resid,
        out_full,
        cot_low,
        cot_high,
        weights_low,
        weights_high,
        gain_two,
    )
    grads = grads.reshape(ways, 3 * units, d)
    grads = lax.psum_scatter(grads, "tensor", scatter_dimension=0)
    attended_grad = attended_grad.reshape(group_rows, local_width)
    mixed_grad = attend_back(
        bucket, q, k, kt, v, attended_grad, *kept, cos_wide, sine_wide, head_dim
    )
    grads, mixed_grad = lax.optimization_barrier((grads, mixed_grad))
    grads = lax.all_gather(grads, "dp", axis=0)
    normed_one_grad, out_grad, qkv_grad, norm_grads = tail(
        mixed_grad,
        qkv_weights,
        out_grad.reshape(ways, local_width, d),
        rows_one.reshape(group_rows, d),
        tokens,
        norm_grads,
        ways,
    )
    gate_up_grad, down_grad, qkv_grad, out_grad, token_grad = finish(
        grads,
        qkv_grad.reshape(3 * local_width, d),
        out_grad,
        normed_one_grad,
        resid_grad,
        tokens,
        gain_one,
    )
    gate_up_grad = gate_up_grad.reshape(d, 8, 2, units).transpose(0, 2, 1, 3)
    gate_up_grad = gate_up_grad.reshape(d, 2, hidden_width)
    qkv_grad = qkv_grad.transpose(1, 0, 2)
    gain_one_grad, shift_one_grad, gain_two_grad, shift_two_grad = (norm_grads[i] for i in range(4))
    return (
        layer_out,
        token_grad,
        gain_one_grad,
        shift_one_grad,
        qkv_grad,
        out_grad,
        gain_two_grad,
        shift_two_grad,
        gate_up_grad,
        down_grad,
    )


def solution(mesh):
    in_specs = (
        P(("dp", "tensor"), None),
        P("dp"),
        P(),
        P(),
        P(None, None, "tensor"),
        P("tensor", None),
        P(),
        P(),
        P(None, None, "tensor"),
        P("tensor", None),
        P(("dp", "tensor"), None),
    )
    out_specs = (
        P(("dp", "tensor"), None),
        P(("dp", "tensor"), None),
        P(),
        P(),
        P(None, None, "tensor"),
        P("tensor", None),
        P(),
        P(),
        P(None, None, "tensor"),
        P("tensor", None),
    )
    columns = mesh.shape["dp"] == 8 and mesh.shape["tensor"] == 4
    body = shards_columns if columns else shards
    return jax.shard_map(body, mesh=mesh, in_specs=in_specs, out_specs=out_specs, check_vma=False)
```

time: 532 us -> 466 us (0.88)
  Pallas kernels: 352 us -> 423 us
  waiting for transfers between devices: 56.9 us -> 15.7 us
  local copies, waits for them, and re-layouts: 43.5 us -> 8.63 us
  blocking collectives: 22.7 us -> 0 us
  other arithmetic: 22.6 us -> 0.06 us
  starting transfers between devices: 11.9 us -> 0.34 us
    pallas_call x6 -> x5, Pallas kernels: 270 us -> 354 us  [the longest x1 125 us: middle(): pl.pallas_call(middle_kernel, in_specs=[anywhere] * 8 + [inside], out_spe...]
    all_to_all x3 -> x0, waiting for transfers between devices: 37.6 us -> none  [the longest x2 25.6 us: shards(): lax.all_to_all(attended_grad_own[:, :, p].reshape(own_rows, ways * pair_w...]
    unnamed x110 -> x3, local copies, waits for them, and re-layouts: 29.7 us -> 0.98 us
    all_to_all x1 -> x0, blocking collectives: 22.7 us -> none  [shards(): lax.all_to_all(a[0], 'tensor', 0, 1, tiled=True)]
    all_gather x3, waiting for transfers between devices: 18.3 us -> 0.04 us  [the longest x1 0.02 us: shards_columns(): weights_low = lax.all_gather(weight_slice[:split], 'tensor', axis=0)]
    reduce_scatter x1, waiting for transfers between devices: 0.87 us -> 15.6 us  [shards_columns(): grads = lax.psum_scatter(grads, 'tensor', scatter_dimension=0)]
    all_to_all x3 -> x0, starting transfers between devices: 11.8 us -> none  [the longest x2 7.63 us: shards(): lax.all_to_all(attended_grad_own[:, :, p].reshape(own_rows, ways * pair_w...]
    pallas_call x2 -> x1, Pallas kernels: 51.8 us -> 42.7 us  [attend_back(): pl.pallas_call(functools.partial(attend_back_kernel, head_dim), grid_spec...]
  transfers between devices with their start and end apart: 7 -> 4, of which waited for: 5 -> 1; matrix products, arithmetic and copies ran while one was open for 7% -> 1% of each run, Pallas kernels for 49% -> 61%
where the time goes in v3:
time: 466 us; the launch traced here: 462 us
  Pallas kernels  423 us (91%)
  waiting for transfers between devices  15.7 us (3%)
  between operations  14.7 us (3%)
  local copies, waits for them, and re-layouts  8.63 us (2%)
    pallas_call x1, Pallas kernels, middle(): pl.pallas_call(middle_kernel, in_specs=[anywhere] * 8 + [inside], out_spe...  125 us
    pallas_call x1, Pallas kernels, front(): pl.pallas_call(functools.partial(front_kernel, head_dim), in_specs=[pl.Bl...  92.5 us
    pallas_call x1, Pallas kernels, tail(): pl.pallas_call(tail_kernel, in_specs=[inside, inside, anywhere, inside, i...  83.5 us
    pallas_call x1, Pallas kernels, attend_back(): pl.pallas_call(functools.partial(attend_back_kernel, head_dim), grid_spec...  42.7 us
    pallas_call x1, Pallas kernels, collect(): pl.pallas_call(collect_kernel, in_specs=[anywhere] + [inside] * 4 + [anyw...  38.5 us
    pallas_call x1, Pallas kernels, attend(): pl.pallas_call(functools.partial(attend_kernel, head_dim), grid_spec=pltp...  25.9 us
    reduce_scatter x1, waiting for transfers between devices, shards_columns(): grads = lax.psum_scatter(grads, 'tensor', scatter_dimension=0)  15.6 us
    pallas_call x1, Pallas kernels, finish(): pl.pallas_call(finish_kernel, grid=(8,), in_specs=[pl.BlockSpec((8, 2 * u...  14.7 us
  transfers between devices with their start and end apart: 4, of which 1 were waited for; matrix products, arithmetic and copies ran while one was open for 1% of the time, Pallas kernels for 61%

profile of v3, /device:TPU:0, one launch (start us, length us, event | category | flops | bytes accessed | tf_op | source)
XLA Modules:
  0.0 462.0 jit_solution(8274966697856352916)
XLA Ops:
  7.2 0.0 all-gather.7.cloned.1.call-start
  7.2 1.4 dynamic-slice_bitcast_fusion
  8.6 0.4 copy.24
  9.1 0.8 slice.28
  9.9 0.0 all-gather.9.cloned.1.call-start
  10.6 0.6 broadcast_in_dim_tile.3.freq_ref
  11.2 92.5 %front.1 = (bf16[2048,256]{1,0:T(8,128)(2,1)}, bf16[2048,256]{1,0:T(8,128)(2,1)}, bf16[2048,256]{1,0:T(8,128)(2,1)}, bf16[256,2048]{1,0:T(8,128)(2,1)}, bf16[256...) custom-call(s32[1]{0:T(128)S(6)} %copy.26.bucket_ref, ...), custom_call_target="tpu_custom_call" | custom-call | flops 54999998464 | bytes 16777216 | tf_op jit(solution)/shard_map/front/pallas_call | solution.py:774
  103.7 1.0 constant_dynamic-slice_fusion
  104.6 0.1 pad_maximum_fusion
  104.7 0.8 slice.23
  105.5 0.2 reduce-scatter.2.cloned.1.call-start
  105.7 1.2 slice.21
  106.9 25.9 %attend.1 = (bf16[2048,256]{1,0:T(8,128)(2,1)}, f32[256,2048]{1,0:T(8,128)}, f32[8,2048]{1,0:T(8,128)}) custom-call(s32[1]{0:T(128)} %bitcast.5.bucket_ref, bf16[2048,256]{1,0:T(8,128)(2,1)} %get-tuple-element.50.q_ref, bf16[2048,256]{1,0:T(8,128)(2,1)} %get-tuple-element.51.k_ref, bf16[256,2048]{1,0:T(8,128)(2,1)} %get-tuple-element.52.vt_ref), custom_call_target="tpu_custom_call" | custom-call | flops 17179869184 | bytes 5242880 | tf_op jit(solution)/shard_map/attend/pallas_call | solution.py:183
  132.9 38.5 %collect.1 = (bf16[4,512,256]{2,1,0:T(8,128)(2,1)}, f32[512,1024]{1,0:T(8,128)}, bf16[512,1024]{1,0:T(8,128)(2,1)}, bf16[8,256,1024]{2,1,0:T(8,128)(2,1)}) custom-call(bf16[2048,256]{1,0:T(8,128)(2,1)} %get-tuple-element.53.att_ref, bf16[512,1024]{1,0:T(8,128)(2,1)} %tok_ref.7, bf16[1024,1024]{1,0:T(8,128)(2,1)} %bitcast.52, f32[1,1024]{1,0:T(1,128)} %bitcast.49, ...), custom_call_target="tpu_custom_call" | custom-call | flops 30000001024 | bytes 8388608 | tf_op jit(solution)/shard_map/collect/pallas_call | solution.py:938
  171.4 0.0 all-gather.7.cloned.1.call-done
  171.4 0.0 all-gather.9.cloned.1.call-done
  171.4 124.8 %middle.1 = (bf16[4,512,256]{2,1,0:T(8,128)(2,1)}, f32[512,1024]{1,0:T(8,128)}, bf16[2,512,1024]{2,1,0:T(8,128)(2,1)}, bf16[512,1024]{1,0:T(8,128)(2,1)}, bf16[3...) custom-call(bf16[512,1024]{1,0:T(8,128)(2,1)} %get-tuple-element.55.x_ref, bf16[4,512,256]{2,1,0:T(8,128)(2,1)} %get-tuple-element.56.at_ref, ...), custom_call_target="tpu_custom_call" | custom-call | flops 130000003072 | bytes 20971520 | tf_op jit(solution)/shard_map/middle/pallas_call | solution.py:1367
  296.2 0.0 all-gather.11.cloned.1.call-start
  296.3 42.7 %attend_back.1.mixed_ref = bf16[2048,768]{1,0:T(8,128)(2,1)} custom-call(s32[1]{0:T(128)} %bitcast.5.bucket_ref, bf16[2048,256]{1,0:T(8,128)(2,1)} %get-tuple-element.50.q_ref, bf16[2048,256]{1,0:T(8,128)(2,1)} %get-tuple-element.51.k_ref, bf16[256,2048]{1,0:T(8,128)(2,1)} %get-tuple-element.63.kt_ref, bf16[2048,256]{1,0:T(8,128)(2,1)} %get-tuple-element.64.v_ref, ...), custom_call_target="tpu_custom_call" | custom-call | flops 42949672960 | bytes 12582912 | tf_op jit(solution)/shard_map/attend_back/pallas_call | solution.py:295
  339.0 15.6 %reduce-scatter.2.cloned.1.call-done = bf16[1,384,1024]{2,1,0:T(8,128)(2,1)} async-done(((bf16[4,384,1024]{2,1,0:T(8,128)(2,1)}), bf16[1,384,1024]{2,1,0:T(8,128)(2,1)}) %reduce-scatter.2.cloned.1.call-update) | async-done | bytes 786448 | tf_op jit(solution)/shard_map/reduce_scatter | solution.py:2141
  354.5 83.5 %tail.1 = (f32[512,1024]{1,0:T(8,128)}, bf16[8,32,1024]{2,1,0:T(8,128)(2,1)}, bf16[4,192,1024]{2,1,0:T(8,128)(2,1)}, f32[8,1024]{1,0:T(8,128)}) custom-call(bf16[2048,768]{1,0:T(8,128)(2,1)} %attend_back.1.mixed_ref, bf16[3,1024,256]{2,1,0:T(8,128)(2,1)} %get-tuple-element.72.w_ref, bf16[4,256,1024]{2,1,0:T(8,128)(2,1)} %bitcast.54, ...), custom_call_target="tpu_custom_call" | custom-call | flops 74999996416 | bytes 20971520 | tf_op jit(solution)/shard_map/tail/pallas_call | solution.py:1839
  438.1 1.5 fusion
  439.6 14.7 %finish.1 = (f32[16384,128]{1,0:T(8,128)}, f32[1024,1024]{1,0:T(8,128)}, f32[3,1024,256]{2,1,0:T(8,128)}, f32[256,1024]{1,0:T(8,128)}, f32[512,1024]{1,0:T(8,128)}) custom-call(bf16[8,384,1024]{2,1,0:T(8,128)(2,1)} %bitcast.29, bf16[8,384,1024]{2,1,0:T(8,128)(2,1)} %bitcast.30, bf16[768,1024]{1,0:T(8,128)(2,1)} %bitcast.34, ...), custom_call_target="tpu_custom_call" | custom-call | tf_op jit(solution)/shard_map/finish/pallas_call | solution.py:1936
  454.3 1.0 copy.27
  (9 shorter events, 0.1 us)
Async XLA Ops:
  7.2 164.2 %all-gather.7.cloned.1.call-start = ((), (), s32[]{:S(2)}) async-start(), calls=%async_computation.2 | async-start | bytes 1966080 | tf_op jit(solution)/shard_map/all_gather | solution.py:2109
  9.9 161.5 %all-gather.9.cloned.1.call-start = ((), (), s32[]{:S(2)}) async-start(), calls=%async_computation.3 | async-start | bytes 1966080 | tf_op jit(solution)/shard_map/all_gather | solution.py:2122
  105.5 249.0 %reduce-scatter.2.cloned.1.call-start = ((), (), s32[]{:S(2)}) async-start(), calls=%async_computation.1 | async-start | bytes 3932160 | tf_op jit(solution)/shard_map/reduce_scatter | solution.py:2141
  296.2 143.4 %all-gather.11.cloned.1.call-start = ((), (), s32[]{:S(2)}) async-start(), calls=%async_computation.4 | async-start | bytes 7077888 | tf_op jit(solution)/shard_map/all_gather | solution.py:2147
  439.6 14.7 %copy-start = (bf16[512,1024]{1,0:T(8,128)(2,1)S(1)}, bf16[512,1024]{1,0:T(8,128)(2,1)}, u32[]{:S(2)}) copy-start(bf16[512,1024]{1,0:T(8,128)(2,1)} %get-tuple-element.100) | copy-start | bytes 3145732
Sparse Core Ops, SparseCore 0:
  10.2 66.0 all-gather.6
  105.6 36.0 all-gather.8
  296.3 58.1 reduce-scatter.1
  356.3 58.9 all-gather.10

commit v4 on v3

--- a/solution.py
+++ b/solution.py
@@ -14,6 +14,7 @@
 norm_eps = 1e-05
 mask_fill = -1e30
 rope_base = 10000.0
+log2_e = 1.4426950408889634
 VMEM_LIMIT = 62 * 2**20
 F32 = jnp.float32
 BF16 = jnp.bfloat16
@@ -86,7 +87,7 @@
     q = q * cos + swap_halves(q, head_dim) * sin
     k = k * cos + swap_halves(k, head_dim) * sin
     k_low = k.astype(BF16)
-    q_ref[...] = (q.astype(BF16).astype(F32) * head_dim ** (-0.5)).astype(BF16)
+    q_ref[...] = (q * (head_dim ** (-0.5) * log2_e)).astype(BF16)
     k_ref[...] = k_low
     v_ref[...] = v
     kt_ref[...] = k_low.T
@@ -151,12 +152,12 @@
             if masked:
                 scores = scores + bias_ref[: last - first, :]
             top = jnp.max(scores, axis=0, keepdims=True)
-            weights = jnp.exp(scores - top)
+            weights = jnp.exp2(scores - top)
             totals = jnp.sum(weights, axis=0, keepdims=True)
             ot_ref[hs, at] = dot_nn(vt_ref[hs, first:last], weights.astype(BF16)) / totals
-            l_ref[pl.ds(h, 1), at] = top + jnp.log(totals)
-
-    @pl.when(bucket_ref[0] == 1)
+            l_ref[pl.ds(h, 1), at] = top + jnp.log2(totals)
+
+    @pl.when(bucket_ref[0, 0] == 1)
     def _():
         block(slice(0, rows), 0, total, False)
 
@@ -164,7 +165,7 @@
     for start in range(0, total, sub):
         first, last = key_range(start, sub, total)
 
-        @pl.when((bucket_ref[0] != 1) & (step == start // rows))
+        @pl.when((bucket_ref[0, 0] != 1) & (step == start // rows))
         def _():
             bias_ref[: last - first, :] = window_bias(first, last - first, start, sub, total)
             block(slice(start % rows, start % rows + sub), first, last, True)
@@ -178,26 +179,24 @@
     block = min(1024, n)
     pairs = n * n * heads
     lanes = -(-heads // 8) * 8
-    row = pl.BlockSpec((block, width), lambda i, *_: (i, 0))
-    col = pl.BlockSpec((width, block), lambda i, *_: (0, i))
+    row = pl.BlockSpec((block, width), lambda i: (i, 0))
+    col = pl.BlockSpec((width, block), lambda i: (0, i))
     return pl.pallas_call(
         functools.partial(attend_kernel, head_dim),
-        grid_spec=pltpu.PrefetchScalarGridSpec(
-            num_scalar_prefetch=1,
-            grid=(n // block,),
-            in_specs=[
-                row,
-                pl.BlockSpec((n, width), lambda i, *_: (0, 0)),
-                pl.BlockSpec((width, n), lambda i, *_: (0, 0)),
-            ],
-            out_specs=[row, col, pl.BlockSpec((lanes, block), lambda i, *_: (0, i))],
-            scratch_shapes=[pltpu.VMEM((n, min(512, block)), F32)],
-        ),
+        grid=(n // block,),
+        in_specs=[
+            pl.BlockSpec(memory_space=pltpu.SMEM),
+            row,
+            pl.BlockSpec((n, width), lambda i: (0, 0)),
+            pl.BlockSpec((width, n), lambda i: (0, 0)),
+        ],
+        out_specs=[row, col, pl.BlockSpec((lanes, block), lambda i: (0, i))],
         out_shape=[
             jax.ShapeDtypeStruct((n, width), BF16),
             jax.ShapeDtypeStruct((width, n), F32),
             jax.ShapeDtypeStruct((lanes, n), F32),
         ],
+        scratch_shapes=[pltpu.VMEM((n, min(512, block)), F32)],
         compiler_params=pltpu.CompilerParams(vmem_limit_bytes=VMEM_LIMIT),
         cost_estimate=pl.CostEstimate(
             flops=pairs * 1024, bytes_accessed=10 * n * width, transcendentals=pairs
@@ -247,7 +246,7 @@
             scores = dot_nt(k_ref[keys, :], qh)
             if masked:
                 scores = scores + bias_ref[: last - first, :]
-            probs = jnp.exp(scores - l_ref[pl.ds(h, 1), :])
+            probs = jnp.exp2(scores - l_ref[pl.ds(h, 1), :])
             prob_grad = dot_nt(v_ref[keys, :], gh)
             delta = jnp.sum(gt_ref[hs, :], axis=0, keepdims=True)
             score_grad = (probs * (prob_grad - delta)).astype(BF16)
@@ -255,14 +254,14 @@
             dk_ref[keys, :] += dot_nn(score_grad, qh)
             dq_ref[hs, :] = dot_nn(kt_ref[hs, keys], score_grad)
 
-    @pl.when(bucket_ref[0] == 1)
+    @pl.when(bucket_ref[0, 0] == 1)
     def _():
         block(0, total, False)
 
     for start in range(0, total, rows):
         first, last = key_range(start, rows, total)
 
-        @pl.when((bucket_ref[0] != 1) & (step == start // rows))
+        @pl.when((bucket_ref[0, 0] != 1) & (step == start // rows))
         def _():
             bias_ref[: last - first, :] = window_bias(first, last - first, start, rows, total)
             block(first, last, True)
@@ -279,7 +278,7 @@
         @pl.loop(0, total // rows)
         def _(i):
             at = pl.ds(pl.multiple_of(i * rows, rows), rows)
-            out_ref[at, width : 2 * width] = turn_back(dk_ref[at, :], at)
+            out_ref[at, width : 2 * width] = turn_back(dk_ref[at, :] * (1.0 / log2_e), at)
             out_ref[at, 2 * width :] = dv_ref[at, :].astype(BF16)
 
 
@@ -288,36 +287,34 @@
     heads = width // head_dim
     block = min(512, n)
     pairs = n * n * heads
-    row = pl.BlockSpec((block, width), lambda i, *_: (i, 0))
-    col = pl.BlockSpec((width, block), lambda i, *_: (0, i))
-    full = lambda rows, cols: pl.BlockSpec((rows, cols), lambda i, *_: (0, 0))
+    row = pl.BlockSpec((block, width), lambda i: (i, 0))
+    col = pl.BlockSpec((width, block), lambda i: (0, i))
+    full = lambda rows, cols: pl.BlockSpec((rows, cols), lambda i: (0, 0))
     table = full(n, cos_wide.shape[1])
     return pl.pallas_call(
         functools.partial(attend_back_kernel, head_dim),
-        grid_spec=pltpu.PrefetchScalarGridSpec(
-            num_scalar_prefetch=1,
-            grid=(n // block,),
-            in_specs=[
-                row,
-                full(n, width),
-                full(width, n),
-                full(n, width),
-                row,
-                col,
-                pl.BlockSpec((log_totals.shape[0], block), lambda i, *_: (0, i)),
-                table,
-                table,
-            ],
-            out_specs=full(n, 3 * width),
-            scratch_shapes=[
-                pltpu.VMEM((n, block), F32),
-                pltpu.VMEM((width, block), F32),
-                pltpu.VMEM((width, block), F32),
-                pltpu.VMEM((n, width), F32),
-                pltpu.VMEM((n, width), F32),
-            ],
-        ),
+        grid=(n // block,),
+        in_specs=[
+            pl.BlockSpec(memory_space=pltpu.SMEM),
+            row,
+            full(n, width),
+            full(width, n),
+            full(n, width),
+            row,
+            col,
+            pl.BlockSpec((log_totals.shape[0], block), lambda i: (0, i)),
+            table,
+            table,
+        ],
+        out_specs=full(n, 3 * width),
         out_shape=jax.ShapeDtypeStruct((n, 3 * width), BF16),
+        scratch_shapes=[
+            pltpu.VMEM((n, block), F32),
+            pltpu.VMEM((width, block), F32),
+            pltpu.VMEM((width, block), F32),
+            pltpu.VMEM((n, width), F32),
+            pltpu.VMEM((n, width), F32),
+        ],
         compiler_params=pltpu.CompilerParams(vmem_limit_bytes=VMEM_LIMIT),
         cost_estimate=pl.CostEstimate(
             flops=pairs * 2560, bytes_accessed=24 * n * width, transcendentals=pairs
@@ -689,6 +686,12 @@
     wq_copy = pltpu.make_async_copy(wq, wq_out, local.at[0])
     wq_copy.start()
 
+    stores = [
+        pltpu.make_async_copy(rows_all, rows_out, local.at[1]),
+        pltpu.make_async_copy(cots, cots_out, local.at[2]),
+        pltpu.make_async_copy(wos, wos_out, local.at[3]),
+    ]
+
     @pl.when(jnp.logical_not(home))
     def _():
         give[1].wait_recv()
@@ -709,6 +712,9 @@
             relay.wait_recv()
             shares[3].start()
             shares[3].wait_recv()
+            stores[0].start()
+            gather_finish(cot_copies)
+            stores[1].start()
 
         block = lax.bitwise_xor(z, i)
         at = pl.ds(pl.multiple_of(block * rows, rows), rows)
@@ -718,23 +724,15 @@
         v = v.astype(BF16)
         q = q * cos + swap_halves(q, head_dim) * sin
         k = (k * cos + swap_halves(k, head_dim) * sin).astype(BF16)
-        q_ref[at, :] = (q.astype(BF16).astype(F32) * head_dim ** (-0.5)).astype(BF16)
+        q_ref[at, :] = (q * (head_dim ** (-0.5) * log2_e)).astype(BF16)
         k_ref[at, :] = k
         v_ref[at, :] = v
         kt_ref[:, at] = k.T
         vt_ref[:, at] = v.T
 
-    gather_finish(cot_copies)
     gather_finish(out_copies)
-    stores = [
-        wq_copy,
-        pltpu.make_async_copy(rows_all, rows_out, local.at[1]),
-        pltpu.make_async_copy(cots, cots_out, local.at[2]),
-        pltpu.make_async_copy(wos, wos_out, local.at[3]),
-    ]
-    for store in stores[1:]:
-        store.start()
-    for store in stores:
+    stores[2].start()
+    for store in (wq_copy, *stores):
         store.wait()
 
     @pl.when(home)
@@ -894,23 +892,33 @@
     gather_start(copies)
     gather_forward(copies)
 
-    for s in range(ways):
+    turn = jnp.where(z > 2 * core, 2, 0)
+    step = min(256, rows)
+
+    @pl.loop(0, ways)
+    def _(k):
+        s = lax.bitwise_xor(k, turn)
         source_core, source_z = head_source(s)
 
         @pl.when(jnp.logical_not((source_core == core) & (source_z == z)))
         def _():
             in_wait(s).wait_recv()
 
-    step = min(256, rows)
+        at_ref[s] = at[s]
+        weights = wo_ref[pl.ds(pl.multiple_of(s * quarter, quarter), quarter), :]
+
+        @pl.when(k == 0)
+        def _():
+            resid_ref[...] = tok_ref[...].astype(F32) + dot_nn(at[s], weights)
+
+        @pl.when(k > 0)
+        def _():
+            resid_ref[...] += dot_nn(at[s], weights)
 
     @pl.loop(0, rows // step)
     def _(k):
         rs = pl.ds(pl.multiple_of(k * step, step), step)
-        acc = tok_ref[rs, :].astype(F32)
-        for s in range(ways):
-            acc += dot_nn(at[s, rs, :], wo_ref[s * quarter : (s + 1) * quarter, :])
-            at_ref[s, rs, :] = at[s, rs, :]
-        resid_ref[rs, :] = acc
+        acc = resid_ref[rs, :]
         centred = acc - jnp.mean(acc, axis=-1, keepdims=True)
         root = lax.rsqrt(jnp.mean(centred * centred, axis=-1, keepdims=True) + norm_eps)
         n_ref[rs, :] = (centred * root * gain_ref[...] + shift_ref[...]).astype(BF16)
@@ -978,6 +986,7 @@
     rg_ref,
     og_ref,
     out_ref,
+    high_ref,
     grads_ref,
     ng_ref,
     wgu_ref,
@@ -1006,16 +1015,22 @@
     orecv,
     csem,
     wsem,
+    upsend,
+    uprecv,
+    downsend,
+    downrecv,
     lsem,
     credit,
 ):
-    ways, split = w_low_ref.shape[:2]
-    unit = 2 * split // 3
-    units = ways * unit
+    ways, unit = w_low_ref.shape[0], w_low_ref.shape[1] // 3
+    part_units = ways * unit
+    units = 2 * part_units
     rows, d = x_ref.shape
     quarter = d // ways
     half = rows // 2
     low, high = pl.ds(0, half), pl.ds(half, half)
+    keep = out_ref.shape[0]
+    kept, others_at = pl.ds(0, keep), pl.ds(keep, rows - keep)
     me, z = lax.axis_index("dp"), lax.axis_index("tensor")
     core, heads_of, group_of = head_share()
     sib, across, along = plane_peers()
@@ -1035,40 +1050,114 @@
         for i in range(8)
         for k, (ref, side) in enumerate(((c_low_ref, low), (c_high_ref, high)))
     ]
-    weights = []
-    for t in range(ways):
-        dst = pl.ds(t * unit, unit)
-        places = (wgu_ref.at[dst], wgu_ref.at[pl.ds(units + t * unit, unit)], wd_ref.at[dst])
-        for j, place in enumerate(places):
-            for k, (ref, first) in enumerate(((w_low_ref, 0), (w_high_ref, split))):
-                start = max(j * unit, first)
-                size = min((j + 1) * unit, first + split) - start
-                if size > 0:
-                    src = ref.at[t, pl.ds(start - first, size)]
-                    dst_rows = place.at[pl.ds(start - j * unit, size)]
-                    weights.append(pltpu.make_async_copy(src, dst_rows, wsem.at[t, j, k]))
+
+    def weight_place(t, j, upper):
+        first = part_units * (upper if j == 2 else 2 * upper + j) + t * unit
+        ref = wd_ref if j == 2 else wgu_ref
+        return ref.at[pl.ds(first if isinstance(first, int) else pl.multiple_of(first, 16), unit)]
+
+    weights = [
+        pltpu.make_async_copy(
+            w_low_ref.at[t, pl.ds(j * unit, unit)], weight_place(t, j, 0), wsem.at[t, j]
+        )
+        for t in range(ways)
+        for j in range(3)
+    ]
+    upper_own = [
+        pltpu.make_async_copy(
+            w_high_ref.at[pl.ds(j * unit, unit)], weight_place(z, j, 1), wsem.at[ways, j]
+        )
+        for j in range(3)
+    ]
+    above, below = {"tensor": lax.rem(z + 1, ways)}, {"tensor": lax.rem(z + ways - 1, ways)}
+
+    def weight_up(t):
+        return [
+            pltpu.make_async_remote_copy(
+                src_ref=weight_place(t, j, 1),
+                dst_ref=weight_place(t, j, 1),
+                send_sem=upsend.at[t, j],
+                recv_sem=uprecv.at[t, j],
+                device_id=above,
+                device_id_type=MESH_ID,
+            )
+            for j in range(3)
+        ]
+
+    def weight_down(t):
+        return [
+            pltpu.make_async_remote_copy(
+                src_ref=weight_place(t, j, 1),
+                dst_ref=weight_place(t, j, 1),
+                send_sem=downsend.at[t, j],
+                recv_sem=downrecv.at[t, j],
+                device_id=below,
+                device_id_type=MESH_ID,
+            )
+            for j in range(3)
+        ]
+
+    def weight_round(r):
+        t = z + 1 + r
+
+        @pl.when(t < ways)
+        def _():
+            for copy in weight_down(t):
+                copy.wait_recv()
+
+            @pl.when(z > 0)
+            def _():
+                for copy in weight_down(t):
+                    copy.start()
+
+        u = z - 1 - r
+
+        @pl.when(u >= 0)
+        def _():
+            for copy in weight_up(u):
+                copy.wait_recv()
+
+            @pl.when(z < ways - 1)
+            def _():
+                for copy in weight_up(u):
+                    copy.start()
+
     own.wait()
     copies = gather_copies(lambda s, side: half_of(xs.at[s], side), gsend, grecv, False)
     gather_start(copies)
-    for load in (*weights, *cots, *first_loads):
+    for load in (*upper_own, *weights, *cots, *first_loads):
         load.start()
+    for load in upper_own:
+        load.wait()
+
+    @pl.when(z < ways - 1)
+    def _():
+        for copy in weight_up(z):
+            copy.start()
+
+    @pl.when(z > 0)
+    def _():
+        for copy in weight_down(z):
+            copy.start()
+
     down_acc[...] = jnp.zeros_like(down_acc)
     gate_up_acc[...] = jnp.zeros_like(gate_up_acc)
     for load in weights:
         load.wait()
 
-    def plane_sums(send, recv, src, landing):
+    def plane_sums(send, recv, src, landing, size):
+        first, second = pl.ds(0, size // 2), pl.ds(size // 2, size // 2)
         steps = [
             ("1", src(1), landing[0], sib),
             ("3", src(3), landing[1], sib),
             ("5", src(5), landing[2], sib),
             ("7", src(7), landing[3], sib),
-            ("6l", src(6).at[low], from_far.at[low], across),
-            ("6h", src(6).at[high], from_far.at[high], along),
-            ("2l", src(2).at[low], from_x.at[low], across),
-            ("2h", src(2).at[high], from_x.at[high], across),
-            ("4l", src(4).at[low], from_y.at[low], along),
-            ("4h", src(4).at[high], from_y.at[high], along),
+            ("6l", src(6).at[first], from_far.at[first], across),
+            ("6h", src(6).at[second], from_far.at[second], along),
+            ("2l", src(2).at[first], from_x.at[first], across),
+            ("2h", src(2).at[second], from_x.at[second], across),
+            ("4l", src(4).at[first], from_y.at[first], along),
+            ("4h", src(4).at[second], from_y.at[second], along),
         ]
         return {
             name: remote(ref, dst, send, recv, i, peer)
@@ -1081,96 +1170,116 @@
     def slot(i):
         return i // 2 if i % 2 == 0 else 4 + (i // 2) % 2
 
-    landing = [from_sib.at[0], from_sib.at[1], from_sib.at[2], from_sib.at[0]]
-    sums = plane_sums(ssend, srecv, lambda i: part.at[slot(i)], landing)
+    landing = [from_sib.at[0], from_sib.at[0], from_sib.at[1], from_sib.at[2]]
+    sums = plane_sums(ssend, srecv, lambda i: part.at[slot(i)], landing, rows)
+
+    def forward(i, place, into):
+        both = dot_nt(xs[i], wgu_ref[...])
+        hidden_grad = dot_nt(cs[i], wd_ref[...])
+        for upper in range(2):
+            of_units = slice(upper * part_units, (upper + 1) * part_units)
+            first = upper * units
+            gate = both[:, first : first + part_units]
+            up = both[:, first + part_units : first + units]
+            grad = hidden_grad[:, of_units]
+            sig = jax.nn.sigmoid(gate)
+            silu = gate * sig
+            hid[place, :, of_units] = (silu * up).astype(BF16)
+            branch[place, :, first : first + part_units] = (
+                grad * up * sig * (1.0 + gate * (1.0 - sig))
+            ).astype(BF16)
+            branch[place, :, first + part_units : first + units] = (grad * silu).astype(BF16)
+        part[into] = dot_nn(branch[place], wgu_ref[...]).astype(BF16)
 
     def grads(i, place):
         down_acc[...] += dot_tn(hid[place], cs[i])
         gate_up_acc[...] += dot_tn(branch[place], xs[i])
         cs[i] = dot_nn(hid[place], wd_ref[...]).astype(BF16)
 
-    @pl.loop(0, 8)
-    def _(i):
-        @pl.when(i == 1)
-        def _():
-            copies["0-1"].wait_recv()
-
-        @pl.when(i == 2)
-        def _():
-            gather_forward(copies)
-
-        @pl.when(i == 3)
-        def _():
-            copies["2-3"].wait_recv()
-
-        @pl.when(i == 4)
-        def _():
-            sums["1"].wait_recv()
-            add_to(part.at[0], from_sib.at[0])
-
-        @pl.when(i == 5)
-        def _():
-            copies["4-5"].wait_recv()
-            sums["3"].wait_recv()
-            add_to(part.at[1], from_sib.at[1])
-            sums["2l"].start()
-            sums["1"].wait_send()
-
-        @pl.when(i == 6)
-        def _():
-            copies["2-6"].wait_recv()
-            copies["4-6"].wait_recv()
-            copies["6-7"].start()
-
-        @pl.when(i == 7)
-        def _():
-            copies["6-7"].wait_recv()
-            sums["5"].wait_recv()
-            add_to(part.at[2], from_sib.at[2])
-            sums["4h"].start()
-            sums["3"].wait_send()
-
-        for k in range(8):
+    def cot_wait(i, slots):
+        for k in slots:
 
             @pl.when(i == k)
             def _(k=k):
                 cots[2 * k].wait()
                 cots[2 * k + 1].wait()
 
-        both = dot_nt(xs[i], wgu_ref[...])
-        gate, up = both[:, :units], both[:, units:]
-        sig = jax.nn.sigmoid(gate)
-        silu = gate * sig
-        place = jnp.where(i < 2, i, i - 2)
-        hid[place] = (silu * up).astype(BF16)
-        hidden_grad = dot_nt(cs[i], wd_ref[...])
-        branch[place, :, :units] = (
-            hidden_grad * up * sig * (1.0 + gate * (1.0 - sig))
-        ).astype(BF16)
-        branch[place, :, units:] = (hidden_grad * silu).astype(BF16)
+    weight_round(0)
+    weight_round(1)
+    gather_forward(copies)
+    for r in range(2, ways - 1):
+        weight_round(r)
+
+    @pl.loop(2, 8)
+    def _(i):
+        @pl.when(i == 3)
+        def _():
+            copies["2-3"].wait_recv()
+
+        @pl.when(i == 5)
+        def _():
+            copies["4-5"].wait_recv()
+            sums["3"].wait_recv()
+            add_to(part.at[1], from_sib.at[0])
+            sums["2l"].start()
+
+        @pl.when(i == 6)
+        def _():
+            copies["2-6"].wait_recv()
+            copies["4-6"].wait_recv()
+            copies["6-7"].start()
+
+        @pl.when(i == 7)
+        def _():
+            copies["6-7"].wait_recv()
+            sums["5"].wait_recv()
+            add_to(part.at[2], from_sib.at[1])
+            sums["4h"].start()
+            sums["3"].wait_send()
+
+        cot_wait(i, range(2, 8))
         even = lax.rem(i, 2) == 0
-        into = jnp.where(even, i // 2, 4 + lax.rem(i // 2, 2))
-        part[into] = dot_nn(branch[place], wgu_ref[...]).astype(BF16)
-        for odd in (1, 3, 5, 7):
+        forward(i, i - 2, jnp.where(even, i // 2, 4 + lax.rem(i // 2, 2)))
+        for odd in (3, 5, 7):
 
             @pl.when(i == odd)
             def _(odd=odd):
                 sums[str(odd)].start()
 
-        @pl.when(i < 2)
-        def _():
-            grads(i, i)
-
     @pl.loop(2, 8)
     def _(i):
         @pl.when(i == 3)
         def _():
             sums["7"].wait_recv()
-            add_to(part.at[3], from_sib.at[0])
+            add_to(part.at[3], from_sib.at[2])
             sums["6l"].start()
             sums["6h"].start()
 
-        @pl.when(i == 7)
+        grads(i, i - 2)
+
+    def grant(k, peer):
+        pl.semaphore_signal(credit.at[k], inc=1, device_id=peer, device_id_type=MESH_ID)
+
+    grant(0, sib)
+    outs = plane_sums(
+        fsend,
+        frecv,
+        lambda i: cs.at[i],
+        [from_sib.at[0], from_sib.at[1], branch.at[5], from_sib.at[2]],
+        keep,
+    )
+    pl.semaphore_wait(credit.at[0], 1)
+    for name in ("7", "3", "5"):
+        outs[name].start()
+    copies["0-1"].wait_recv()
+    sums["5"].wait_send()
+
+    @pl.loop(0, 2)
+    def _(i):
+        cot_wait(i, (0, 1))
+        forward(i, i, 4 * i)
+
+        @pl.when(i == 0)
         def _():
             sums["6l"].wait_recv()
             add_to(part.at[2, low], from_far.at[low])
@@ -1178,20 +1287,29 @@
             sums["6h"].wait_recv()
             add_to(part.at[1, high], from_far.at[high])
             sums["2h"].start()
-
-        grads(i, i - 2)
-
-    pl.semaphore_signal(credit.at[0], inc=1, device_id=sib, device_id_type=MESH_ID)
+            grant(1, across)
+            grant(2, along)
+
+        @pl.when(i == 1)
+        def _():
+            sums["1"].start()
+
+        grads(i, i)
+
+    sums["1"].wait_recv()
+    add_to(part.at[0], from_sib.at[0])
+    grant(3, sib)
     for copy in copies.values():
         copy.wait_send()
     for t in range(ways):
-        for j, (acc, first) in enumerate(
-            ((gate_up_acc, t * unit), (gate_up_acc, units + t * unit), (down_acc, t * unit))
-        ):
-            row = (3 * t + j) * unit
-            branch[row // rows, row % rows : row % rows + unit] = acc[first : first + unit].astype(
-                BF16
-            )
+        for j in range(3):
+            for upper in range(2):
+                row = 2 * (3 * t + j) * unit + upper * unit
+                first = part_units * (upper if j == 2 else 2 * upper + j) + t * unit
+                acc = down_acc if j == 2 else gate_up_acc
+                branch[row // rows, row % rows : row % rows + unit] = acc[
+                    first : first + unit
+                ].astype(BF16)
     for load in first_loads:
         load.wait()
     grads_copy = pltpu.make_async_copy(branch.at[pl.ds(0, grads_ref.shape[0])], grads_ref, lsem.at[1])
@@ -1205,19 +1323,22 @@
     for load in wo_loads:
         load.start()
 
-    outs = plane_sums(
-        fsend,
-        frecv,
-        lambda i: cs.at[i],
-        [from_sib.at[0], from_sib.at[1], from_sib.at[2], branch.at[5]],
-    )
-    pl.semaphore_wait(credit.at[0], 1)
-    for name in ("7", "3", "5", "1"):
-        outs[name].start()
+    outs["7"].wait_recv()
+    add_to(cs.at[6], from_sib.at[2])
+    outs["3"].wait_recv()
+    add_to(cs.at[2], from_sib.at[1])
+    outs["5"].wait_recv()
+    add_to(cs.at[4], branch.at[5])
+    pl.semaphore_wait(credit.at[3], 1)
+    outs["1"].start()
 
     grad = gate_up_acc
     for name in ("2l", "2h", "4l", "4h"):
         sums[name].wait_recv()
+    pl.semaphore_wait(credit.at[1], 1)
+    pl.semaphore_wait(credit.at[2], 1)
+    outs["6l"].start()
+    outs["6h"].start()
 
     @pl.loop(0, rows // step)
     def _(k):
@@ -1226,20 +1347,8 @@
             part[0, rs, :].astype(F32) + from_x[rs, :].astype(F32) + from_y[rs, :].astype(F32)
         )
 
-    pl.semaphore_signal(credit.at[1], inc=1, device_id=across, device_id_type=MESH_ID)
-    pl.semaphore_signal(credit.at[2], inc=1, device_id=along, device_id_type=MESH_ID)
-    outs["7"].wait_recv()
-    add_to(cs.at[6], branch.at[5])
-    pl.semaphore_wait(credit.at[1], 1)
-    pl.semaphore_wait(credit.at[2], 1)
-    outs["6l"].start()
-    outs["6h"].start()
-    outs["3"].wait_recv()
-    add_to(cs.at[2], from_sib.at[1])
-    outs["2l"].start()
-    outs["5"].wait_recv()
-    add_to(cs.at[4], from_sib.at[2])
-    outs["4h"].start()
+    grant(4, across)
+    grant(5, along)
 
     for load in wo_loads:
         load.wait()
@@ -1305,6 +1414,11 @@
         def _():
             agr[z] = xs[2, :, s * quarter : (s + 1) * quarter]
 
+    pl.semaphore_wait(credit.at[4], 1)
+    pl.semaphore_wait(credit.at[5], 1)
+    outs["2l"].start()
+    outs["4h"].start()
+
     for s in range(ways):
         place = 6 + s // half_wo
         first = (s % half_wo) * quarter
@@ -1312,11 +1426,20 @@
     og_copy = pltpu.make_async_copy(xs.at[pl.ds(6, 2)], og_ref, lsem.at[2])
     og_copy.start()
 
+    outs["1"].wait_recv()
+    add_to(cs.at[0], from_sib.at[0])
+    high_copies = [
+        pltpu.make_async_copy(cs.at[2 * k, others_at], high_ref.at[k], csem.at[k, 0])
+        for k in range(4)
+    ]
+    for copy in high_copies:
+        copy.start()
+    first, second = pl.ds(0, keep // 2), pl.ds(keep // 2, keep // 2)
     outs["6l"].wait_recv()
-    add_to(cs.at[4, low], from_far.at[low])
+    add_to(cs.at[4, first], from_far.at[first])
     outs["4l"].start()
     outs["6h"].wait_recv()
-    add_to(cs.at[2, high], from_far.at[high])
+    add_to(cs.at[2, second], from_far.at[second])
     outs["2h"].start()
 
     for source in range(ways):
@@ -1327,24 +1450,30 @@
 
     ag_copy = pltpu.make_async_copy(agr, ag_ref, lsem.at[3])
     ag_copy.start()
-    outs["1"].wait_recv()
     for name in ("2l", "2h", "4l", "4h"):
         outs[name].wait_recv()
-
-    @pl.loop(0, rows // step)
-    def _(k):
-        rs = pl.ds(pl.multiple_of(k * step, step), step)
-        total = resid[rs, :] + cs[0, rs, :].astype(F32) + from_sib[0, rs, :].astype(F32)
-        total += from_x[rs, :].astype(F32) + from_y[rs, :].astype(F32)
-        xs[0, rs, :] = total.astype(BF16)
-
+    total = resid[kept, :] + cs[0, kept, :].astype(F32)
+    total += from_x[kept, :].astype(F32) + from_y[kept, :].astype(F32)
+    xs[0, kept, :] = total.astype(BF16)
     grads_copy.wait()
-    lo_copy = pltpu.make_async_copy(xs.at[0], out_ref, lsem.at[1])
+    lo_copy = pltpu.make_async_copy(xs.at[0, kept], out_ref, lsem.at[1])
     lo_copy.start()
-    for name in ("5", "7", "6l", "6h", "2l", "2h", "4l", "4h"):
+    for name in ("1", "7", "6l", "6h", "2l", "2h", "4l", "4h"):
         sums[name].wait_send()
     for copy in outs.values():
         copy.wait_send()
+    for t in range(ways):
+
+        @pl.when((t <= z) & (z < ways - 1))
+        def _():
+            for copy in weight_up(t):
+                copy.wait_send()
+
+        @pl.when((t >= z) & (z > 0))
+        def _():
+            for copy in weight_down(t):
+                copy.wait_send()
+
     for s in range(ways):
         to_core, to_z = head_source(s)
 
@@ -1352,14 +1481,14 @@
         def _():
             out_copy(s).wait_send()
 
-    for copy in (rg_copy, og_copy, ag_copy, lo_copy):
+    for copy in (rg_copy, og_copy, ag_copy, lo_copy, *high_copies):
         copy.wait()
 
 
 def middle(x, attended, resid, out_full, cot_low, cot_high, w_low, w_high, gain):
     rows, d = x.shape
-    ways = w_low.shape[0]
-    units = ways * 2 * w_low.shape[1] // 3
+    ways, unit = w_low.shape[0], w_low.shape[1] // 3
+    units = 2 * ways * unit
     quarter = d // ways
     anywhere = pl.BlockSpec(memory_space=pl.ANY)
     inside = pl.BlockSpec(memory_space=pltpu.VMEM)
@@ -1367,12 +1496,13 @@
     return pl.pallas_call(
         middle_kernel,
         in_specs=[anywhere] * 8 + [inside],
-        out_specs=[anywhere] * 5 + [inside],
+        out_specs=[anywhere] * 6 + [inside],
         out_shape=[
             jax.ShapeDtypeStruct((ways, rows, quarter), BF16),
             jax.ShapeDtypeStruct((rows, d), F32),
             jax.ShapeDtypeStruct((2, rows, d), BF16),
-            jax.ShapeDtypeStruct((rows, d), BF16),
+            jax.ShapeDtypeStruct((rows - rows // 4, d), BF16),
+            jax.ShapeDtypeStruct((4, rows // 4, d), BF16),
             jax.ShapeDtypeStruct((3 * units // rows, rows, d), BF16),
             jax.ShapeDtypeStruct((8, d), F32),
         ],
@@ -1400,9 +1530,12 @@
         + sems(ways)
         + [
             pltpu.SemaphoreType.DMA((8, 2)),
-            pltpu.SemaphoreType.DMA((ways, 3, 2)),
+            pltpu.SemaphoreType.DMA((ways + 1, 3)),
+        ]
+        + [pltpu.SemaphoreType.DMA((ways, 3))] * 4
+        + [
             pltpu.SemaphoreType.DMA((5,)),
-            pltpu.SemaphoreType.REGULAR((3,)),
+            pltpu.SemaphoreType.REGULAR((6,)),
         ],
         compiler_params=pltpu.CompilerParams(
             collective_id=1, has_side_effects=True, vmem_limit_bytes=VMEM_LIMIT
@@ -1418,6 +1551,7 @@
     mixed_ref,
     w_ref,
     out_parts_ref,
+    ffn_parts_ref,
     rows_ref,
     tok_ref,
     norm_ref,
@@ -1425,6 +1559,7 @@
     og_ref,
     qkv_ref,
     ng_ref,
+    ffn_ref,
     lines,
     line_sib,
     line_z,
@@ -1445,7 +1580,12 @@
     qkv_z,
     qkvs,
     norms,
+    norm_sum,
     norms_z,
+    ffn,
+    ffn_far,
+    ffn_x,
+    ffn_y,
     lsend,
     lrecv,
     hsend,
@@ -1466,7 +1606,10 @@
     nrecv,
     zsend,
     zrecv,
+    fsend,
+    frecv,
     load_sem,
+    ffn_sem,
 ):
     me, z = lax.axis_index("dp"), lax.axis_index("tensor")
     ways, rows = lines.shape[0], lines.shape[1]
@@ -1482,7 +1625,8 @@
     others = [{"tensor": lax.rem(z + k, ways)} for k in range(1, ways)]
     z1, z2, z3 = (lax.bitwise_xor(z, k) for k in (1, 2, 3))
     near, far = {"tensor": z1}, {"tensor": z2}
-    enter([sib, across, along] + others)
+    plane = [{"dp": lax.bitwise_xor(me, k)} for k in range(1, 8)]
+    enter(plane + others)
 
     loads = []
     for i in range(8):
@@ -1500,6 +1644,9 @@
         for load in loads[-1]:
             load.start()
 
+    ffn_load = pltpu.make_async_copy(ffn_parts_ref, ffn, ffn_sem)
+    ffn_load.start()
+
     def add_to(ref, other):
         ref[...] = (ref[...].astype(F32) + other[...].astype(F32)).astype(BF16)
 
@@ -1535,20 +1682,6 @@
     to_far = remote(lines.at[z2, part_of(core)], line_z.at[2], lsend, lrecv, 2, far)
     last_away = remote(line_z.at[2], line_end, lsend, lrecv, 3, sib)
     last_home = remote(lines.at[z, part_of(core)], line_end, lsend, lrecv, 3, sib)
-
-    @pl.loop(0, ways)
-    def _(k):
-        i = ways - 1 - k
-        i = jnp.where(i == 2, 1, jnp.where(i == 1, 2, i))
-        line(i)
-        for fixed in range(ways):
-
-            @pl.when(i == fixed)
-            def _(fixed=fixed):
-                share(fixed).start()
-                if fixed == 1:
-                    share_join(3)
-                    to_near[0].start()
 
     sums = [
         ("1", part.at[1], from_sib.at[0], sib),
@@ -1566,15 +1699,40 @@
         name: remote(src, dst, ssend, srecv, i, peer)
         for i, (name, src, dst, peer) in enumerate(sums)
     }
-    for i in (7, 3, 5, 1):
-        for load in loads[i]:
-            load.wait()
-        sums[str(i)].start()
+
+    def qkv_rows(j):
+        at = pl.ds(pl.multiple_of(j * width, width), width)
+        qkv[at, :] = dot_tn(mixed_ref[:, at], rows_ref[...]).astype(BF16)
+
+    edge = ffn.shape[1] // 2
+    first, second = pl.ds(0, edge), pl.ds(edge, edge)
+    ffns = [
+        ("3l", ffn.at[3, first], ffn_far.at[first], across),
+        ("3h", ffn.at[3, second], ffn_far.at[second], along),
+        ("1l", ffn.at[1, first], ffn_x.at[first], across),
+        ("1h", ffn.at[1, second], ffn_x.at[second], across),
+        ("2l", ffn.at[2, first], ffn_y.at[first], along),
+        ("2h", ffn.at[2, second], ffn_y.at[second], along),
+    ]
+    ffns = {
+        name: remote(src, dst, fsend, frecv, i, peer)
+        for i, (name, src, dst, peer) in enumerate(ffns)
+    }
+    ffn_load.wait()
+    for name in ("3l", "3h", "1l", "2h"):
+        ffns[name].start()
+
+    line(3)
+    share(3).start()
 
     @pl.loop(0, 3)
     def _(j):
-        at = pl.ds(pl.multiple_of(j * width, width), width)
-        qkv[at, :] = dot_tn(mixed_ref[:, at], rows_ref[...]).astype(BF16)
+        qkv_rows(j)
+
+        @pl.when(j == 0)
+        def _():
+            share_join(3)
+            to_near[0].start()
 
     piece = qkv_sum.shape[0]
     small = piece // 2
@@ -1601,7 +1759,33 @@
     for name in ("3l", "3h", "1l", "2h"):
         pieces[name].start()
 
+    @pl.loop(0, ways - 1)
+    def _(k):
+        i = lax.rem(k + 1, ways - 1)
+        line(i)
+        for fixed in range(ways - 1):
+
+            @pl.when(i == fixed)
+            def _(fixed=fixed):
+                share(fixed).start()
+
+    for i in (7, 3, 5, 1):
+        for load in loads[i]:
+            load.wait()
+        sums[str(i)].start()
+
+    pieces["3l"].wait_recv()
+    add_to(qkv_at(2, 0), side_of(qkv_far, 0))
+    pieces["2l"].start()
+    pieces["3h"].wait_recv()
+    add_to(qkv_at(1, 1), side_of(qkv_far, 1))
+    pieces["1h"].start()
     share_join(1)
+    share_join(2)
+    to_near[0].wait_recv()
+    to_near[1].start()
+    add_to(lines.at[z2, part_of(core)], line_z.at[0])
+    to_far.start()
     for i, j, names in ((6, 3, ("6l", "6h")), (2, 1, ("2l",)), (4, 2, ("4h",))):
         for load in loads[i]:
             load.wait()
@@ -1609,25 +1793,7 @@
         add_to(part.at[i], from_sib.at[j])
         for name in names:
             sums[name].start()
-    share_join(2)
-    to_near[0].wait_recv()
-    to_near[1].start()
-    add_to(lines.at[z2, part_of(core)], line_z.at[0])
-    to_far.start()
     share_join(0)
-
-    pieces["3l"].wait_recv()
-    add_to(qkv_at(2, 0), side_of(qkv_far, 0))
-    pieces["2l"].start()
-    pieces["3h"].wait_recv()
-    add_to(qkv_at(1, 1), side_of(qkv_far, 1))
-    pieces["1h"].start()
-    sums["6l"].wait_recv()
-    add_to(part.at[4, low], from_far.at[low])
-    sums["4l"].start()
-    sums["6h"].wait_recv()
-    add_to(part.at[2, high], from_far.at[high])
-    sums["2h"].start()
 
     for name in ("1l", "1h", "2l", "2h"):
         pieces[name].wait_recv()
@@ -1654,6 +1820,19 @@
     def _():
         qkv_z[group_of] = qkv_sum[...]
 
+    ffns["3l"].wait_recv()
+    add_to(ffn.at[2, first], ffn_far.at[first])
+    ffns["2l"].start()
+    ffns["3h"].wait_recv()
+    add_to(ffn.at[1, second], ffn_far.at[second])
+    ffns["1h"].start()
+    sums["6l"].wait_recv()
+    add_to(part.at[4, low], from_far.at[low])
+    sums["4l"].start()
+    sums["6h"].wait_recv()
+    add_to(part.at[2, high], from_far.at[high])
+    sums["2h"].start()
+
     for load in loads[0]:
         load.wait()
     sums["1"].wait_recv()
@@ -1711,6 +1890,10 @@
     gathers = gather_copies(view, gsend, grecv, True)
     gather_start(gathers)
 
+    for name in ("1l", "1h", "2l", "2h"):
+        ffns[name].wait_recv()
+    ffn_ref[...] = ffn[0].astype(F32) + ffn_x[...].astype(F32) + ffn_y[...].astype(F32)
+
     to_near[1].wait_recv()
     add_to(lines.at[z, part_of(core)], line_z.at[1])
 
@@ -1732,7 +1915,7 @@
     last_away.wait_recv()
     n_ref[part_of(1 - core), :] = line_end[...].astype(F32)
 
-    norms[0] = norm_ref[...]
+    norms[me] = norm_ref[...]
     step = min(128, rows)
 
     @pl.loop(0, rows // step)
@@ -1742,14 +1925,14 @@
         centred = values - jnp.mean(values, axis=-1, keepdims=True)
         root = lax.rsqrt(jnp.mean(centred * centred, axis=-1, keepdims=True) + norm_eps)
         grad = n_ref[at, :]
-        norms[0, 0:1] += jnp.sum(grad * (centred * root), axis=0, keepdims=True)
-        norms[0, 1:2] += jnp.sum(grad, axis=0, keepdims=True)
-
-    swaps = [
-        remote(norms.at[i], norms.at[4 + i], nsend, nrecv, i, peer)
-        for i, peer in enumerate((sib, across, along))
-    ]
-    swaps[0].start()
+        norms[me, 0:1] += jnp.sum(grad * (centred * root), axis=0, keepdims=True)
+        norms[me, 1:2] += jnp.sum(grad, axis=0, keepdims=True)
+
+    def swap(k, source):
+        return remote(norms.at[source], norms.at[source], nsend, nrecv, k, plane[k])
+
+    for k in range(7):
+        swap(k, me).start()
 
     gather_forward(gathers)
 
@@ -1762,15 +1945,13 @@
         y_on.start()
         to_sib[2].start()
 
-    for i, swap in enumerate(swaps):
-        if i:
-            swap.start()
-        swap.wait_recv()
-        norms[i + 1] = norms[i] + norms[4 + i]
+    for k in range(7):
+        swap(k, lax.bitwise_xor(me, k + 1)).wait_recv()
+    norm_sum[...] = sum(norms[k] for k in range(8))
 
     def norm_copy(k, to, source):
         return pltpu.make_async_remote_copy(
-            src_ref=norms.at[3],
+            src_ref=norm_sum,
             dst_ref=norms_z.at[source],
             send_sem=zsend.at[k],
             recv_sem=zrecv.at[source],
@@ -1780,7 +1961,7 @@
 
     for k in range(1, ways):
         norm_copy(k, lax.rem(z + k, ways), z).start()
-    norms_z[z] = norms[3]
+    norms_z[z] = norm_sum[...]
     gather_finish(gathers)
     og_ref[...] = ogs[...]
 
@@ -1818,8 +1999,10 @@
     def _():
         last_home.wait_send()
 
-    for copy in (*sums.values(), *gathers.values(), *pieces.values(), *swaps, *to_near, to_far):
+    for copy in (*sums.values(), *gathers.values(), *pieces.values(), *ffns.values(), *to_near, to_far):
         copy.wait_send()
+    for k in range(7):
+        swap(k, me).wait_send()
     for i in range(ways):
         share(i).wait_send()
     for k in range(1, ways):
@@ -1828,7 +2011,7 @@
         norm_copy(k, to, z).wait_send()
 
 
-def tail(mixed, w, out_parts, rows_one, tokens, norm_grads, ways):
+def tail(mixed, w, out_parts, ffn_parts, rows_one, tokens, norm_grads, ways):
     rows, d = tokens.shape
     out_rows = out_parts.shape[1] // 8
     qkv_rows = mixed.shape[1] // 4
@@ -1838,13 +2021,14 @@
     sems = lambda n: [pltpu.SemaphoreType.DMA((n,))] * 2
     return pl.pallas_call(
         tail_kernel,
-        in_specs=[inside, inside, anywhere, inside, inside, inside],
-        out_specs=[inside] * 4,
+        in_specs=[inside] * 2 + [anywhere] * 2 + [inside] * 3,
+        out_specs=[inside] * 5,
         out_shape=[
             jax.ShapeDtypeStruct((rows, d), F32),
             jax.ShapeDtypeStruct((8, out_rows, d), BF16),
             jax.ShapeDtypeStruct((4, qkv_rows, d), BF16),
             jax.ShapeDtypeStruct((8, d), F32),
+            jax.ShapeDtypeStruct(ffn_parts.shape[1:], F32),
         ],
         scratch_shapes=[
             pltpu.VMEM((ways, rows, d), BF16),
@@ -1867,8 +2051,11 @@
             pltpu.VMEM((2, qkv_rows, d), BF16),
             pltpu.VMEM((4, qkv_rows, d), BF16),
             pltpu.VMEM((8, 8, d), F32),
+            pltpu.VMEM((8, d), F32),
             pltpu.VMEM((ways, 8, d), F32),
+            pltpu.VMEM(ffn_parts.shape, BF16),
         ]
+        + [pltpu.VMEM(ffn_parts.shape[1:], BF16)] * 3
         + sems(4)
         + sems(ways)
         + sems(10)
@@ -1877,9 +2064,10 @@
         + sems(6)
         + sems(2)
         + sems(8)
-        + sems(3)
+        + sems(7)
         + sems(ways)
-        + [pltpu.SemaphoreType.DMA((ways, 8))],
+        + sems(6)
+        + [pltpu.SemaphoreType.DMA((ways, 8)), pltpu.SemaphoreType.DMA],
         compiler_params=pltpu.CompilerParams(
             collective_id=2, has_side_effects=True, vmem_limit_bytes=VMEM_LIMIT
         ),
@@ -1887,10 +2075,11 @@
             flops=75 * 10**9, bytes_accessed=40 * rows * d, transcendentals=0
         ),
         name="tail",
-    )(mixed, w, out_parts, rows_one, tokens, norm_grads)
+    )(mixed, w, out_parts, ffn_parts, rows_one, tokens, norm_grads)
 
 
 def finish_kernel(
+    kept,
     both_ref,
     down_ref,
     features_ref,
@@ -1899,11 +2088,17 @@
     resid_ref,
     tok_ref,
     gain_ref,
+    low_ref,
+    high_ref,
+    before_ref,
+    norms_ref,
     gate_up_ref,
     down_out_ref,
     qkv_ref,
     og_out_ref,
     token_ref,
+    layer_ref,
+    *norm_refs,
 ):
     units = both_ref.shape[1] // 2
     for p in range(8):
@@ -1924,17 +2119,29 @@
     first_mean = jnp.mean(scaled, axis=-1, keepdims=True)
     second_mean = jnp.mean(scaled * unit_rows, axis=-1, keepdims=True)
     token_ref[...] = resid_ref[...] + root * (scaled - first_mean - unit_rows * second_mean)
-
-
-def finish(grads, features, out_grad, norm_grad, resid_grad, tokens, gain):
+    for k, ref in enumerate(norm_refs):
+        ref[...] = norms_ref[k : k + 1]
+    step = pl.program_id(0)
+
+    @pl.when(step < kept)
+    def _():
+        layer_ref[...] = low_ref[...]
+
+    @pl.when(step >= kept)
+    def _():
+        layer_ref[...] = (before_ref[...] + high_ref[...]).astype(BF16)
+
+
+def finish(grads, features, out_grad, norm_grad, resid_grad, tokens, gain, low, high, resid, norms):
     rows, d = tokens.shape
     units = grads.shape[1] // 3
     block = d // 8
     width = features.shape[0] // 3
     out_rows = out_grad.shape[1]
     own = pl.BlockSpec((rows // 8, d), lambda i: (i, 0))
+    kept = 8 * low.shape[0] // rows
     return pl.pallas_call(
-        finish_kernel,
+        functools.partial(finish_kernel, kept),
         grid=(8,),
         in_specs=[
             pl.BlockSpec((8, 2 * units, block), lambda i: (0, 0, i)),
@@ -1945,6 +2152,10 @@
             own,
             own,
             pl.BlockSpec((1, d), lambda i: (0, 0)),
+            pl.BlockSpec((rows // 8, d), lambda i: (jnp.minimum(i, kept - 1), 0)),
+            pl.BlockSpec((rows // 8, d), lambda i: (jnp.maximum(i - kept, 0), 0)),
+            own,
+            pl.BlockSpec(norms.shape, lambda i: (0, 0)),
         ],
         out_specs=[
             pl.BlockSpec((16 * block, units), lambda i: (i, 0)),
@@ -1952,17 +2163,34 @@
             pl.BlockSpec((3, block, width), lambda i: (0, i, 0)),
             pl.BlockSpec((out_rows, d), lambda i: (i, 0)),
             own,
-        ],
+            own,
+        ]
+        + [pl.BlockSpec((1, d), lambda i: (0, 0))] * 4,
         out_shape=[
             jax.ShapeDtypeStruct((16 * d, units), F32),
             jax.ShapeDtypeStruct((8 * units, d), F32),
             jax.ShapeDtypeStruct((3, d, width), F32),
             jax.ShapeDtypeStruct((8 * out_rows, d), F32),
             jax.ShapeDtypeStruct((rows, d), F32),
-        ],
+            jax.ShapeDtypeStruct((rows, d), BF16),
+        ]
+        + [jax.ShapeDtypeStruct((1, d), F32)] * 4,
         compiler_params=pltpu.CompilerParams(vmem_limit_bytes=VMEM_LIMIT),
         name="finish",
-    )(grads, grads, features, out_grad, norm_grad, resid_grad, tokens, gain[None])
+    )(
+        grads,
+        grads,
+        features,
+        out_grad,
+        norm_grad,
+        resid_grad,
+        tokens,
+        gain[None],
+        low,
+        high,
+        resid,
+        norms,
+    )
 
 
 def shards(
@@ -2007,7 +2235,7 @@
     cos_wide, sine_wide = rotary_wide(group_bucket[0], group_rows, head_dim, pair_width)
     qkv_weights = w_qkv.transpose(1, 0, 2)
     q, k, v, kt, vt = project(rows_one, qkv_weights, cos_wide, sine_wide, head_dim)
-    attended, *kept = attend(group_bucket, q, k, vt, head_dim)
+    attended, *kept = attend(group_bucket[None], q, k, vt, head_dim)
     attended_own = lax.all_to_all(attended, "tensor", 0, 1, tiled=True)
     resid = rows_in + dot_nn(attended_own, out_full)
     normed_two, unit_two, root_two = norm_forward(resid, gain_two, shift_two)
@@ -2043,7 +2271,7 @@
     grads = lax.psum_scatter(grads, "tensor", scatter_dimension=0)
 
     mixed_grad = attend_back(
-        group_bucket, q, k, kt, v, attended_grad, *kept, cos_wide, sine_wide, head_dim
+        group_bucket[None], q, k, kt, v, attended_grad, *kept, cos_wide, sine_wide, head_dim
     )
     grads, mixed_grad = lax.optimization_barrier((grads, mixed_grad))
     grads = lax.all_gather(grads, "dp", axis=0)
@@ -2102,11 +2330,12 @@
 
     gate_up_slice = lax.dynamic_slice_in_dim(w_gate_up, replica * units, units, axis=2)
     down_slice = lax.dynamic_slice_in_dim(w_down, replica * units, units, axis=0)
-    weight_slice = jnp.concatenate(
-        [gate_up_slice.transpose(1, 2, 0).reshape(2 * units, d), down_slice]
+    gate_up_slice = gate_up_slice.transpose(1, 2, 0)
+    half = units // 2
+    slice_low, slice_high = (
+        jnp.concatenate([gate_up_slice[:, at].reshape(units, d), down_slice[at]])
+        for at in (slice(0, half), slice(half, units))
     )
-    split = 3 * units // 2
-    weights_low = lax.all_gather(weight_slice[:split], "tensor", axis=0)
     q, k, v, kt, vt, cos_wide, sine_wide, bucket, rows_one, cot_low, out_full, qkv_weights = front(
         group_bucket,
         tokens,
@@ -2118,15 +2347,14 @@
         head_dim,
         ways,
     )
-    bucket, weight_slice = lax.optimization_barrier((bucket, weight_slice))
-    weights_high = lax.all_gather(weight_slice[split:], "tensor", axis=0)
-    bucket = bucket[0, :1]
+    bucket, slice_low = lax.optimization_barrier((bucket, slice_low))
+    weights_low = lax.all_gather(slice_low, "tensor", axis=0)
     out_full = out_full.reshape(d, d)
     attended, *kept = attend(bucket, q, k, vt, head_dim)
     attended_own, resid, normed_two, cot_high = collect(
         attended, tokens, out_full, gain_two, shift_two, cotangent, ways
     )
-    attended_grad, resid_grad, out_grad, layer_out, grads, norm_grads = middle(
+    attended_grad, resid_grad, out_grad, layer_low, ffn_parts, grads, norm_grads = middle(
         normed_two,
         attended_own,
         resid,
@@ -2134,7 +2362,7 @@
         cot_low,
         cot_high,
         weights_low,
-        weights_high,
+        slice_high,
         gain_two,
     )
     grads = grads.reshape(ways, 3 * units, d)
@@ -2145,16 +2373,17 @@
     )
     grads, mixed_grad = lax.optimization_barrier((grads, mixed_grad))
     grads = lax.all_gather(grads, "dp", axis=0)
-    normed_one_grad, out_grad, qkv_grad, norm_grads = tail(
+    normed_one_grad, out_grad, qkv_grad, norm_grads, layer_high = tail(
         mixed_grad,
         qkv_weights,
         out_grad.reshape(ways, local_width, d),
+        ffn_parts,
         rows_one.reshape(group_rows, d),
         tokens,
         norm_grads,
         ways,
     )
-    gate_up_grad, down_grad, qkv_grad, out_grad, token_grad = finish(
+    gate_up_grad, down_grad, qkv_grad, out_grad, token_grad, layer_out, *norm_grads = finish(
         grads,
         qkv_grad.reshape(3 * local_width, d),
         out_grad,
@@ -2162,11 +2391,15 @@
         resid_grad,
         tokens,
         gain_one,
+        layer_low,
+        layer_high,
+        resid,
+        norm_grads,
     )
     gate_up_grad = gate_up_grad.reshape(d, 8, 2, units).transpose(0, 2, 1, 3)
     gate_up_grad = gate_up_grad.reshape(d, 2, hidden_width)
     qkv_grad = qkv_grad.transpose(1, 0, 2)
-    gain_one_grad, shift_one_grad, gain_two_grad, shift_two_grad = (norm_grads[i] for i in range(4))
+    gain_one_grad, shift_one_grad, gain_two_grad, shift_two_grad = (g[0] for g in norm_grads)
     return (
         layer_out,
         token_grad,

time: 466 us -> 436 us (0.936)
  Pallas kernels: 423 us -> 394 us
  local copies, waits for them, and re-layouts: 8.63 us -> 3.45 us
    pallas_call x1, Pallas kernels: 92.5 us -> 64.6 us  [front(): pl.pallas_call(functools.partial(front_kernel, head_dim), in_specs=[pl.Bl...]
  transfers between devices with their start and end apart: 4 -> 3, of which waited for: 1 -> 1; matrix products, arithmetic and copies ran while one was open for 1% -> 0% of each run, Pallas kernels for 61% -> 44%
where the time goes in v4:
time: 436 us; the launch traced here: 432 us
  Pallas kernels  394 us (90%)
  waiting for transfers between devices  17.6 us (4%)
  between operations  14.7 us (3%)
    pallas_call x1, Pallas kernels, middle(): pl.pallas_call(middle_kernel, in_specs=[anywhere] * 8 + [inside], out_spe...  121 us
    pallas_call x1, Pallas kernels, tail(): pl.pallas_call(tail_kernel, in_specs=[inside] * 2 + [anywhere] * 2 + [ins...  85 us
    pallas_call x1, Pallas kernels, front(): pl.pallas_call(functools.partial(front_kernel, head_dim), in_specs=[pl.Bl...  64.6 us
    pallas_call x1, Pallas kernels, collect(): pl.pallas_call(collect_kernel, in_specs=[anywhere] + [inside] * 4 + [anyw...  41.2 us
    pallas_call x1, Pallas kernels, attend_back(): pl.pallas_call(functools.partial(attend_back_kernel, head_dim), grid=(n /...  41 us
    pallas_call x1, Pallas kernels, attend(): pl.pallas_call(functools.partial(attend_kernel, head_dim), grid=(n // blo...  24.8 us
    reduce_scatter x1, waiting for transfers between devices, shards_columns(): grads = lax.psum_scatter(grads, 'tensor', scatter_dimension=0)  17.5 us
    pallas_call x1, Pallas kernels, finish(): pl.pallas_call(functools.partial(finish_kernel, kept), grid=(8,), in_spec...  16.3 us
  transfers between devices with their start and end apart: 3, of which 1 were waited for; matrix products, arithmetic and copies ran while one was open for 0% of the time, Pallas kernels for 44%

profile of v4, /device:TPU:0, one launch (start us, length us, event | category | flops | bytes accessed | tf_op | source)
XLA Modules:
  0.0 431.9 jit_solution(15841080521090941249)
XLA Ops:
  7.2 0.0 all-gather.5.cloned.1.call-start
  7.9 0.6 broadcast_in_dim_tile.3.freq_ref
  8.5 1.4 constant_dynamic-slice_fusion.2
  9.9 0.4 copy.26
  10.4 1.0 constant_dynamic-slice_fusion.1
  11.4 0.8 pad_maximum_fusion
  12.1 64.6 %front.1 = (bf16[2048,256]{1,0:T(8,128)(2,1)}, bf16[2048,256]{1,0:T(8,128)(2,1)}, bf16[2048,256]{1,0:T(8,128)(2,1)}, bf16[256,2048]{1,0:T(8,128)(2,1)}, bf16[256...) custom-call(s32[1]{0:T(128)S(6)} %copy.27.bucket_ref, ...), custom_call_target="tpu_custom_call" | custom-call | flops 54999998464 | bytes 16777216 | tf_op jit(solution)/shard_map/front/pallas_call | solution.py:772
  76.8 0.0 all-gather.5.cloned.1.call-update
  76.8 0.3 reduce-scatter.2.cloned.1.call-start
  77.1 0.8 pad_maximum_fusion.1.w_high_ref
  77.9 24.8 %attend.1 = (bf16[2048,256]{1,0:T(8,128)(2,1)}, f32[256,2048]{1,0:T(8,128)}, f32[8,2048]{1,0:T(8,128)}) custom-call(s32[8,128]{1,0:T(8,128)} %get-tuple-element.56.bucket_ref, bf16[2048,256]{1,0:T(8,128)(2,1)} %get-tuple-element.57.q_ref, bf16[2048,256]{1,0:T(8,128)(2,1)} %get-tuple-element.58.k_ref, bf16[256,2048]{1,0:T(8,128)(2,1)} %get-tuple-element.59.vt_ref), custom_call_target="tpu_custom_call" | custom-call | flops 17179869184 | bytes 5242880 | tf_op jit(solution)/shard_map/attend/pallas_call | solution.py:184
  102.6 41.2 %collect.1 = (bf16[4,512,256]{2,1,0:T(8,128)(2,1)}, f32[512,1024]{1,0:T(8,128)}, bf16[512,1024]{1,0:T(8,128)(2,1)}, bf16[8,256,1024]{2,1,0:T(8,128)(2,1)}) custom-call(bf16[2048,256]{1,0:T(8,128)(2,1)} %get-tuple-element.60.att_ref, bf16[512,1024]{1,0:T(8,128)(2,1)} %tok_ref.7, bf16[1024,1024]{1,0:T(8,128)(2,1)} %bitcast.51, f32[1,1024]{1,0:T(1,128)} %bitcast.43, ...), custom_call_target="tpu_custom_call" | custom-call | flops 30000001024 | bytes 8388608 | tf_op jit(solution)/shard_map/collect/pallas_call | solution.py:946
  143.9 0.0 all-gather.5.cloned.1.call-done
  143.9 121.3 %middle.1 = (bf16[4,512,256]{2,1,0:T(8,128)(2,1)}, f32[512,1024]{1,0:T(8,128)}, bf16[2,512,1024]{2,1,0:T(8,128)(2,1)}, bf16[384,1024]{1,0:T(8,128)(2,1)}, bf16[4...) custom-call(bf16[512,1024]{1,0:T(8,128)(2,1)} %get-tuple-element.62.x_ref, ...), custom_call_target="tpu_custom_call" | custom-call | flops 130000003072 | bytes 20971520 | tf_op jit(solution)/shard_map/middle/pallas_call | solution.py:1496
  265.2 0.0 reduce-scatter.2.cloned.1.call-update
  265.2 0.0 all-gather.7.cloned.1.call-start
  265.2 41.0 %attend_back.1.mixed_ref = bf16[2048,768]{1,0:T(8,128)(2,1)} custom-call(s32[8,128]{1,0:T(8,128)} %get-tuple-element.56.bucket_ref, bf16[2048,256]{1,0:T(8,128)(2,1)} %get-tuple-element.57.q_ref, bf16[2048,256]{1,0:T(8,128)(2,1)} %get-tuple-element.58.k_ref, bf16[256,2048]{1,0:T(8,128)(2,1)} %get-tuple-element.69.kt_ref, ...), custom_call_target="tpu_custom_call" | custom-call | flops 42949672960 | bytes 12582912 | tf_op jit(solution)/shard_map/attend_back/pallas_call | solution.py:294
  306.3 17.5 %reduce-scatter.2.cloned.1.call-done = bf16[1,384,1024]{2,1,0:T(8,128)(2,1)} async-done(((bf16[4,384,1024]{2,1,0:T(8,128)(2,1)}), bf16[1,384,1024]{2,1,0:T(8,128)(2,1)}) %reduce-scatter.2.cloned.1.call-update) | async-done | bytes 786448 | tf_op jit(solution)/shard_map/reduce_scatter | solution.py:2369
  323.8 0.0 all-gather.7.cloned.1.call-update
  323.8 85.0 %tail.1 = (f32[512,1024]{1,0:T(8,128)}, bf16[8,32,1024]{2,1,0:T(8,128)(2,1)}, bf16[4,192,1024]{2,1,0:T(8,128)(2,1)}, f32[8,1024]{1,0:T(8,128)}, f32[128,1024]{1,0:T(8,128)}) custom-call(bf16[2048,768]{1,0:T(8,128)(2,1)} %attend_back.1.mixed_ref, bf16[3,1024,256]{2,1,0:T(8,128)(2,1)} %get-tuple-element.78.w_ref, bf16[4,256,1024]{2,1,0:T(8,128)(2,1)} %bitcast.50, ...), custom_call_target="tpu_custom_call" | custom-call | flops 74999996416 | bytes 20971520 | tf_op jit(solution)/shard_map/tail/pallas_call | solution.py:2022
  408.8 0.0 all-gather.7.cloned.1.call-done
  408.8 16.3 %finish.1 = (f32[16384,128]{1,0:T(8,128)}, f32[1024,1024]{1,0:T(8,128)}, f32[3,1024,256]{2,1,0:T(8,128)}, f32[256,1024]{1,0:T(8,128)}, f32[512,1024]{1,0:T(8,128...) custom-call(bf16[8,384,1024]{2,1,0:T(8,128)(2,1)} %bitcast.27, ...), custom_call_target="tpu_custom_call" | custom-call | tf_op jit(solution)/shard_map/finish/pallas_call | solution.py:2143
  (3 shorter events, 0.0 us)
Async XLA Ops:
  7.2 136.7 %all-gather.5.cloned.1.call-start = ((), (), s32[]{:S(2)}) async-start(), calls=%async_computation.2 | async-start | bytes 1966080 | tf_op jit(solution)/shard_map/all_gather | solution.py:2351
  76.8 247.0 %reduce-scatter.2.cloned.1.call-start = ((), (), s32[]{:S(2)}) async-start(), calls=%async_computation.1 | async-start | bytes 3932160 | tf_op jit(solution)/shard_map/reduce_scatter | solution.py:2369
  265.2 143.6 %all-gather.7.cloned.1.call-start = ((), (), s32[]{:S(2)}) async-start(), calls=%async_computation.3 | async-start | bytes 7077888 | tf_op jit(solution)/shard_map/all_gather | solution.py:2375
Sparse Core Ops, SparseCore 0:
  76.9 49.3 all-gather.4
  265.3 58.4 reduce-scatter.1
  325.7 65.7 all-gather.6

commit v5 on v4

--- a/solution.py
+++ b/solution.py
@@ -1547,11 +1547,70 @@
     )(x, attended, resid, out_full, cot_low, cot_high, w_low, w_high, gain[None])
 
 
+def ffn_rest_kernel(parts_ref, out_ref, ffn, ffn_far, ffn_x, ffn_y, fsend, frecv, load_sem):
+    _, across, along = plane_peers()
+    load = pltpu.make_async_copy(parts_ref, ffn, load_sem)
+    load.start()
+    enter([across, along])
+
+    def add_to(ref, other):
+        ref[...] = (ref[...].astype(F32) + other[...].astype(F32)).astype(BF16)
+
+    edge = ffn.shape[1] // 2
+    first, second = pl.ds(0, edge), pl.ds(edge, edge)
+    ffns = [
+        ("3l", ffn.at[3, first], ffn_far.at[first], across),
+        ("3h", ffn.at[3, second], ffn_far.at[second], along),
+        ("1l", ffn.at[1, first], ffn_x.at[first], across),
+        ("1h", ffn.at[1, second], ffn_x.at[second], across),
+        ("2l", ffn.at[2, first], ffn_y.at[first], along),
+        ("2h", ffn.at[2, second], ffn_y.at[second], along),
+    ]
+    ffns = {
+        name: remote(src, dst, fsend, frecv, i, peer)
+        for i, (name, src, dst, peer) in enumerate(ffns)
+    }
+    load.wait()
+    for name in ("3l", "3h", "1l", "2h"):
+        ffns[name].start()
+    ffns["3l"].wait_recv()
+    add_to(ffn.at[2, first], ffn_far.at[first])
+    ffns["2l"].start()
+    ffns["3h"].wait_recv()
+    add_to(ffn.at[1, second], ffn_far.at[second])
+    ffns["1h"].start()
+    for name in ("1l", "1h", "2l", "2h"):
+        ffns[name].wait_recv()
+    out_ref[...] = ffn[0].astype(F32) + ffn_x[...].astype(F32) + ffn_y[...].astype(F32)
+    for copy in ffns.values():
+        copy.wait_send()
+
+
+def ffn_rest(parts):
+    _, rows, d = parts.shape
+    return pl.pallas_call(
+        ffn_rest_kernel,
+        in_specs=[pl.BlockSpec(memory_space=pl.ANY)],
+        out_specs=pl.BlockSpec(memory_space=pltpu.VMEM),
+        out_shape=jax.ShapeDtypeStruct((rows, d), F32),
+        scratch_shapes=[pltpu.VMEM(parts.shape, BF16)]
+        + [pltpu.VMEM((rows, d), BF16)] * 3
+        + [pltpu.SemaphoreType.DMA((6,))] * 2
+        + [pltpu.SemaphoreType.DMA],
+        compiler_params=pltpu.CompilerParams(
+            collective_id=4, has_side_effects=True, vmem_limit_bytes=VMEM_LIMIT
+        ),
+        cost_estimate=pl.CostEstimate(
+            flops=8 * 10**9, bytes_accessed=8 * rows * d, transcendentals=0
+        ),
+        name="ffn_rest",
+    )(parts)
+
+
 def tail_kernel(
     mixed_ref,
     w_ref,
     out_parts_ref,
-    ffn_parts_ref,
     rows_ref,
     tok_ref,
     norm_ref,
@@ -1559,7 +1618,6 @@
     og_ref,
     qkv_ref,
     ng_ref,
-    ffn_ref,
     lines,
     line_sib,
     line_z,
@@ -1582,10 +1640,6 @@
     norms,
     norm_sum,
     norms_z,
-    ffn,
-    ffn_far,
-    ffn_x,
-    ffn_y,
     lsend,
     lrecv,
     hsend,
@@ -1606,10 +1660,7 @@
     nrecv,
     zsend,
     zrecv,
-    fsend,
-    frecv,
     load_sem,
-    ffn_sem,
 ):
     me, z = lax.axis_index("dp"), lax.axis_index("tensor")
     ways, rows = lines.shape[0], lines.shape[1]
@@ -1644,9 +1695,6 @@
         for load in loads[-1]:
             load.start()
 
-    ffn_load = pltpu.make_async_copy(ffn_parts_ref, ffn, ffn_sem)
-    ffn_load.start()
-
     def add_to(ref, other):
         ref[...] = (ref[...].astype(F32) + other[...].astype(F32)).astype(BF16)
 
@@ -1703,24 +1751,6 @@
     def qkv_rows(j):
         at = pl.ds(pl.multiple_of(j * width, width), width)
         qkv[at, :] = dot_tn(mixed_ref[:, at], rows_ref[...]).astype(BF16)
-
-    edge = ffn.shape[1] // 2
-    first, second = pl.ds(0, edge), pl.ds(edge, edge)
-    ffns = [
-        ("3l", ffn.at[3, first], ffn_far.at[first], across),
-        ("3h", ffn.at[3, second], ffn_far.at[second], along),
-        ("1l", ffn.at[1, first], ffn_x.at[first], across),
-        ("1h", ffn.at[1, second], ffn_x.at[second], across),
-        ("2l", ffn.at[2, first], ffn_y.at[first], along),
-        ("2h", ffn.at[2, second], ffn_y.at[second], along),
-    ]
-    ffns = {
-        name: remote(src, dst, fsend, frecv, i, peer)
-        for i, (name, src, dst, peer) in enumerate(ffns)
-    }
-    ffn_load.wait()
-    for name in ("3l", "3h", "1l", "2h"):
-        ffns[name].start()
 
     line(3)
     share(3).start()
@@ -1820,12 +1850,6 @@
     def _():
         qkv_z[group_of] = qkv_sum[...]
 
-    ffns["3l"].wait_recv()
-    add_to(ffn.at[2, first], ffn_far.at[first])
-    ffns["2l"].start()
-    ffns["3h"].wait_recv()
-    add_to(ffn.at[1, second], ffn_far.at[second])
-    ffns["1h"].start()
     sums["6l"].wait_recv()
     add_to(part.at[4, low], from_far.at[low])
     sums["4l"].start()
@@ -1890,10 +1914,6 @@
     gathers = gather_copies(view, gsend, grecv, True)
     gather_start(gathers)
 
-    for name in ("1l", "1h", "2l", "2h"):
-        ffns[name].wait_recv()
-    ffn_ref[...] = ffn[0].astype(F32) + ffn_x[...].astype(F32) + ffn_y[...].astype(F32)
-
     to_near[1].wait_recv()
     add_to(lines.at[z, part_of(core)], line_z.at[1])
 
@@ -1999,7 +2019,7 @@
     def _():
         last_home.wait_send()
 
-    for copy in (*sums.values(), *gathers.values(), *pieces.values(), *ffns.values(), *to_near, to_far):
+    for copy in (*sums.values(), *gathers.values(), *pieces.values(), *to_near, to_far):
         copy.wait_send()
     for k in range(7):
         swap(k, me).wait_send()
@@ -2011,7 +2031,7 @@
         norm_copy(k, to, z).wait_send()
 
 
-def tail(mixed, w, out_parts, ffn_parts, rows_one, tokens, norm_grads, ways):
+def tail(mixed, w, out_parts, rows_one, tokens, norm_grads, ways):
     rows, d = tokens.shape
     out_rows = out_parts.shape[1] // 8
     qkv_rows = mixed.shape[1] // 4
@@ -2021,14 +2041,13 @@
     sems = lambda n: [pltpu.SemaphoreType.DMA((n,))] * 2
     return pl.pallas_call(
         tail_kernel,
-        in_specs=[inside] * 2 + [anywhere] * 2 + [inside] * 3,
-        out_specs=[inside] * 5,
+        in_specs=[inside] * 2 + [anywhere] + [inside] * 3,
+        out_specs=[inside] * 4,
         out_shape=[
             jax.ShapeDtypeStruct((rows, d), F32),
             jax.ShapeDtypeStruct((8, out_rows, d), BF16),
             jax.ShapeDtypeStruct((4, qkv_rows, d), BF16),
             jax.ShapeDtypeStruct((8, d), F32),
-            jax.ShapeDtypeStruct(ffn_parts.shape[1:], F32),
         ],
         scratch_shapes=[
             pltpu.VMEM((ways, rows, d), BF16),
@@ -2053,9 +2072,7 @@
             pltpu.VMEM((8, 8, d), F32),
             pltpu.VMEM((8, d), F32),
             pltpu.VMEM((ways, 8, d), F32),
-            pltpu.VMEM(ffn_parts.shape, BF16),
         ]
-        + [pltpu.VMEM(ffn_parts.shape[1:], BF16)] * 3
         + sems(4)
         + sems(ways)
         + sems(10)
@@ -2066,8 +2083,7 @@
         + sems(8)
         + sems(7)
         + sems(ways)
-        + sems(6)
-        + [pltpu.SemaphoreType.DMA((ways, 8)), pltpu.SemaphoreType.DMA],
+        + [pltpu.SemaphoreType.DMA((ways, 8))],
         compiler_params=pltpu.CompilerParams(
             collective_id=2, has_side_effects=True, vmem_limit_bytes=VMEM_LIMIT
         ),
@@ -2075,7 +2091,7 @@
             flops=75 * 10**9, bytes_accessed=40 * rows * d, transcendentals=0
         ),
         name="tail",
-    )(mixed, w, out_parts, ffn_parts, rows_one, tokens, norm_grads)
+    )(mixed, w, out_parts, rows_one, tokens, norm_grads)
 
 
 def finish_kernel(
@@ -2106,11 +2122,14 @@
         for g in range(2):
             at = pl.ds(2 * p + g, turned.shape[0], stride=16)
             gate_up_ref[at, :] = turned[:, g * units : (g + 1) * units]
-    down_out_ref[...] = down_ref[0].astype(F32)
+    for p in range(down_ref.shape[0]):
+        down_out_ref[p * units : (p + 1) * units] = down_ref[p].astype(F32)
     width = qkv_ref.shape[2]
     for j in range(3):
         qkv_ref[j] = features_ref[j * width : (j + 1) * width].astype(F32).T
-    og_out_ref[...] = og_ref[0].astype(F32)
+    out_rows = og_ref.shape[1]
+    for p in range(og_ref.shape[0]):
+        og_out_ref[p * out_rows : (p + 1) * out_rows] = og_ref[p].astype(F32)
     values = tok_ref[...].astype(F32)
     centred = values - jnp.mean(values, axis=-1, keepdims=True)
     root = lax.rsqrt(jnp.mean(centred * centred, axis=-1, keepdims=True) + norm_eps)
@@ -2135,33 +2154,35 @@
 def finish(grads, features, out_grad, norm_grad, resid_grad, tokens, gain, low, high, resid, norms):
     rows, d = tokens.shape
     units = grads.shape[1] // 3
-    block = d // 8
     width = features.shape[0] // 3
     out_rows = out_grad.shape[1]
-    own = pl.BlockSpec((rows // 8, d), lambda i: (i, 0))
-    kept = 8 * low.shape[0] // rows
+    steps = 4
+    each = 8 // steps
+    block = d // steps
+    own = pl.BlockSpec((rows // steps, d), lambda i: (i, 0))
+    kept = steps * low.shape[0] // rows
     return pl.pallas_call(
         functools.partial(finish_kernel, kept),
-        grid=(8,),
+        grid=(steps,),
         in_specs=[
             pl.BlockSpec((8, 2 * units, block), lambda i: (0, 0, i)),
-            pl.BlockSpec((1, units, d), lambda i: (i, 2, 0)),
+            pl.BlockSpec((each, units, d), lambda i: (i, 2, 0)),
             pl.BlockSpec((3 * width, block), lambda i: (0, i)),
-            pl.BlockSpec((1, out_rows, d), lambda i: (i, 0, 0)),
+            pl.BlockSpec((each, out_rows, d), lambda i: (i, 0, 0)),
             own,
             own,
             own,
             pl.BlockSpec((1, d), lambda i: (0, 0)),
-            pl.BlockSpec((rows // 8, d), lambda i: (jnp.minimum(i, kept - 1), 0)),
-            pl.BlockSpec((rows // 8, d), lambda i: (jnp.maximum(i - kept, 0), 0)),
-            own,
+            pl.BlockSpec((rows // steps, d), lambda i: (jnp.minimum(i, kept - 1), 0)),
+            pl.BlockSpec((rows // steps, d), lambda i: (jnp.maximum(i - kept, 0), 0)),
+            pl.BlockSpec((rows // steps, d), lambda i: (jnp.maximum(i, kept), 0)),
             pl.BlockSpec(norms.shape, lambda i: (0, 0)),
         ],
         out_specs=[
             pl.BlockSpec((16 * block, units), lambda i: (i, 0)),
-            pl.BlockSpec((units, d), lambda i: (i, 0)),
+            pl.BlockSpec((each * units, d), lambda i: (i, 0)),
             pl.BlockSpec((3, block, width), lambda i: (0, i, 0)),
-            pl.BlockSpec((out_rows, d), lambda i: (i, 0)),
+            pl.BlockSpec((each * out_rows, d), lambda i: (i, 0)),
             own,
             own,
         ]
@@ -2371,13 +2392,14 @@
     mixed_grad = attend_back(
         bucket, q, k, kt, v, attended_grad, *kept, cos_wide, sine_wide, head_dim
     )
-    grads, mixed_grad = lax.optimization_barrier((grads, mixed_grad))
+    ffn_parts, mixed_grad = lax.optimization_barrier((ffn_parts, mixed_grad))
+    layer_high = ffn_rest(ffn_parts)
+    grads, mixed_grad, layer_high = lax.optimization_barrier((grads, mixed_grad, layer_high))
     grads = lax.all_gather(grads, "dp", axis=0)
-    normed_one_grad, out_grad, qkv_grad, norm_grads, layer_high = tail(
+    normed_one_grad, out_grad, qkv_grad, norm_grads = tail(
         mixed_grad,
         qkv_weights,
         out_grad.reshape(ways, local_width, d),
-        ffn_parts,
         rows_one.reshape(group_rows, d),
         tokens,
         norm_grads,

time: 436 us -> 433 us (level)
  waiting for transfers between devices: 17.6 us -> 0.11 us
  Pallas kernels: 394 us -> 410 us
    reduce_scatter x1, waiting for transfers between devices: 17.5 us -> 0.02 us  [shards_columns(): grads = lax.psum_scatter(grads, 'tensor', scatter_dimension=0)]
    pallas_call x2 -> x3, Pallas kernels: 101 us -> 117 us  [the longest x1 77.9 us: tail(): pl.pallas_call(tail_kernel, in_specs=[inside] * 2 + [anywhere] + [inside]...]
  transfers between devices with their start and end apart: 3 -> 3, of which waited for: 1 -> 0; matrix products, arithmetic and copies ran while one was open for 0% -> 0% of each run, Pallas kernels for 44% -> 49%
where the time goes in v5:
time: 433 us; the launch traced here: 430 us
  Pallas kernels  410 us (95%)
  between operations  14.8 us (3%)
    pallas_call x1, Pallas kernels, middle(): pl.pallas_call(middle_kernel, in_specs=[anywhere] * 8 + [inside], out_spe...  121 us
    pallas_call x1, Pallas kernels, tail(): pl.pallas_call(tail_kernel, in_specs=[inside] * 2 + [anywhere] + [inside]...  77.9 us
    pallas_call x1, Pallas kernels, front(): pl.pallas_call(functools.partial(front_kernel, head_dim), in_specs=[pl.Bl...  64.6 us
    pallas_call x1, Pallas kernels, collect(): pl.pallas_call(collect_kernel, in_specs=[anywhere] + [inside] * 4 + [anyw...  41.2 us
    pallas_call x1, Pallas kernels, attend_back(): pl.pallas_call(functools.partial(attend_back_kernel, head_dim), grid=(n /...  41 us
    pallas_call x1, Pallas kernels, attend(): pl.pallas_call(functools.partial(attend_kernel, head_dim), grid=(n // blo...  24.8 us
    pallas_call x1, Pallas kernels, ffn_rest(): pl.pallas_call(ffn_rest_kernel, in_specs=[pl.BlockSpec(memory_space=pl.AN...  24.4 us
    pallas_call x1, Pallas kernels, finish(): pl.pallas_call(functools.partial(finish_kernel, kept), grid=(steps,), in_...  14.4 us
  transfers between devices with their start and end apart: 3, of which 0 were waited for; matrix products, arithmetic and copies ran while one was open for 0% of the time, Pallas kernels for 49%

profile of v5, /device:TPU:0, one launch (start us, length us, event | category | flops | bytes accessed | tf_op | source)
XLA Modules:
  0.0 429.9 jit_solution(10505110843880918602)
XLA Ops:
  7.2 0.0 all-gather.5.cloned.1.call-start
  7.9 0.6 broadcast_in_dim_tile.3.freq_ref
  8.5 1.4 constant_dynamic-slice_fusion.2
  9.9 0.4 copy.26
  10.4 1.0 constant_dynamic-slice_fusion.1
  11.4 0.8 pad_maximum_fusion
  12.1 64.6 %front.1 = (bf16[2048,256]{1,0:T(8,128)(2,1)}, bf16[2048,256]{1,0:T(8,128)(2,1)}, bf16[2048,256]{1,0:T(8,128)(2,1)}, bf16[256,2048]{1,0:T(8,128)(2,1)}, bf16[256...) custom-call(s32[1]{0:T(128)S(6)} %copy.27.bucket_ref, ...), custom_call_target="tpu_custom_call" | custom-call | flops 54999998464 | bytes 16777216 | tf_op jit(solution)/shard_map/front/pallas_call | solution.py:772
  76.8 0.0 all-gather.5.cloned.1.call-update
  76.8 0.3 reduce-scatter.2.cloned.1.call-start
  77.1 0.8 pad_maximum_fusion.1.w_high_ref
  77.9 24.8 %attend.1 = (bf16[2048,256]{1,0:T(8,128)(2,1)}, f32[256,2048]{1,0:T(8,128)}, f32[8,2048]{1,0:T(8,128)}) custom-call(s32[8,128]{1,0:T(8,128)} %get-tuple-element.58.bucket_ref, bf16[2048,256]{1,0:T(8,128)(2,1)} %get-tuple-element.59.q_ref, bf16[2048,256]{1,0:T(8,128)(2,1)} %get-tuple-element.60.k_ref, bf16[256,2048]{1,0:T(8,128)(2,1)} %get-tuple-element.61.vt_ref), custom_call_target="tpu_custom_call" | custom-call | flops 17179869184 | bytes 5242880 | tf_op jit(solution)/shard_map/attend/pallas_call | solution.py:184
  102.6 41.2 %collect.1 = (bf16[4,512,256]{2,1,0:T(8,128)(2,1)}, f32[512,1024]{1,0:T(8,128)}, bf16[512,1024]{1,0:T(8,128)(2,1)}, bf16[8,256,1024]{2,1,0:T(8,128)(2,1)}) custom-call(bf16[2048,256]{1,0:T(8,128)(2,1)} %get-tuple-element.62.att_ref, bf16[512,1024]{1,0:T(8,128)(2,1)} %tok_ref.7, bf16[1024,1024]{1,0:T(8,128)(2,1)} %bitcast.51, f32[1,1024]{1,0:T(1,128)} %bitcast.43, ...), custom_call_target="tpu_custom_call" | custom-call | flops 30000001024 | bytes 8388608 | tf_op jit(solution)/shard_map/collect/pallas_call | solution.py:946
  143.9 0.0 all-gather.5.cloned.1.call-done
  143.9 121.3 %middle.1 = (bf16[4,512,256]{2,1,0:T(8,128)(2,1)}, f32[512,1024]{1,0:T(8,128)}, bf16[2,512,1024]{2,1,0:T(8,128)(2,1)}, bf16[384,1024]{1,0:T(8,128)(2,1)}, bf16[4...) custom-call(bf16[512,1024]{1,0:T(8,128)(2,1)} %get-tuple-element.64.x_ref, ...), custom_call_target="tpu_custom_call" | custom-call | flops 130000003072 | bytes 20971520 | tf_op jit(solution)/shard_map/middle/pallas_call | solution.py:1496
  265.2 0.0 reduce-scatter.2.cloned.1.call-update
  265.2 0.0 all-gather.7.cloned.1.call-start
  265.3 41.0 %attend_back.1.mixed_ref = bf16[2048,768]{1,0:T(8,128)(2,1)} custom-call(s32[8,128]{1,0:T(8,128)} %get-tuple-element.58.bucket_ref, bf16[2048,256]{1,0:T(8,128)(2,1)} %get-tuple-element.59.q_ref, bf16[2048,256]{1,0:T(8,128)(2,1)} %get-tuple-element.60.k_ref, bf16[256,2048]{1,0:T(8,128)(2,1)} %get-tuple-element.72.kt_ref, ...), custom_call_target="tpu_custom_call" | custom-call | flops 42949672960 | bytes 12582912 | tf_op jit(solution)/shard_map/attend_back/pallas_call | solution.py:294
  306.3 24.4 %ffn_rest.1.high_ref = f32[128,1024]{1,0:T(8,128)} custom-call(bf16[4,128,1024]{2,1,0:T(8,128)(2,1)} %get-tuple-element.80.parts_ref), custom_call_target="tpu_custom_call" | custom-call | flops 8000000000 | bytes 1048576 | tf_op jit(solution)/shard_map/ffn_rest/pallas_call | solution.py:1591
  330.7 0.0 reduce-scatter.2.cloned.1.call-done
  330.8 0.0 all-gather.7.cloned.1.call-update
  330.8 77.9 %tail.1 = (f32[512,1024]{1,0:T(8,128)}, bf16[8,32,1024]{2,1,0:T(8,128)(2,1)}, bf16[4,192,1024]{2,1,0:T(8,128)(2,1)}, f32[8,1024]{1,0:T(8,128)}) custom-call(bf16[2048,768]{1,0:T(8,128)(2,1)} %attend_back.1.mixed_ref, bf16[3,1024,256]{2,1,0:T(8,128)(2,1)} %get-tuple-element.83.w_ref, bf16[4,256,1024]{2,1,0:T(8,128)(2,1)} %bitcast.50, ...), custom_call_target="tpu_custom_call" | custom-call | flops 74999996416 | bytes 20971520 | tf_op jit(solution)/shard_map/tail/pallas_call | solution.py:2042
  408.7 0.0 all-gather.7.cloned.1.call-done
  408.7 14.4 %finish.1 = (f32[16384,128]{1,0:T(8,128)}, f32[1024,1024]{1,0:T(8,128)}, f32[3,1024,256]{2,1,0:T(8,128)}, f32[256,1024]{1,0:T(8,128)}, f32[512,1024]{1,0:T(8,128...) custom-call(bf16[8,384,1024]{2,1,0:T(8,128)(2,1)} %bitcast.27, ...), custom_call_target="tpu_custom_call" | custom-call | tf_op jit(solution)/shard_map/finish/pallas_call | solution.py:2164
  (3 shorter events, 0.1 us)
Async XLA Ops:
  7.2 136.7 %all-gather.5.cloned.1.call-start = ((), (), s32[]{:S(2)}) async-start(), calls=%async_computation.2 | async-start | bytes 1966080 | tf_op jit(solution)/shard_map/all_gather | solution.py:2372
  76.8 253.9 %reduce-scatter.2.cloned.1.call-start = ((), (), s32[]{:S(2)}) async-start(), calls=%async_computation.1 | async-start | bytes 3932160 | tf_op jit(solution)/shard_map/reduce_scatter | solution.py:2390
  265.2 143.5 %all-gather.7.cloned.1.call-start = ((), (), s32[]{:S(2)}) async-start(), calls=%async_computation.3 | async-start | bytes 7077888 | tf_op jit(solution)/shard_map/all_gather | solution.py:2398
Sparse Core Ops, SparseCore 0:
  76.9 49.6 all-gather.4
  265.3 58.3 reduce-scatter.1
  330.9 57.0 all-gather.6

commit v6 on v5

--- a/solution.py
+++ b/solution.py
@@ -14,7 +14,6 @@
 norm_eps = 1e-05
 mask_fill = -1e30
 rope_base = 10000.0
-log2_e = 1.4426950408889634
 VMEM_LIMIT = 62 * 2**20
 F32 = jnp.float32
 BF16 = jnp.bfloat16
@@ -87,7 +86,7 @@
     q = q * cos + swap_halves(q, head_dim) * sin
     k = k * cos + swap_halves(k, head_dim) * sin
     k_low = k.astype(BF16)
-    q_ref[...] = (q * (head_dim ** (-0.5) * log2_e)).astype(BF16)
+    q_ref[...] = (q.astype(BF16).astype(F32) * head_dim ** (-0.5)).astype(BF16)
     k_ref[...] = k_low
     v_ref[...] = v
     kt_ref[...] = k_low.T
@@ -152,10 +151,10 @@
             if masked:
                 scores = scores + bias_ref[: last - first, :]
             top = jnp.max(scores, axis=0, keepdims=True)
-            weights = jnp.exp2(scores - top)
+            weights = jnp.exp(scores - top)
             totals = jnp.sum(weights, axis=0, keepdims=True)
             ot_ref[hs, at] = dot_nn(vt_ref[hs, first:last], weights.astype(BF16)) / totals
-            l_ref[pl.ds(h, 1), at] = top + jnp.log2(totals)
+            l_ref[pl.ds(h, 1), at] = top + jnp.log(totals)
 
     @pl.when(bucket_ref[0, 0] == 1)
     def _():
@@ -246,7 +245,7 @@
             scores = dot_nt(k_ref[keys, :], qh)
             if masked:
                 scores = scores + bias_ref[: last - first, :]
-            probs = jnp.exp2(scores - l_ref[pl.ds(h, 1), :])
+            probs = jnp.exp(scores - l_ref[pl.ds(h, 1), :])
             prob_grad = dot_nt(v_ref[keys, :], gh)
             delta = jnp.sum(gt_ref[hs, :], axis=0, keepdims=True)
             score_grad = (probs * (prob_grad - delta)).astype(BF16)
@@ -278,7 +277,7 @@
         @pl.loop(0, total // rows)
         def _(i):
             at = pl.ds(pl.multiple_of(i * rows, rows), rows)
-            out_ref[at, width : 2 * width] = turn_back(dk_ref[at, :] * (1.0 / log2_e), at)
+            out_ref[at, width : 2 * width] = turn_back(dk_ref[at, :], at)
             out_ref[at, 2 * width :] = dv_ref[at, :].astype(BF16)
 
 
@@ -724,7 +723,7 @@
         v = v.astype(BF16)
         q = q * cos + swap_halves(q, head_dim) * sin
         k = (k * cos + swap_halves(k, head_dim) * sin).astype(BF16)
-        q_ref[at, :] = (q * (head_dim ** (-0.5) * log2_e)).astype(BF16)
+        q_ref[at, :] = (q.astype(BF16).astype(F32) * head_dim ** (-0.5)).astype(BF16)
         k_ref[at, :] = k
         v_ref[at, :] = v
         kt_ref[:, at] = k.T

time: 433 us -> 434 us (level)
  Pallas kernels: 410 us -> 405 us
    pallas_call x1, Pallas kernels: 24.4 us -> 12.6 us  [ffn_rest(): pl.pallas_call(ffn_rest_kernel, in_specs=[pl.BlockSpec(memory_space=pl.AN...]
    pallas_call x1, Pallas kernels: 77.9 us -> 84.8 us  [tail(): pl.pallas_call(tail_kernel, in_specs=[inside] * 2 + [anywhere] + [inside]...]
  transfers between devices with their start and end apart: 3 -> 3, of which waited for: 0 -> 1; matrix products, arithmetic and copies ran while one was open for 0% -> 0% of each run, Pallas kernels for 49% -> 48%
where the time goes in v6:
time: 434 us; the launch traced here: 430 us
  Pallas kernels  405 us (93%)
  between operations  14.7 us (3%)
    pallas_call x1, Pallas kernels, middle(): pl.pallas_call(middle_kernel, in_specs=[anywhere] * 8 + [inside], out_spe...  121 us
    pallas_call x1, Pallas kernels, tail(): pl.pallas_call(tail_kernel, in_specs=[inside] * 2 + [anywhere] + [inside]...  84.8 us
    pallas_call x1, Pallas kernels, front(): pl.pallas_call(functools.partial(front_kernel, head_dim), in_specs=[pl.Bl...  64.6 us
    pallas_call x1, Pallas kernels, attend_back(): pl.pallas_call(functools.partial(attend_back_kernel, head_dim), grid=(n /...  41.6 us
    pallas_call x1, Pallas kernels, collect(): pl.pallas_call(collect_kernel, in_specs=[anywhere] + [inside] * 4 + [anyw...  40.7 us
    pallas_call x1, Pallas kernels, attend(): pl.pallas_call(functools.partial(attend_kernel, head_dim), grid=(n // blo...  25.3 us
    pallas_call x1, Pallas kernels, finish(): pl.pallas_call(functools.partial(finish_kernel, kept), grid=(steps,), in_...  14.4 us
    pallas_call x1, Pallas kernels, ffn_rest(): pl.pallas_call(ffn_rest_kernel, in_specs=[pl.BlockSpec(memory_space=pl.AN...  12.6 us
  transfers between devices with their start and end apart: 3, of which 1 were waited for; matrix products, arithmetic and copies ran while one was open for 0% of the time, Pallas kernels for 48%

profile of v6, /device:TPU:0, one launch (start us, length us, event | category | flops | bytes accessed | tf_op | source)
XLA Modules:
  0.0 429.7 jit_solution(12143327898048393228)
XLA Ops:
  7.2 0.0 all-gather.5.cloned.1.call-start
  7.9 0.6 broadcast_in_dim_tile.3.freq_ref
  8.5 1.4 constant_dynamic-slice_fusion.2
  9.9 0.4 copy.26
  10.4 1.0 constant_dynamic-slice_fusion.1
  11.4 0.8 pad_maximum_fusion
  12.1 64.6 %front.1 = (bf16[2048,256]{1,0:T(8,128)(2,1)}, bf16[2048,256]{1,0:T(8,128)(2,1)}, bf16[2048,256]{1,0:T(8,128)(2,1)}, bf16[256,2048]{1,0:T(8,128)(2,1)}, bf16[256...) custom-call(s32[1]{0:T(128)S(6)} %copy.27.bucket_ref, ...), custom_call_target="tpu_custom_call" | custom-call | flops 54999998464 | bytes 16777216 | tf_op jit(solution)/shard_map/front/pallas_call | solution.py:771
  76.8 0.0 all-gather.5.cloned.1.call-update
  76.8 0.3 reduce-scatter.2.cloned.1.call-start
  77.1 0.8 pad_maximum_fusion.1.w_high_ref
  77.9 25.3 %attend.1 = (bf16[2048,256]{1,0:T(8,128)(2,1)}, f32[256,2048]{1,0:T(8,128)}, f32[8,2048]{1,0:T(8,128)}) custom-call(s32[8,128]{1,0:T(8,128)} %get-tuple-element.58.bucket_ref, bf16[2048,256]{1,0:T(8,128)(2,1)} %get-tuple-element.59.q_ref, bf16[2048,256]{1,0:T(8,128)(2,1)} %get-tuple-element.60.k_ref, bf16[256,2048]{1,0:T(8,128)(2,1)} %get-tuple-element.61.vt_ref), custom_call_target="tpu_custom_call" | custom-call | flops 17179869184 | bytes 5242880 | tf_op jit(solution)/shard_map/attend/pallas_call | solution.py:183
  103.2 40.7 %collect.1 = (bf16[4,512,256]{2,1,0:T(8,128)(2,1)}, f32[512,1024]{1,0:T(8,128)}, bf16[512,1024]{1,0:T(8,128)(2,1)}, bf16[8,256,1024]{2,1,0:T(8,128)(2,1)}) custom-call(bf16[2048,256]{1,0:T(8,128)(2,1)} %get-tuple-element.62.att_ref, bf16[512,1024]{1,0:T(8,128)(2,1)} %tok_ref.7, bf16[1024,1024]{1,0:T(8,128)(2,1)} %bitcast.51, f32[1,1024]{1,0:T(1,128)} %bitcast.43, ...), custom_call_target="tpu_custom_call" | custom-call | flops 30000001024 | bytes 8388608 | tf_op jit(solution)/shard_map/collect/pallas_call | solution.py:945
  143.9 0.0 all-gather.5.cloned.1.call-done
  143.9 121.1 %middle.1 = (bf16[4,512,256]{2,1,0:T(8,128)(2,1)}, f32[512,1024]{1,0:T(8,128)}, bf16[2,512,1024]{2,1,0:T(8,128)(2,1)}, bf16[384,1024]{1,0:T(8,128)(2,1)}, bf16[4...) custom-call(bf16[512,1024]{1,0:T(8,128)(2,1)} %get-tuple-element.64.x_ref, ...), custom_call_target="tpu_custom_call" | custom-call | flops 130000003072 | bytes 20971520 | tf_op jit(solution)/shard_map/middle/pallas_call | solution.py:1495
  265.1 0.0 reduce-scatter.2.cloned.1.call-update
  265.1 0.0 all-gather.7.cloned.1.call-start
  265.2 41.6 %attend_back.1.mixed_ref = bf16[2048,768]{1,0:T(8,128)(2,1)} custom-call(s32[8,128]{1,0:T(8,128)} %get-tuple-element.58.bucket_ref, bf16[2048,256]{1,0:T(8,128)(2,1)} %get-tuple-element.59.q_ref, bf16[2048,256]{1,0:T(8,128)(2,1)} %get-tuple-element.60.k_ref, bf16[256,2048]{1,0:T(8,128)(2,1)} %get-tuple-element.72.kt_ref, ...), custom_call_target="tpu_custom_call" | custom-call | flops 42949672960 | bytes 12582912 | tf_op jit(solution)/shard_map/attend_back/pallas_call | solution.py:293
  306.8 12.6 %ffn_rest.1.high_ref = f32[128,1024]{1,0:T(8,128)} custom-call(bf16[4,128,1024]{2,1,0:T(8,128)(2,1)} %get-tuple-element.80.parts_ref), custom_call_target="tpu_custom_call" | custom-call | flops 8000000000 | bytes 1048576 | tf_op jit(solution)/shard_map/ffn_rest/pallas_call | solution.py:1590
  319.4 4.2 reduce-scatter.2.cloned.1.call-done
  323.7 0.0 all-gather.7.cloned.1.call-update
  323.7 84.8 %tail.1 = (f32[512,1024]{1,0:T(8,128)}, bf16[8,32,1024]{2,1,0:T(8,128)(2,1)}, bf16[4,192,1024]{2,1,0:T(8,128)(2,1)}, f32[8,1024]{1,0:T(8,128)}) custom-call(bf16[2048,768]{1,0:T(8,128)(2,1)} %attend_back.1.mixed_ref, bf16[3,1024,256]{2,1,0:T(8,128)(2,1)} %get-tuple-element.83.w_ref, bf16[4,256,1024]{2,1,0:T(8,128)(2,1)} %bitcast.50, ...), custom_call_target="tpu_custom_call" | custom-call | flops 74999996416 | bytes 20971520 | tf_op jit(solution)/shard_map/tail/pallas_call | solution.py:2041
  408.5 0.0 all-gather.7.cloned.1.call-done
  408.5 14.4 %finish.1 = (f32[16384,128]{1,0:T(8,128)}, f32[1024,1024]{1,0:T(8,128)}, f32[3,1024,256]{2,1,0:T(8,128)}, f32[256,1024]{1,0:T(8,128)}, f32[512,1024]{1,0:T(8,128...) custom-call(bf16[8,384,1024]{2,1,0:T(8,128)(2,1)} %bitcast.27, ...), custom_call_target="tpu_custom_call" | custom-call | tf_op jit(solution)/shard_map/finish/pallas_call | solution.py:2163
  (3 shorter events, 0.1 us)
Async XLA Ops:
  7.2 136.8 %all-gather.5.cloned.1.call-start = ((), (), s32[]{:S(2)}) async-start(), calls=%async_computation.2 | async-start | bytes 1966080 | tf_op jit(solution)/shard_map/all_gather | solution.py:2371
  76.8 246.9 %reduce-scatter.2.cloned.1.call-start = ((), (), s32[]{:S(2)}) async-start(), calls=%async_computation.1 | async-start | bytes 3932160 | tf_op jit(solution)/shard_map/reduce_scatter | solution.py:2389
  265.1 143.4 %all-gather.7.cloned.1.call-start = ((), (), s32[]{:S(2)}) async-start(), calls=%async_computation.3 | async-start | bytes 7077888 | tf_op jit(solution)/shard_map/all_gather | solution.py:2397
Sparse Core Ops, SparseCore 0:
  76.9 49.4 all-gather.4
  265.2 58.3 reduce-scatter.1
  325.6 62.3 all-gather.6
